TPU v7x, 1024 devices: a whole 4x4x32 slice. The times are simulated.
1024 devices in a mesh: dp: 4 (over y), expert: 32 (over x, z_lo), mp: 8 (over z_hi, core).
Axes of the slice: x: 4, y: 4, z: 32 (z_hi: 4, z_lo: 8; z = z_hi * 8 + z_lo), core: 2. Of those that a mesh axis runs over, the one named last changes fastest.
Arguments:
- tokens: bfloat16 [16384, 2048], P(('dp', 'expert')), may hold values from -6 to 6
- cotangent: bfloat16 [16384, 2048], P(('dp', 'expert')), may hold values from -1.5 to 1.5
- gate_value: float32 [16384], P(('dp', 'expert')), may hold values from 0.25 to 1
- expert_id: int32 [16384], P(('dp', 'expert')), may hold values from 0 to 31, as said below
- token_slot: int32 [16384], P(('dp', 'expert')), may hold values from -1 to 3, as said below
- w_in: bfloat16 [32, 2048, 5120], P('expert', 'dp', 'mp'), may hold values from -0.125 to 0.125
- w_out: bfloat16 [32, 5120, 2048], P('expert', 'mp', 'dp'), may hold values from -0.078125 to 0.078125
Outputs:
- grad_tokens: bfloat16 [16384, 4, 512], P(('dp', 'expert'), None, 'mp')
- grad_w_in: bfloat16 [32, 2048, 5120], P('expert', 'dp', 'mp')
- grad_w_out: bfloat16 [32, 5120, 2048], P('expert', 'mp', 'dp')
Inputs may be any that keep to these rules, and one draw needn't show every extreme that they name: `expert_id`: in every group of 128 consecutive tokens some expert is named by 4 + 1 tokens or more. `token_slot`: A kept token's slot counts the earlier tokens of its group that name the same expert; tokens whose count reaches 4 have slot -1. Every group drops tokens, and some expert has all 4 slots used by every group.
All inputs are finite; a program needn't handle non-finite values.
Results may differ from a plain program's by a relative error of at most 0.025.
Values may be sent and summed in bfloat16 or wider, within the bound.
No kernel may reach another device: no remote copies, remote signals or barrier semaphores. Data moves between devices by JAX's collectives and lax.ppermute only.
A program may use at most 32 MiB of HBM per device.

v0:
```python
import jax
import jax.numpy as jnp
from jax import lax
from jax.sharding import PartitionSpec as P

tanh_scale = 0.7978845608028654
cubic_coef = 0.044715


def gelu_pair(pre_act):
    tanh_arg = tanh_scale * (pre_act + cubic_coef * pre_act * pre_act * pre_act)
    tanh_val = jnp.tanh(tanh_arg)
    gelu_value = 0.5 * pre_act * (1.0 + tanh_val)
    gelu_slope = 0.5 * (1.0 + tanh_val) + 0.5 * pre_act * (
        1.0 - tanh_val * tanh_val
    ) * tanh_scale * (1.0 + 3.0 * cubic_coef * pre_act * pre_act)
    return (gelu_value, gelu_slope)


def local(tokens, cotangent, gate_value, expert_id, token_slot, w_in, w_out):
    experts = lax.axis_size("expert")
    replicas = lax.axis_size("dp")
    tok_rows, model_width = tokens.shape
    capacity = tok_rows // experts
    gated_dy = (gate_value[:, None] * cotangent.astype(jnp.float32)).astype(jnp.bfloat16)
    is_kept = token_slot >= 0
    target = jnp.where(is_kept, expert_id * capacity + token_slot, experts * capacity)
    zero_rows = jnp.zeros((experts * capacity + 1, model_width), jnp.bfloat16)
    send_x = zero_rows.at[target].set(tokens)[:-1].reshape(experts, capacity, model_width)
    send_dy = zero_rows.at[target].set(gated_dy)[:-1].reshape(experts, capacity, model_width)
    section_x, section_dy = (
        lax.all_to_all(send_x, "expert", split_axis=0, concat_axis=0, tiled=True),
        lax.all_to_all(send_dy, "expert", split_axis=0, concat_axis=0, tiled=True),
    )
    recv_x, recv_dy = (
        lax.all_to_all(section_x, "dp", split_axis=2, concat_axis=1, tiled=True),
        lax.all_to_all(section_dy, "dp", split_axis=2, concat_axis=1, tiled=True),
    )
    quarter = recv_x.shape[2]
    disp_x = recv_x.reshape(-1, quarter)
    disp_dy = recv_dy.reshape(-1, quarter)
    weight_in = w_in[0]
    weight_out = w_out[0]
    hidden_part = jnp.dot(disp_x, weight_in, preferred_element_type=jnp.float32)
    back_part = lax.dot_general(
        disp_dy, weight_out, (((1,), (1,)), ((), ())), preferred_element_type=jnp.float32
    )
    pre_act, grad_act = (
        lax.psum(hidden_part.astype(jnp.bfloat16), "dp").astype(jnp.float32),
        lax.psum(back_part.astype(jnp.bfloat16), "dp").astype(jnp.float32),
    )
    gelu_value, gelu_slope = gelu_pair(pre_act)
    activation = gelu_value.astype(jnp.bfloat16)
    d_hidden = (grad_act * gelu_slope).astype(jnp.bfloat16)
    grad_in = lax.dot_general(
        disp_x, d_hidden, (((0,), (0,)), ((), ())), preferred_element_type=jnp.float32
    )
    grad_out = lax.dot_general(
        activation, disp_dy, (((0,), (0,)), ((), ())), preferred_element_type=jnp.float32
    )
    summed = lax.psum_scatter(
        lax.dot_general(
            weight_in, d_hidden, (((1,), (1,)), ((), ())), preferred_element_type=jnp.float32
        ).astype(jnp.bfloat16),
        "mp",
        scatter_dimension=0,
        tiled=True,
    ).astype(jnp.float32)
    col_count = summed.shape[0]
    send_back = summed.astype(jnp.bfloat16).reshape(col_count, experts, replicas, capacity)
    arrived = lax.all_to_all(
        lax.all_to_all(send_back, "dp", split_axis=2, concat_axis=2, tiled=True),
        "expert",
        split_axis=1,
        concat_axis=1,
        tiled=True,
    )
    row_table = jnp.transpose(arrived, (1, 3, 2, 0)).reshape(
        experts * capacity, replicas, col_count
    )
    row_table = jnp.concatenate(
        [row_table, jnp.zeros((1, replicas, col_count), jnp.bfloat16)], axis=0
    )
    grad_tokens = row_table[target]
    return (grad_tokens, grad_in.astype(jnp.bfloat16)[None], grad_out.astype(jnp.bfloat16)[None])


def solution(mesh):
    in_specs = (
        P(("dp", "expert"), None),
        P(("dp", "expert"), None),
        P(("dp", "expert")),
        P(("dp", "expert")),
        P(("dp", "expert")),
        P("expert", "dp", "mp"),
        P("expert", "mp", "dp"),
    )
    out_specs = (P(("dp", "expert"), None, "mp"), P("expert", "dp", "mp"), P("expert", "mp", "dp"))
    return jax.shard_map(local, mesh=mesh, in_specs=in_specs, out_specs=out_specs, check_vma=False)
```

profile of v0, /device:TPU:1, one launch (start us, length us, event | category | flops | bytes accessed | tf_op | source)
XLA Modules:
  0.0 340.1 jit_solution(12731631963720011275)
XLA Ops:
  7.9 2.0 scatter_custom_fusion.1
  10.0 1.0 reshape.29
  11.0 15.9 %all-to-all-start.2 = ((bf16[32,4,2048]{2,1,0:T(4,128)(2,1)}), bf16[32,4,2048]{2,1,0:T(4,128)(2,1)S(1)}, u32[]{:S(2)}, u32[]{:S(2)}) async-start(bf16[32,4,2048]{2,1,0:T(4,128)(2,1)} %reshape.29), calls=%async_computation.2 | async-start | bytes 1048576 | tf_op jit(solution)/shard_map/all_to_all | solution.py:32
  27.0 1.6 scatter_custom_fusion
  28.6 1.0 reshape.27
  29.6 26.5 %all-to-all-done.2 = bf16[32,4,2048]{2,1,0:T(4,128)(2,1)S(1)} async-done(((bf16[32,4,2048]{2,1,0:T(4,128)(2,1)}), bf16[32,4,2048]{2,1,0:T(4,128)(2,1)S(1)}, u32[]{:S(2)}, u32[]{:S(2)}) %all-to-all-start.2) | async-done | bytes 524320 | tf_op jit(solution)/shard_map/all_to_all | solution.py:32
  56.1 5.7 %all-to-all-start = ((bf16[32,4,2048]{2,1,0:T(4,128)(2,1)}), bf16[32,4,2048]{2,1,0:T(4,128)(2,1)}, u32[]{:S(2)}, u32[]{:S(2)}) async-start(bf16[32,4,2048]{2,1,0:T(4,128)(2,1)} %reshape.27), calls=%async_computation | async-start | bytes 1048576 | tf_op jit(solution)/shard_map/all_to_all | solution.py:33
  61.8 1.5 copy.22
  63.4 2.9 reshape.66
  66.3 24.8 %all-to-all-done = bf16[32,4,2048]{2,1,0:T(4,128)(2,1)} async-done(((bf16[32,4,2048]{2,1,0:T(4,128)(2,1)}), bf16[32,4,2048]{2,1,0:T(4,128)(2,1)}, u32[]{:S(2)}, u32[]{:S(2)}) %all-to-all-start) | async-done | bytes 524320 | tf_op jit(solution)/shard_map/all_to_all | solution.py:33
  91.1 4.2 %all-to-all-start.3 = ((bf16[4,2,32768]{2,1,0:T(2,128)(2,1)}), bf16[4,2,32768]{2,1,0:T(2,128)(2,1)S(1)}, u32[]{:S(2)}, u32[]{:S(2)}) async-start(bf16[4,2,32768]{2,1,0:T(2,128)(2,1)} %reshape.66), calls=%async_computation.3 | async-start | bytes 1048576 | tf_op jit(solution)/shard_map/all_to_all | solution.py:36
  95.3 3.1 copy.20
  98.4 2.9 reshape.68
  101.4 1.0 all-to-all-done.3
  102.4 4.1 %all-to-all-start.1 = ((bf16[4,2,32768]{2,1,0:T(2,128)(2,1)}), bf16[4,2,32768]{2,1,0:T(2,128)(2,1)}, u32[]{:S(2)}, u32[]{:S(2)}) async-start(bf16[4,2,32768]{2,1,0:T(2,128)(2,1)} %reshape.68), calls=%async_computation.1 | async-start | bytes 1048576 | tf_op jit(solution)/shard_map/all_to_all | solution.py:37
  106.6 1.1 reshape.67
  107.7 1.3 copy.23
  110.0 3.6 %all-to-all-done.1 = bf16[4,2,32768]{2,1,0:T(2,128)(2,1)} async-done(((bf16[4,2,32768]{2,1,0:T(2,128)(2,1)}), bf16[4,2,32768]{2,1,0:T(2,128)(2,1)}, u32[]{:S(2)}, u32[]{:S(2)}) %all-to-all-start.1) | async-done | bytes 524320 | tf_op jit(solution)/shard_map/all_to_all | solution.py:37
  113.6 2.9 reshape.69
  116.4 1.3 copy.21
  118.0 2.7 convolution_convert_fusion.2
  120.6 1.4 convolution_convert_fusion.3
  122.2 82.6 %all-reduce.4.cloned.1.call-done = (bf16[512,640]{1,0:T(8,128)(2,1)}, bf16[512,640]{1,0:T(8,128)(2,1)}) async-done(((bf16[512,640]{1,0:T(8,128)(2,1)}, bf16[512,640]{1,0:T(8,128)(2,1)}), (bf16[512,640]{1,0:T(8,128)(2,1)}, bf16[512,640]{1,0:T(8,128)(2,1)})) %all-reduce.4.cloned.1.call-update) | async-done | bytes 1310736 | tf_op jit(solution)/shard_map/psum | solution.py:49
  204.8 2.2 fusion.6
  207.6 1.0 copy.29
  208.6 85.2 %reduce-scatter.4.cloned.1.call-done = bf16[64,512]{1,0:T(8,128)(2,1)} async-done(((bf16[512,512]{1,0:T(8,128)(2,1)}), bf16[64,512]{1,0:T(8,128)(2,1)}) %reduce-scatter.4.cloned.1.call-update) | async-done | bytes 65552
  293.9 1.0 copy.30
  295.1 9.6 %all_to_all.50 = bf16[4,2,4096]{2,1,0:T(2,128)(2,1)S(1)} all-to-all(bf16[4,2,4096]{2,1,0:T(2,128)(2,1)S(1)} %reshape.70), channel_id=1, replica_groups=mesh['dp'=4,'expert'=32,'mp'=8] {'dp'}, dimensions={0} | all-to-all | bytes 131072 | tf_op jit(solution)/shard_map/all_to_all | solution.py:72
  305.6 14.2 %all-to-all-start.5 = ((bf16[32,2,512]{2,1,0:T(2,128)(2,1)}), bf16[32,2,512]{2,1,0:T(2,128)(2,1)S(1)}, u32[]{:S(2)}, u32[]{:S(2)}) async-start(bf16[32,2,512]{2,1,0:T(2,128)(2,1)} %reshape.72), calls=%async_computation.5 | async-start | bytes 131072 | tf_op jit(solution)/shard_map/all_to_all | solution.py:71
  319.8 1.4 fusion.11
  321.3 1.6 fusion.12
  322.9 8.4 %all-to-all-done.5 = bf16[32,2,512]{2,1,0:T(2,128)(2,1)S(1)} async-done(((bf16[32,2,512]{2,1,0:T(2,128)(2,1)}), bf16[32,2,512]{2,1,0:T(2,128)(2,1)S(1)}, u32[]{:S(2)}, u32[]{:S(2)}) %all-to-all-start.5) | async-done | bytes 65568 | tf_op jit(solution)/shard_map/all_to_all | solution.py:71
  (39 shorter events, 5.7 us)
Async XLA Ops:
  7.2 110.8 %copy-start = (bf16[1,512,640]{2,1,0:T(8,128)(2,1)S(1)}, bf16[1,512,640]{2,1,0:T(8,128)(2,1)}, u32[]{:S(2)}) copy-start(bf16[1,512,640]{2,1,0:T(8,128)(2,1)} %param.12) | copy-start | bytes 1966084
  9.9 17.0 %copy-start.2 = (bf16[128,2048]{1,0:T(8,128)(2,1)S(1)}, bf16[128,2048]{1,0:T(8,128)(2,1)}, u32[]{:S(2)}) copy-start(bf16[128,2048]{1,0:T(8,128)(2,1)} %param.8) | copy-start | bytes 1572868
  10.0 17.0 %copy-start.6 = (f32[128]{0:T(128)S(1)}, f32[128]{0:T(128)}, u32[]{:S(2)}) copy-start(f32[128]{0:T(128)} %param.9) | copy-start | bytes 1540
  11.0 45.1 %all-to-all-start.2 = ((bf16[32,4,2048]{2,1,0:T(4,128)(2,1)}), bf16[32,4,2048]{2,1,0:T(4,128)(2,1)S(1)}, u32[]{:S(2)}, u32[]{:S(2)}) async-start(bf16[32,4,2048]{2,1,0:T(4,128)(2,1)} %reshape.29), calls=%async_computation.2 | async-start | bytes 1048576 | tf_op jit(solution)/shard_map/all_to_all | solution.py:32
  56.1 35.0 %all-to-all-start = ((bf16[32,4,2048]{2,1,0:T(4,128)(2,1)}), bf16[32,4,2048]{2,1,0:T(4,128)(2,1)}, u32[]{:S(2)}, u32[]{:S(2)}) async-start(bf16[32,4,2048]{2,1,0:T(4,128)(2,1)} %reshape.27), calls=%async_computation | async-start | bytes 1048576 | tf_op jit(solution)/shard_map/all_to_all | solution.py:33
  91.1 11.3 %all-to-all-start.3 = ((bf16[4,2,32768]{2,1,0:T(2,128)(2,1)}), bf16[4,2,32768]{2,1,0:T(2,128)(2,1)S(1)}, u32[]{:S(2)}, u32[]{:S(2)}) async-start(bf16[4,2,32768]{2,1,0:T(2,128)(2,1)} %reshape.66), calls=%async_computation.3 | async-start | bytes 1048576 | tf_op jit(solution)/shard_map/all_to_all | solution.py:36
  102.4 11.1 %all-to-all-start.1 = ((bf16[4,2,32768]{2,1,0:T(2,128)(2,1)}), bf16[4,2,32768]{2,1,0:T(2,128)(2,1)}, u32[]{:S(2)}, u32[]{:S(2)}) async-start(bf16[4,2,32768]{2,1,0:T(2,128)(2,1)} %reshape.68), calls=%async_computation.1 | async-start | bytes 1048576 | tf_op jit(solution)/shard_map/all_to_all | solution.py:37
  106.6 98.2 %all-reduce.4.cloned.1.call-start = ((), (), s32[]{:S(2)}) async-start(), calls=%async_computation.8 | async-start | bytes 2621440 | tf_op jit(solution)/shard_map/psum | solution.py:49
  117.8 2.8 copy-start.7
  117.9 4.1 %copy-start.4 = (bf16[512,512]{1,0:T(8,128)(2,1)}, bf16[512,512]{1,0:T(8,128)(2,1)S(1)}, u32[]{:S(2)}) copy-start(bf16[512,512]{1,0:T(8,128)(2,1)S(1)} %reshape.28) | copy-start | bytes 1572868
  122.1 171.8 %reduce-scatter.4.cloned.1.call-start = ((), (), s32[]{:S(2)}) async-start(), calls=%async_computation.7 | async-start | bytes 589824
  208.6 111.2 %copy-start.3 = (bf16[512,512]{1,0:T(8,128)(2,1)S(1)}, bf16[512,512]{1,0:T(8,128)(2,1)}, u32[]{:S(2)}) copy-start(bf16[512,512]{1,0:T(8,128)(2,1)} %reshape.30) | copy-start | bytes 1572868
  304.6 16.6 %copy-start.1 = (bf16[512,640]{1,0:T(8,128)(2,1)S(1)}, bf16[512,640]{1,0:T(8,128)(2,1)}, u32[]{:S(2)}) copy-start(bf16[512,640]{1,0:T(8,128)(2,1)} %get-tuple-element.12) | copy-start | bytes 1966084
  304.6 16.6 %copy-start.5 = (bf16[512,512]{1,0:T(8,128)(2,1)S(1)}, bf16[512,512]{1,0:T(8,128)(2,1)}, u32[]{:S(2)}) copy-start(bf16[512,512]{1,0:T(8,128)(2,1)} %copy-done.4) | copy-start | bytes 1572868
  305.6 25.7 %all-to-all-start.5 = ((bf16[32,2,512]{2,1,0:T(2,128)(2,1)}), bf16[32,2,512]{2,1,0:T(2,128)(2,1)S(1)}, u32[]{:S(2)}, u32[]{:S(2)}) async-start(bf16[32,2,512]{2,1,0:T(2,128)(2,1)} %reshape.72), calls=%async_computation.5 | async-start | bytes 131072 | tf_op jit(solution)/shard_map/all_to_all | solution.py:71
Sparse Core Ops, SparseCore 0:
  122.2 82.5 all-reduce.3
  208.8 85.0 reduce-scatter.3
where the time goes:
time: 341 us; the launch traced here: 340 us
  waiting for transfers between devices  232 us (68%)
  starting transfers between devices  44.2 us (13%)
  local copies, waits for them, and re-layouts  27.4 us (8%)
  between operations  14.3 us (4%)
  blocking collectives  9.58 us (3%)
  matrix products  7.81 us (2%)
  other arithmetic  4.52 us (1%)
    unnamed x3, waiting for transfers between devices  85.3 us
    psum x1, waiting for transfers between devices, local(): lax.psum(hidden_part.astype(jnp.bfloat16), 'dp').astype(jnp.float32)  82.6 us
    all_to_all x1, waiting for transfers between devices, local(): lax.all_to_all(send_x, 'expert', split_axis=0, concat_axis=0, tiled=True)  26.5 us
    all_to_all x1, waiting for transfers between devices, local(): lax.all_to_all(send_dy, 'expert', split_axis=0, concat_axis=0, tiled=True)  24.8 us
    all_to_all x1, starting transfers between devices, local(): lax.all_to_all(send_x, 'expert', split_axis=0, concat_axis=0, tiled=True)  15.9 us
    all_to_all x1, starting transfers between devices, local(): lax.all_to_all(lax.all_to_all(send_back, 'dp', split_axis=2, concat_axis=...  14.2 us
    unnamed x28, local copies, waits for them, and re-layouts  13.8 us
    all_to_all x1, blocking collectives, local(): lax.all_to_all(send_back, 'dp', split_axis=2, concat_axis=2, tiled=True)  9.58 us
  transfers between devices with their start and end apart: 7, of which 7 were waited for; matrix products, arithmetic and copies ran while one was open for 6% of the time, Pallas kernels for 0%

commit v1 on v0

v1 whole, which is shorter than its diff:
```python
import jax
import jax.numpy as jnp
from jax import lax
from jax.experimental import pallas as pl
from jax.experimental.pallas import tpu as pltpu
from jax.sharding import Mesh, PartitionSpec as P

tanh_scale = 0.7978845608028654
cubic_coef = 0.044715
f32 = jnp.float32
bf16 = jnp.bfloat16


def gelu_pair(pre_act):
    tanh_arg = tanh_scale * (pre_act + cubic_coef * pre_act * pre_act * pre_act)
    tanh_val = jnp.tanh(tanh_arg)
    gelu_value = 0.5 * pre_act * (1.0 + tanh_val)
    gelu_slope = 0.5 * (1.0 + tanh_val) + 0.5 * pre_act * (
        1.0 - tanh_val * tanh_val
    ) * tanh_scale * (1.0 + 3.0 * cubic_coef * pre_act * pre_act)
    return (gelu_value, gelu_slope)


def dot(a, b, dims):
    return lax.dot_general(a, b, ((dims[0], dims[1]), ((), ())), preferred_element_type=f32)


def call(kernel, outs, *args, flops=0):
    moved = sum(a.size * a.dtype.itemsize for a in args) + sum(
        jnp.dtype(d).itemsize * size(s) for s, d in outs
    )
    core = lax.axis_index("c").astype(jnp.int32).reshape(1)
    return pl.pallas_call(
        kernel,
        out_shape=[jax.ShapeDtypeStruct(s, d) for s, d in outs],
        in_specs=[pl.BlockSpec(memory_space=pltpu.SMEM)]
        + [pl.BlockSpec(memory_space=pltpu.VMEM)] * len(args),
        out_specs=[pl.BlockSpec(memory_space=pltpu.VMEM)] * len(outs),
        compiler_params=pltpu.CompilerParams(vmem_limit_bytes=32 * 1024 * 1024),
        cost_estimate=pl.CostEstimate(flops=flops, bytes_accessed=moved, transcendentals=0),
    )(core, *args)


def size(shape):
    n = 1
    for s in shape:
        n *= s
    return n


def slot_onehot(expert_id, token_slot, half, rows):
    low = token_slot - 2 * half
    target = jnp.where((low >= 0) & (low < 2), expert_id * 2 + low, -1)
    at = lax.broadcasted_iota(jnp.int32, (rows, expert_id.shape[1]), 0)
    return at == target


def dispatch_kernel(core, eid, slot, gate, tok, cot, out):
    quarters, feats = 4, out.shape[3]
    xs, rows = out.shape[0] // quarters, out.shape[2]
    hit = slot_onehot(eid[...], slot[...], core[0], xs * rows)
    onehot = hit.astype(f32).astype(bf16)
    row_gate = jnp.sum(jnp.where(hit, gate[...], 0.0), axis=1, keepdims=True)
    for q in range(quarters):
        cols = slice(q * feats, (q + 1) * feats)
        got_x = dot(onehot, tok[:, cols], ((1,), (0,))).astype(bf16)
        got_dy = (row_gate * dot(onehot, cot[:, cols], ((1,), (0,)))).astype(bf16)
        for x in range(xs):
            out[q * xs + x, 0] = got_x[x * rows : (x + 1) * rows]
            out[q * xs + x, 1] = got_dy[x * rows : (x + 1) * rows]


def swap_matrix(outer, inner):
    n = outer * inner * 2
    row = lax.broadcasted_iota(jnp.int32, (n, n), 0)
    col = lax.broadcasted_iota(jnp.int32, (n, n), 1)
    pair = row // 2
    source = ((pair % outer) * inner + pair // outer) * 2 + row % 2
    return (source == col).astype(f32).astype(bf16)


def regroup_kernel(core, got, out):
    perm = swap_matrix(got.shape[0], out.shape[0])
    n = perm.shape[0]
    for which in range(2):
        rows = got[:, which].reshape(n, -1)
        moved = dot(perm, rows, ((1,), (0,))).astype(bf16)
        out[:, which] = moved.reshape(out.shape[0], out.shape[2], -1)


def parts_kernel(core, own, other, w_in, w_out, out):
    half = out.shape[0] // 2
    hid = w_in.shape[1]
    for at, src in ((0, own), (half, other)):
        x = src[:, 0].reshape(half, -1)
        dy = src[:, 1].reshape(half, -1)
        out[at : at + half, :hid] = dot(x, w_in[...], ((1,), (0,))).astype(bf16)
        out[at : at + half, hid:] = dot(dy, w_out[...], ((1,), (1,))).astype(bf16)


def gelu_kernel(core, got, dh, act):
    hid = dh.shape[2]
    total = got[0].astype(f32)
    for q in range(1, got.shape[0]):
        total = total + got[q].astype(f32)
    gelu_value, gelu_slope = gelu_pair(total[:, :hid])
    activation = gelu_value.astype(bf16)
    d_hidden = (total[:, hid:] * gelu_slope).astype(bf16)
    for q in range(got.shape[0]):
        dh[q] = d_hidden
        act[q] = activation


def back_kernel(core, dh, w_in, mine, theirs):
    hs, block = 4, w_in.shape[0] // 8
    for out, c in ((theirs, 1 - core[0]), (mine, core[0])):
        w = jnp.concatenate(
            [
                w_in[pl.ds(pl.multiple_of(h * 2 * block + c * block, block), block), :]
                for h in range(hs)
            ],
            axis=0,
        )
        out[...] = dot(dh[...], w, ((1,), (1,))).astype(out.dtype)


def pack_kernel(core, mine, got, out):
    ls, hs, rows, lanes = out.shape
    half = mine.shape[0] // 2
    own = (mine[:half] + got[half:].astype(f32)).astype(bf16)
    other = (mine[half:] + got[:half].astype(f32)).astype(bf16)
    f = lanes // 2
    for h in range(hs):
        cols = slice(h * f, (h + 1) * f)
        both = jnp.concatenate([own[:, cols], other[:, cols]], axis=1)
        out[:, h] = both.reshape(ls, rows, lanes)


def sum_kernel(core, got, out):
    ls, hs, rows, lanes = got.shape
    total = got[:, 0].astype(f32)
    for h in range(1, hs):
        total = total + got[:, h].astype(f32)
    total = total.astype(bf16).reshape(ls * rows, lanes)
    perm = swap_matrix(ls, rows // 2)
    out[...] = dot(perm, total, ((1,), (0,))).astype(bf16).reshape(out.shape)


def token_kernel(core, eid, slot, got, out):
    quarters, f = out.shape[0], out.shape[1]
    xs = got.shape[0] // quarters
    rows = xs * got.shape[1]
    first = slot_onehot(eid[...], slot[...], core[0], rows).astype(f32).astype(bf16)
    second = slot_onehot(eid[...], slot[...], 1 - core[0], rows).astype(f32).astype(bf16)
    for q in range(quarters):
        table = got[q * xs : (q + 1) * xs].reshape(rows, 2 * f)
        low = dot(table, first, ((0,), (0,)))
        high = dot(table, second, ((0,), (0,)))
        out[q] = (low[:f] + high[f:]).astype(bf16)


def grads_kernel(core, own, other, dh, act, g_in, g_out):
    half = dh.shape[0] // 2
    x = jnp.concatenate([own[:, 0].reshape(half, -1), other[:, 0].reshape(half, -1)], axis=0)
    g_in[...] = dot(x, dh[...], ((0,), (0,))).astype(bf16)
    dy = jnp.concatenate([own[:, 1].reshape(half, -1), other[:, 1].reshape(half, -1)], axis=0)
    g_out[...] = dot(act[...], dy, ((0,), (0,))).astype(bf16)


def exchange(x, axes):
    return lax.all_to_all(x, axes, split_axis=0, concat_axis=0, tiled=True)


def other_core(x):
    return lax.ppermute(x, "c", [(0, 1), (1, 0)])


def local(tokens, cotangent, gate_value, expert_id, token_slot, w_in, w_out):
    ys, xs, ls, hs = (lax.axis_size(a) for a in ("y", "x", "l", "h"))
    width, hid = w_in.shape[1:]
    toks = tokens.shape[0]
    w_in, w_out = w_in[0], w_out[0]
    eid, slot, gate = (a.reshape(1, toks) for a in (expert_id, token_slot, gate_value))
    yx, rows = ys * xs, ys * xs * ls * 4
    (sent,) = call(dispatch_kernel, [((yx, 2, ls * 2, width), bf16)], eid, slot, gate, tokens, cotangent)
    got = exchange(sent, ("y", "x"))
    (sent,) = call(regroup_kernel, [((ls, 2, yx * 2, width), bf16)], got)
    own = exchange(sent, "l")
    other = other_core(own)
    (parts,) = call(parts_kernel, [((rows, 2 * hid), bf16)], own, other, w_in, w_out)
    got = exchange(parts.reshape(ys, rows // ys, 2 * hid), "y")
    dh, act = call(gelu_kernel, [((ys, rows // ys, hid), bf16)] * 2, got)
    dh = exchange(dh, "y").reshape(rows, hid)
    act = exchange(act, "y").reshape(rows, hid)
    mine, theirs = call(back_kernel, [((rows, width // 2), f32), ((rows, width // 2), bf16)], dh, w_in)
    got = other_core(theirs)
    f = width // 8
    (sent,) = call(pack_kernel, [((ls, hs, yx * 2, 2 * f), bf16)], mine, got)
    sent = sent.reshape(ls * hs, yx * 2, 2 * f)
    got = exchange(sent, ("l", "h")).reshape(ls, hs, yx * 2, 2 * f)
    g_in, g_out = call(grads_kernel, [((width, hid), bf16), ((hid, width), bf16)], own, other, dh, act)
    (sent,) = call(sum_kernel, [((yx, ls * 2, 2 * f), bf16)], got)
    got = exchange(sent, ("y", "x"))
    (grad_t,) = call(token_kernel, [((ys, f, toks), bf16)], eid, slot, got)
    return jnp.transpose(grad_t, (2, 0, 1)), g_in[None], g_out[None]


def solution(mesh):
    dp, expert, mp = mesh.devices.shape
    fine = Mesh(mesh.devices.reshape(dp, 4, expert // 4, mp // 2, 2), ("y", "x", "l", "h", "c"))
    group, ffn = ("y", "x", "l"), ("h", "c")
    in_specs = (
        P(group, None),
        P(group, None),
        P(group),
        P(group),
        P(group),
        P(("x", "l"), "y", ffn),
        P(("x", "l"), ffn, "y"),
    )
    out_specs = (P(group, None, ffn), P(("x", "l"), "y", ffn), P(("x", "l"), ffn, "y"))
    return jax.shard_map(local, mesh=fine, in_specs=in_specs, out_specs=out_specs, check_vma=False)
```

time: 341 us -> 189 us (0.55)
  the two profiles are of different devices: /device:TPU:1 before, /device:TPU:64 now
where the time goes in v1:
time: 189 us; the launch traced here: 188 us
  blocking collectives  148 us (78%)
  waiting for transfers between devices  17.9 us (9%)
  starting transfers between devices  10.8 us (6%)
  Pallas kernels  6.96 us (4%)
  local copies, waits for them, and re-layouts  4.05 us (2%)
    all_to_all x5, blocking collectives, exchange(): return lax.all_to_all(x, axes, split_axis=0, concat_axis=0, tiled=True)  148 us
    all_to_all x2, waiting for transfers between devices, exchange(): return lax.all_to_all(x, axes, split_axis=0, concat_axis=0, tiled=True)  14.5 us
    all_to_all x2, starting transfers between devices, exchange(): return lax.all_to_all(x, axes, split_axis=0, concat_axis=0, tiled=True)  6.99 us
    pallas_call x9, Pallas kernels, call(): pl.pallas_call(kernel, out_shape=[jax.ShapeDtypeStruct(s, d) for s, d in...  6.96 us
    unnamed x18, local copies, waits for them, and re-layouts  4.05 us
    ppermute x2, starting transfers between devices, other_core(): return lax.ppermute(x, 'c', [(0, 1), (1, 0)])  3.83 us
  transfers between devices with their start and end apart: 4, of which 4 were waited for; matrix products, arithmetic and copies ran while one was open for 0% of the time, Pallas kernels for 1%

profile of v1, /device:TPU:64, one launch (start us, length us, event | category | flops | bytes accessed | tf_op | source)
XLA Modules:
  0.0 188.2 jit_solution(5364838220763284177)
XLA Ops:
  0.6 0.0 copy-start.2
  0.6 1.0 copy-done.2
  1.7 1.0 copy-done.3
  2.7 0.7 copy-done.4
  3.4 0.7 copy-done.6
  4.0 0.7 copy-done.8
  4.7 0.3 shard_map.94
  5.0 18.4 %all_to_all.35.got = bf16[16,2,16,512]{3,2,1,0:T(8,128)(2,1)S(1)} all-to-all(bf16[16,2,16,512]{3,2,1,0:T(8,128)(2,1)S(1)} %shard_map.94), channel_id=1, replica_groups=mesh['y'=4,'x'=4,'l'=8,'h'=4,'c'=2] {'y','x'}, dimensions={0} | all-to-all | bytes 1048576 | tf_op jit(solution)/shard_map/all_to_all | solution.py:171
  23.4 0.3 shard_map.95
  23.7 36.4 %all_to_all.36.own = bf16[8,2,32,512]{3,2,1,0:T(8,128)(2,1)S(1)} all-to-all(bf16[8,2,32,512]{3,2,1,0:T(8,128)(2,1)S(1)} %shard_map.95), channel_id=1, replica_groups=mesh['y'=4,'x'=4,'l'=8,'h'=4,'c'=2] {'l'}, dimensions={0} | all-to-all | bytes 1048576 | tf_op jit(solution)/shard_map/all_to_all | solution.py:171
  60.0 1.9 %collective-permute-start = (bf16[8,2,32,512]{3,2,1,0:T(8,128)(2,1)S(1)}, bf16[8,2,32,512]{3,2,1,0:T(8,128)(2,1)S(1)}, u32[]{:S(2)}, u32[]{:S(2)}) collective-permute-start(bf16[8,2,32,512]{3,2,1,0:T(8,128)(2,1)S(1)} %all_to_all.36.own), channel_id=1, source_target_pairs={{0,1},{1,0},{2,3},{3,2},{4,5},{5,4},{6,7},{7,6},{8,9},{9,8},{10,11... | collective-permute-start | bytes 1572872 | tf_op jit(solution)/shard_map/ppermute | solution.py:175
  61.9 1.9 collective-permute-done.other
  63.8 0.0 copy-done
  63.8 0.0 copy-done.1
  63.8 1.0 shard_map.96
  64.8 20.9 %all_to_all.37.got = bf16[4,128,1280]{2,1,0:T(8,128)(2,1)S(1)} all-to-all(bf16[4,128,1280]{2,1,0:T(8,128)(2,1)S(1)} %bitcast.16), channel_id=1, replica_groups=mesh['y'=4,'x'=4,'l'=8,'h'=4,'c'=2] {'y'}, dimensions={0} | all-to-all | bytes 2621440 | tf_op jit(solution)/shard_map/all_to_all | solution.py:171
  85.8 1.1 shard_map.97
  86.8 13.0 %all_to_all.38 = bf16[4,128,640]{2,1,0:T(8,128)(2,1)S(1)} all-to-all(bf16[4,128,640]{2,1,0:T(8,128)(2,1)S(1)} %get-tuple-element.9), channel_id=1, replica_groups=mesh['y'=4,'x'=4,'l'=8,'h'=4,'c'=2] {'y'}, dimensions={0} | all-to-all | bytes 1310720 | tf_op jit(solution)/shard_map/all_to_all | solution.py:171
  99.8 0.6 shard_map.98
  100.5 1.9 %collective-permute-start.1 = (bf16[512,256]{1,0:T(8,128)(2,1)S(1)}, bf16[512,256]{1,0:T(8,128)(2,1)S(1)}, u32[]{:S(2)}, u32[]{:S(2)}) collective-permute-start(bf16[512,256]{1,0:T(8,128)(2,1)S(1)} %get-tuple-element.11), channel_id=1, source_target_pairs={{0,1},{1,0},{2,3},{3,2},{4,5},{5,4},{6,7},{7,6},{8,9},{9,8},{10,11... | collective-permute-start | bytes 786440 | tf_op jit(solution)/shard_map/ppermute | solution.py:175
  102.4 1.5 collective-permute-done.1.got
  103.9 0.2 shard_map.99
  104.1 59.0 %all_to_all.39 = bf16[32,32,128]{2,1,0:T(8,128)(2,1)S(1)} all-to-all(bf16[32,32,128]{2,1,0:T(8,128)(2,1)S(1)} %bitcast.21), channel_id=1, replica_groups=mesh['y'=4,'x'=4,'l'=8,'h'=4,'c'=2] {'l','h'}, dimensions={0} | all-to-all | bytes 524288 | tf_op jit(solution)/shard_map/all_to_all | solution.py:171
  163.1 3.5 %all-to-all-start.6 = ((bf16[4,128,640]{2,1,0:T(8,128)(2,1)}), bf16[4,128,640]{2,1,0:T(8,128)(2,1)S(1)}, u32[]{:S(2)}, u32[]{:S(2)}) async-start(bf16[4,128,640]{2,1,0:T(8,128)(2,1)} %get-tuple-element.12), calls=%async_computation.6 | async-start | bytes 1310720 | tf_op jit(solution)/shard_map/all_to_all | solution.py:171
  166.6 0.9 shard_map.100
  167.4 8.7 %all-to-all-done.6 = bf16[4,128,640]{2,1,0:T(8,128)(2,1)S(1)} async-done(((bf16[4,128,640]{2,1,0:T(8,128)(2,1)}), bf16[4,128,640]{2,1,0:T(8,128)(2,1)S(1)}, u32[]{:S(2)}, u32[]{:S(2)}) %all-to-all-start.6) | async-done | bytes 655392 | tf_op jit(solution)/shard_map/all_to_all | solution.py:171
  176.2 3.5 %all-to-all-start.5 = ((bf16[16,16,128]{2,1,0:T(8,128)(2,1)}), bf16[16,16,128]{2,1,0:T(8,128)(2,1)S(1)}, u32[]{:S(2)}, u32[]{:S(2)}) async-start(bf16[16,16,128]{2,1,0:T(8,128)(2,1)} %shard_map.100), calls=%async_computation.5 | async-start | bytes 131072 | tf_op jit(solution)/shard_map/all_to_all | solution.py:171
  179.7 1.8 shard_map.102
  181.5 5.8 %all-to-all-done.5.got = bf16[16,16,128]{2,1,0:T(8,128)(2,1)S(1)} async-done(((bf16[16,16,128]{2,1,0:T(8,128)(2,1)}), bf16[16,16,128]{2,1,0:T(8,128)(2,1)S(1)}, u32[]{:S(2)}, u32[]{:S(2)}) %all-to-all-start.5) | async-done | bytes 65568 | tf_op jit(solution)/shard_map/all_to_all | solution.py:171
  187.3 0.0 copy-done.5
  187.3 0.0 copy-done.7
  187.3 0.9 shard_map.101
  (8 shorter events, 0.0 us)
Async XLA Ops:
  0.6 1.0 copy-start.2
  1.7 1.0 copy-start.3
  2.7 0.7 copy-start.4
  3.4 0.7 copy-start.6
  4.0 0.7 copy-start.8
  23.4 40.5 %copy-start = (bf16[1,512,640]{2,1,0:T(8,128)(2,1)S(1)}, bf16[1,512,640]{2,1,0:T(8,128)(2,1)}, u32[]{:S(2)}) copy-start(bf16[1,512,640]{2,1,0:T(8,128)(2,1)} %param.12) | copy-start | bytes 1966084
  23.4 40.5 %copy-start.1 = (bf16[1,640,512]{2,1,0:T(8,128)(2,1)S(1)}, bf16[1,640,512]{2,1,0:T(8,128)(2,1)}, u32[]{:S(2)}) copy-start(bf16[1,640,512]{2,1,0:T(8,128)(2,1)} %param.13) | copy-start | bytes 1966084
  60.0 3.8 %collective-permute-start = (bf16[8,2,32,512]{3,2,1,0:T(8,128)(2,1)S(1)}, bf16[8,2,32,512]{3,2,1,0:T(8,128)(2,1)S(1)}, u32[]{:S(2)}, u32[]{:S(2)}) collective-permute-start(bf16[8,2,32,512]{3,2,1,0:T(8,128)(2,1)S(1)} %all_to_all.36.own), channel_id=1, source_target_pairs={{0,1},{1,0},{2,3},{3,2},{4,5},{5,4},{6,7},{7,6},{8,9},{9,8},{10,11... | collective-permute-start | bytes 1572872 | tf_op jit(solution)/shard_map/ppermute | solution.py:175
  100.5 3.4 %collective-permute-start.1 = (bf16[512,256]{1,0:T(8,128)(2,1)S(1)}, bf16[512,256]{1,0:T(8,128)(2,1)S(1)}, u32[]{:S(2)}, u32[]{:S(2)}) collective-permute-start(bf16[512,256]{1,0:T(8,128)(2,1)S(1)} %get-tuple-element.11), channel_id=1, source_target_pairs={{0,1},{1,0},{2,3},{3,2},{4,5},{5,4},{6,7},{7,6},{8,9},{9,8},{10,11... | collective-permute-start | bytes 786440 | tf_op jit(solution)/shard_map/ppermute | solution.py:175
  163.1 13.1 %all-to-all-start.6 = ((bf16[4,128,640]{2,1,0:T(8,128)(2,1)}), bf16[4,128,640]{2,1,0:T(8,128)(2,1)S(1)}, u32[]{:S(2)}, u32[]{:S(2)}) async-start(bf16[4,128,640]{2,1,0:T(8,128)(2,1)} %get-tuple-element.12), calls=%async_computation.6 | async-start | bytes 1310720 | tf_op jit(solution)/shard_map/all_to_all | solution.py:171
  167.4 19.9 %copy-start.5 = (s32[128]{0:T(128)S(1)}, s32[128]{0:T(128)}, u32[]{:S(2)}) copy-start(s32[128]{0:T(128)} %param.10) | copy-start | bytes 1540
  167.4 19.9 %copy-start.7 = (s32[128]{0:T(128)S(1)}, s32[128]{0:T(128)}, u32[]{:S(2)}) copy-start(s32[128]{0:T(128)} %param.11) | copy-start | bytes 1540
  176.2 11.1 %all-to-all-start.5 = ((bf16[16,16,128]{2,1,0:T(8,128)(2,1)}), bf16[16,16,128]{2,1,0:T(8,128)(2,1)S(1)}, u32[]{:S(2)}, u32[]{:S(2)}) async-start(bf16[16,16,128]{2,1,0:T(8,128)(2,1)} %shard_map.100), calls=%async_computation.5 | async-start | bytes 131072 | tf_op jit(solution)/shard_map/all_to_all | solution.py:171

commit v2 on v1

v2 whole, which is shorter than its diff:
```python
import jax
import jax.numpy as jnp
from jax import lax
from jax.experimental import pallas as pl
from jax.experimental.pallas import tpu as pltpu
from jax.sharding import Mesh, PartitionSpec as P

tanh_scale = 0.7978845608028654
cubic_coef = 0.044715
f32 = jnp.float32
bf16 = jnp.bfloat16


def gelu_pair(pre_act):
    tanh_arg = tanh_scale * (pre_act + cubic_coef * pre_act * pre_act * pre_act)
    tanh_val = jnp.tanh(tanh_arg)
    gelu_value = 0.5 * pre_act * (1.0 + tanh_val)
    gelu_slope = 0.5 * (1.0 + tanh_val) + 0.5 * pre_act * (
        1.0 - tanh_val * tanh_val
    ) * tanh_scale * (1.0 + 3.0 * cubic_coef * pre_act * pre_act)
    return (gelu_value, gelu_slope)


def dot(a, b, dims):
    return lax.dot_general(a, b, ((dims[0], dims[1]), ((), ())), preferred_element_type=f32)


def size(shape):
    n = 1
    for s in shape:
        n *= s
    return n


def call(kernel, outs, *args, scratch=(), fetch=False, after=()):
    moved = sum(a.size * a.dtype.itemsize for a in args) + sum(
        jnp.dtype(d).itemsize * size(s) for s, d in outs
    )
    place = lax.axis_index(("h", "c")).astype(jnp.int32).reshape(1)
    space = pltpu.HBM if fetch else pltpu.VMEM
    return pl.pallas_call(
        kernel,
        out_shape=[jax.ShapeDtypeStruct(s, d) for s, d in outs],
        in_specs=[pl.BlockSpec(memory_space=pltpu.SMEM)]
        + [pl.BlockSpec(memory_space=space)] * len(args)
        + [pl.BlockSpec(memory_space=pl.ANY)] * len(after),
        out_specs=[pl.BlockSpec(memory_space=pltpu.VMEM)] * len(outs),
        scratch_shapes=scratch,
        compiler_params=pltpu.CompilerParams(vmem_limit_bytes=(60 if fetch else 32) * 1024 * 1024),
        cost_estimate=pl.CostEstimate(flops=0, bytes_accessed=moved, transcendentals=0),
    )(place, *args, *after)


def core(place):
    return place[0] & 1


def as_bf16(mask):
    return mask.astype(f32).astype(bf16)


def dispatch_kernel(place, eid, slot, gate, tok, cot, out, eid_v, slot_v, gate_v, tok_v, cot_v, sems):
    quarters, toks, feats = tok_v.shape
    count = out.shape[0] // quarters
    copies = [
        pltpu.make_async_copy(src, dst, sems.at[i])
        for i, (src, dst) in enumerate(((eid, eid_v), (slot, slot_v), (gate, gate_v)))
    ]
    for src, dst in ((tok, tok_v), (cot, cot_v)):
        for q in range(quarters):
            cols = pl.ds(pl.multiple_of((2 * q + core(place)) * feats, feats), feats)
            copies.append(pltpu.make_async_copy(src.at[:, cols], dst.at[q], sems.at[len(copies)]))
    for copy in copies:
        copy.start()
    for copy in copies[:3]:
        copy.wait()
    row = lax.broadcasted_iota(jnp.int32, (count, toks), 0)
    hit = (row // 8 == eid_v[...]) & (row % 4 == slot_v[...])
    is_x = row % 8 < 4
    take_x = as_bf16(hit & is_x)
    take_dy = as_bf16(hit & ~is_x)
    row_gate = jnp.sum(jnp.where(hit, gate_v[...], 0.0), axis=1, keepdims=True)
    for copy in copies[3:]:
        copy.wait()
    for q in range(quarters):
        got_x = dot(take_x, tok_v[q], ((1,), (0,)))
        got_dy = row_gate * dot(take_dy, cot_v[q], ((1,), (0,)))
        out[q * count : (q + 1) * count] = (got_x + got_dy).astype(bf16)


def regroup_kernel(place, got, out):
    ys, xs = 4, 4
    count = got.shape[0] // ys
    ls = count // (8 * xs)
    n = lax.broadcasted_iota(jnp.int32, (count, count), 0)
    col = lax.broadcasted_iota(jnp.int32, (count, count), 1)
    part = 2 * xs * ls
    low, x, at_l, s_hi, which = (
        n % 2,
        (n // 2) % xs,
        (n // (2 * xs)) % ls,
        (n // part) % 2,
        n // (2 * part),
    )
    perm = as_bf16(col == ((x * ls + at_l) * 2 + which) * 4 + s_hi * 2 + low)
    rows = [dot(perm, got[y * count : (y + 1) * count], ((1,), (0,))) for y in range(ys)]
    width = 2 * xs
    for which in range(2):
        for s_hi in range(2):
            for at_l in range(ls):
                source = slice(
                    which * 2 * part + s_hi * part + at_l * width,
                    which * 2 * part + s_hi * part + (at_l + 1) * width,
                )
                for y in range(0, ys, 2):
                    both = jnp.concatenate([rows[y][source], rows[y + 1][source]], axis=0)
                    at = (s_hi * ls + at_l) * ys * width + y * width
                    out[which, at : at + 2 * width] = both.astype(bf16)


def swap_matrix(outer, inner):
    n = outer * inner * 2
    row = lax.broadcasted_iota(jnp.int32, (n, n), 0)
    col = lax.broadcasted_iota(jnp.int32, (n, n), 1)
    pair = row // 2
    source = ((pair % outer) * inner + pair // outer) * 2 + row % 2
    return as_bf16(source == col)


def halves(place, ref, axis):
    n = ref.shape[axis] // 2
    for c in (core(place), 1 - core(place)):
        part = pl.ds(pl.multiple_of(c * n, n), n)
        yield ref[part, :] if axis == 0 else ref[:, part]


def parts_kernel(place, own, other, w_in, w_out, out):
    hid = w_in.shape[1]
    (in_own, in_other), (out_own, out_other) = halves(place, w_in, 0), halves(place, w_out, 1)
    out[:, :hid] = (
        dot(own[0], in_own, ((1,), (0,))) + dot(other[0], in_other, ((1,), (0,)))
    ).astype(bf16)
    out[:, hid:] = (
        dot(own[1], out_own, ((1,), (1,))) + dot(other[1], out_other, ((1,), (1,)))
    ).astype(bf16)


def gelu_kernel(place, got, dh, act):
    hid = dh.shape[2]
    total = got[0].astype(f32)
    for q in range(1, got.shape[0]):
        total = total + got[q].astype(f32)
    gelu_value, gelu_slope = gelu_pair(total[:, :hid])
    d_hidden = (total[:, hid:] * gelu_slope).astype(bf16)
    for q in range(got.shape[0]):
        dh[q] = d_hidden
    act[...] = gelu_value.astype(bf16)


def back_kernel(place, dh, w_in, mine, theirs):
    hs, block = 4, w_in.shape[0] // 8
    for out, c in ((theirs, 1 - core(place)), (mine, core(place))):
        w = jnp.concatenate(
            [
                w_in[pl.ds(pl.multiple_of(h * 2 * block + c * block, block), block), :]
                for h in range(hs)
            ],
            axis=0,
        )
        out[...] = dot(dh[...], w, ((1,), (1,))).astype(out.dtype)


def pack_kernel(place, mine, got, act, send_p, send_q, keep, acts, total):
    for q in range(acts.shape[0]):
        acts[q] = act[...]
    _, hs, rows, lanes = total.shape
    half, f, h = mine.shape[0] // 2, lanes // 2, place[0] >> 1
    both = mine[...] + got[...].astype(f32)
    for at in range(hs):
        cols = slice(at * f, (at + 1) * f)
        packed = jnp.concatenate([both[:half, cols], both[half:, cols]], axis=1)
        for stream in range(2):
            total[stream, at] = packed[stream * rows : (stream + 1) * rows]
    near, far = h ^ 1, 3 - h
    send_p[0] = total[0, near].astype(bf16)
    send_p[1] = total[0, 3 - near].astype(bf16)
    send_q[0] = total[1, far].astype(bf16)
    send_q[1] = total[1, far ^ 1].astype(bf16)
    keep[0, 0] = total[0, h]
    keep[0, 1] = total[0, far]
    keep[1, 0] = total[1, h]
    keep[1, 1] = total[1, near]


def halve_kernel(place, keep, got_p, got_q, _, send_p, send_q, left):
    for stream, got, send in ((0, got_p, send_p), (1, got_q, send_q)):
        send[...] = (keep[stream, 1] + got[1].astype(f32)).astype(bf16)
        left[stream] = keep[stream, 0] + got[0].astype(f32)


def final_kernel(place, left, got_p, got_q, out):
    rows = left.shape[1]
    out[:rows] = (left[0] + got_p[...].astype(f32)).astype(bf16)
    out[rows:] = (left[1] + got_q[...].astype(f32)).astype(bf16)


def turn_kernel(place, got, out):
    yx, inner, lanes = out.shape
    perm = swap_matrix(inner // 2, yx)
    out[...] = dot(perm, got[...], ((1,), (0,))).astype(bf16).reshape(out.shape)


def token_kernel(place, eid, slot, got, out):
    quarters, f, toks = out.shape
    xs = got.shape[0] // quarters
    rows = xs * got.shape[1]
    row = lax.broadcasted_iota(jnp.int32, (rows, toks), 0)
    mine = row // 2 == eid[...]
    first = as_bf16(mine & (row % 2 == slot[...]))
    second = as_bf16(mine & (row % 2 == slot[...] - 2))
    for q in range(quarters):
        table = got[q * xs : (q + 1) * xs].reshape(rows, 2 * f)
        low = dot(table, first, ((0,), (0,)))
        high = dot(table, second, ((0,), (0,)))
        out[q] = (low[:f] + high[f:]).astype(bf16)


def grads_kernel(place, own, other, dh, act, g_in, g_out):
    n = own.shape[2]
    for src, c in ((own, core(place)), (other, 1 - core(place))):
        part = pl.ds(pl.multiple_of(c * n, n), n)
        g_in[part, :] = dot(src[0], dh[...], ((0,), (0,))).astype(bf16)
        g_out[:, part] = dot(act[...], src[1], ((0,), (0,))).astype(bf16)


def exchange(x, axes):
    return lax.all_to_all(x, axes, split_axis=0, concat_axis=0, tiled=True)


def other_core(x):
    return lax.ppermute(x, "c", [(0, 1), (1, 0)])


def over_h(x, pairing):
    return lax.ppermute(x, "h", [(h, pairing(h)) for h in range(4)])


def local(tokens, cotangent, gate_value, expert_id, token_slot, w_in, w_out):
    ys, xs, ls = (lax.axis_size(a) for a in ("y", "x", "l"))
    width, hid = w_in.shape[1:]
    toks = tokens.shape[0]
    w_in, w_out = w_in[0], w_out[0]
    eid, slot, gate = (a.reshape(1, toks) for a in (expert_id, token_slot, gate_value))
    yx, groups = ys * xs, ys * xs * ls
    rows, part, f = groups * 4, width // 2, width // 8
    near, far = (lambda h: h ^ 1), (lambda h: 3 - h)
    (sent,) = call(
        dispatch_kernel,
        [((groups * 8, part), bf16)],
        eid,
        slot,
        gate,
        tokens,
        cotangent,
        scratch=[
            pltpu.VMEM((1, toks), jnp.int32),
            pltpu.VMEM((1, toks), jnp.int32),
            pltpu.VMEM((1, toks), f32),
            pltpu.VMEM((ys, toks, part), bf16),
            pltpu.VMEM((ys, toks, part), bf16),
            pltpu.SemaphoreType.DMA((3 + 2 * ys,)),
        ],
        fetch=True,
    )
    got = exchange(sent.reshape(groups, 8, part), ("y", "x", "l")).reshape(groups * 8, part)
    (own,) = call(regroup_kernel, [((2, rows, part), bf16)], got)
    other = other_core(own)
    (parts,) = call(parts_kernel, [((rows, 2 * hid), bf16)], own, other, w_in, w_out)
    got = exchange(parts.reshape(ys, rows // ys, 2 * hid), "y")
    block = (rows // ys, hid)
    dh, act = call(gelu_kernel, [((ys,) + block, bf16), (block, bf16)], got)
    dh = exchange(dh, "y").reshape(rows, hid)
    mine, theirs = call(back_kernel, [((rows, part), f32), ((rows, part), bf16)], dh, w_in)
    got = other_core(theirs)
    tile = (rows // 4, 2 * f)
    send_p, send_q, keep, acts = call(
        pack_kernel,
        [((2,) + tile, bf16), ((2,) + tile, bf16), ((2, 2) + tile, f32), ((ys,) + block, bf16)],
        mine,
        got,
        act,
        scratch=[pltpu.VMEM((2, 4) + tile, f32)],
    )
    got_p, got_q = over_h(send_p, near), over_h(send_q, far)
    act = exchange(acts, "y").reshape(rows, hid)
    send_p, send_q, left = call(
        halve_kernel,
        [(tile, bf16), (tile, bf16), ((2,) + tile, f32)],
        keep,
        got_p,
        got_q,
        after=(act,),
    )
    got_p, got_q = over_h(send_p, far), over_h(send_q, near)
    (sent,) = call(final_kernel, [((rows // 2, 2 * f), bf16)], left, got_p, got_q)
    got = exchange(sent.reshape(ls, yx * 2, 2 * f), "l").reshape(rows // 2, 2 * f)
    (sent,) = call(turn_kernel, [((yx, ls * 2, 2 * f), bf16)], got)
    got = exchange(sent, ("y", "x"))
    g_in, g_out = call(grads_kernel, [((width, hid), bf16), ((hid, width), bf16)], own, other, dh, act)
    (grad_t,) = call(token_kernel, [((ys, f, toks), bf16)], eid, slot, got)
    return jnp.transpose(grad_t, (2, 0, 1)), g_in[None], g_out[None]


def solution(mesh):
    dp, expert, mp = mesh.devices.shape
    fine = Mesh(mesh.devices.reshape(dp, 4, expert // 4, mp // 2, 2), ("y", "x", "l", "h", "c"))
    group, ffn = ("y", "x", "l"), ("h", "c")
    in_specs = (
        P(group, None),
        P(group, None),
        P(group),
        P(group),
        P(group),
        P(("x", "l"), "y", ffn),
        P(("x", "l"), ffn, "y"),
    )
    out_specs = (P(group, None, ffn), P(("x", "l"), "y", ffn), P(("x", "l"), ffn, "y"))
    return jax.shard_map(local, mesh=fine, in_specs=in_specs, out_specs=out_specs, check_vma=False)
```

time: 189 us -> 192 us (1.016)
  the two profiles are of different devices: /device:TPU:64 before, /device:TPU:2 now
where the time goes in v2:
time: 192 us
  blocking collectives  104 us (54%)
  starting transfers between devices  53.6 us (28%)
  waiting for transfers between devices  23.8 us (12%)
  Pallas kernels  9.37 us (5%)
    all_to_all x4, blocking collectives, exchange(): return lax.all_to_all(x, axes, split_axis=0, concat_axis=0, tiled=True)  104 us
    ppermute x4, starting transfers between devices, over_h(): return lax.ppermute(x, 'h', [(h, pairing(h)) for h in range(4)])  38.7 us
    ppermute x4, waiting for transfers between devices, over_h(): return lax.ppermute(x, 'h', [(h, pairing(h)) for h in range(4)])  16 us
    all_to_all x2, starting transfers between devices, exchange(): return lax.all_to_all(x, axes, split_axis=0, concat_axis=0, tiled=True)  11 us
    pallas_call x11, Pallas kernels, call(): pl.pallas_call(kernel, out_shape=[jax.ShapeDtypeStruct(s, d) for s, d in...  9.37 us
    all_to_all x2, waiting for transfers between devices, exchange(): return lax.all_to_all(x, axes, split_axis=0, concat_axis=0, tiled=True)  4.45 us
    ppermute x2, starting transfers between devices, other_core(): return lax.ppermute(x, 'c', [(0, 1), (1, 0)])  3.84 us
  transfers between devices with their start and end apart: 8, of which 6 were waited for; matrix products, arithmetic and copies ran while one was open for 0% of the time, Pallas kernels for 1%

profile of v2, /device:TPU:2, one launch (start us, length us, event | category | flops | bytes accessed | tf_op | source)
XLA Modules:
  0.0 191.8 jit_solution(10414208829697896660)
XLA Ops:
  0.6 2.4 %shard_map.94 = bf16[1024,256]{1,0:T(8,128)(2,1)} custom-call(s32[1]{0:T(128)} %bitcast.place, s32[1,128]{1,0:T(1,128)} %bitcast.27, s32[1,128]{1,0:T(1,128)} %bitcast.29, f32[1,128]{1,0:T(1,128)} %bitcast.33, bf16[128,2048]{1,0:T(8,128)(2,1)} %tok.1, bf16[128,2048]{1,0:T(8,128)(2,1)} %cot.1), custom_call_target="tpu_custom_call" | custom-call | bytes 1574400 | tf_op jit(solution)/shard_map/pallas_call | solution.py:41
  3.1 0.0 copy-start
  3.1 0.0 copy-start.1
  3.1 49.5 %all_to_all.30 = bf16[128,8,256]{2,1,0:T(8,128)(2,1)S(1)} all-to-all(bf16[128,8,256]{2,1,0:T(8,128)(2,1)} %bitcast.31), channel_id=1, replica_groups=mesh['y'=4,'x'=4,'l'=8,'h'=4,'c'=2] {'y','x','l'}, dimensions={0} | all-to-all | bytes 1048576 | tf_op jit(solution)/shard_map/all_to_all | solution.py:237
  52.6 0.3 shard_map.95.own
  52.9 1.9 %collective-permute-start = (bf16[2,512,256]{2,1,0:T(8,128)(2,1)S(1)}, bf16[2,512,256]{2,1,0:T(8,128)(2,1)S(1)}, u32[]{:S(2)}, u32[]{:S(2)}) collective-permute-start(bf16[2,512,256]{2,1,0:T(8,128)(2,1)S(1)} %shard_map.95.own), channel_id=1, source_target_pairs={{0,1},{1,0},{2,3},{3,2},{4,5},{5,4},{6,7},{7,6},{8,9},{9,8},{10,11... | collective-permute-start | bytes 1572872 | tf_op jit(solution)/shard_map/ppermute | solution.py:241
  54.8 1.9 collective-permute-done.other
  56.7 0.0 copy-done.1
  56.7 1.0 shard_map.96
  57.7 20.9 %all_to_all.31.got = bf16[4,128,1280]{2,1,0:T(8,128)(2,1)S(1)} all-to-all(bf16[4,128,1280]{2,1,0:T(8,128)(2,1)S(1)} %bitcast.20), channel_id=1, replica_groups=mesh['y'=4,'x'=4,'l'=8,'h'=4,'c'=2] {'y'}, dimensions={0} | all-to-all | bytes 2621440 | tf_op jit(solution)/shard_map/all_to_all | solution.py:237
  78.6 0.4 shard_map.97
  79.0 12.9 %all_to_all.32 = bf16[4,128,640]{2,1,0:T(8,128)(2,1)S(1)} all-to-all(bf16[4,128,640]{2,1,0:T(8,128)(2,1)S(1)} %get-tuple-element.16), channel_id=1, replica_groups=mesh['y'=4,'x'=4,'l'=8,'h'=4,'c'=2] {'y'}, dimensions={0} | all-to-all | bytes 1310720 | tf_op jit(solution)/shard_map/all_to_all | solution.py:237
  91.9 0.6 shard_map.98
  92.5 1.9 %collective-permute-start.1 = (bf16[512,256]{1,0:T(8,128)(2,1)S(1)}, bf16[512,256]{1,0:T(8,128)(2,1)S(1)}, u32[]{:S(2)}, u32[]{:S(2)}) collective-permute-start(bf16[512,256]{1,0:T(8,128)(2,1)S(1)} %get-tuple-element.18), channel_id=1, source_target_pairs={{0,1},{1,0},{2,3},{3,2},{4,5},{5,4},{6,7},{7,6},{8,9},{9,8},{10,11... | collective-permute-start | bytes 786440 | tf_op jit(solution)/shard_map/ppermute | solution.py:241
  94.4 1.5 collective-permute-done.1.got
  95.9 1.1 shard_map.99
  97.0 3.5 %all-to-all-start.3 = ((bf16[4,128,640]{2,1,0:T(8,128)(2,1)}), bf16[4,128,640]{2,1,0:T(8,128)(2,1)S(1)}, u32[]{:S(2)}, u32[]{:S(2)}) async-start(bf16[4,128,640]{2,1,0:T(8,128)(2,1)} %get-tuple-element.23), calls=%async_computation.3 | async-start | bytes 1310720 | tf_op jit(solution)/shard_map/all_to_all | solution.py:237
  100.5 15.7 %collective-permute-start.2 = (bf16[2,128,128]{2,1,0:T(8,128)(2,1)S(1)}, bf16[2,128,128]{2,1,0:T(8,128)(2,1)S(1)}, u32[]{:S(2)}, u32[]{:S(2)}) collective-permute-start(bf16[2,128,128]{2,1,0:T(8,128)(2,1)S(1)} %get-tuple-element.21), channel_id=1, source_target_pairs={{0,2},{2,0},{4,6},{6,4},{1,3},{3,1},{5,7},{7,5},{8,10},{10,8},{12,... | collective-permute-start | bytes 196616 | tf_op jit(solution)/shard_map/ppermute | solution.py:245
  116.2 8.2 %collective-permute-start.3 = (bf16[2,128,128]{2,1,0:T(8,128)(2,1)S(1)}, bf16[2,128,128]{2,1,0:T(8,128)(2,1)S(1)}, u32[]{:S(2)}, u32[]{:S(2)}) collective-permute-start(bf16[2,128,128]{2,1,0:T(8,128)(2,1)S(1)} %get-tuple-element.22), channel_id=1, source_target_pairs={{0,6},{2,4},{4,2},{6,0},{1,7},{3,5},{5,3},{7,1},{8,14},{10,12},{12... | collective-permute-start | bytes 196616 | tf_op jit(solution)/shard_map/ppermute | solution.py:245
  124.4 4.5 %collective-permute-done.2.got_p = bf16[2,128,128]{2,1,0:T(8,128)(2,1)S(1)} collective-permute-done((bf16[2,128,128]{2,1,0:T(8,128)(2,1)S(1)}, bf16[2,128,128]{2,1,0:T(8,128)(2,1)S(1)}, u32[]{:S(2)}, u32[]{:S(2)}) %collective-permute-start.2) | collective-permute-done | bytes 65568 | tf_op jit(solution)/shard_map/ppermute | solution.py:245
  128.9 5.9 %collective-permute-done.3.got_q = bf16[2,128,128]{2,1,0:T(8,128)(2,1)S(1)} collective-permute-done((bf16[2,128,128]{2,1,0:T(8,128)(2,1)S(1)}, bf16[2,128,128]{2,1,0:T(8,128)(2,1)S(1)}, u32[]{:S(2)}, u32[]{:S(2)}) %collective-permute-start.3) | collective-permute-done | bytes 65568 | tf_op jit(solution)/shard_map/ppermute | solution.py:245
  134.8 0.0 all-to-all-done.3
  134.9 5.9 %collective-permute-start.4 = (bf16[128,128]{1,0:T(8,128)(2,1)S(1)}, bf16[128,128]{1,0:T(8,128)(2,1)S(1)}, u32[]{:S(2)}, u32[]{:S(2)}) collective-permute-start(bf16[128,128]{1,0:T(8,128)(2,1)S(1)} %get-tuple-element.25), channel_id=1, source_target_pairs={{0,6},{2,4},{4,2},{6,0},{1,7},{3,5},{5,3},{7,1},{8,14},{10,12},{12... | collective-permute-start | bytes 98312 | tf_op jit(solution)/shard_map/ppermute | solution.py:245
  140.8 8.9 %collective-permute-start.5 = (bf16[128,128]{1,0:T(8,128)(2,1)S(1)}, bf16[128,128]{1,0:T(8,128)(2,1)S(1)}, u32[]{:S(2)}, u32[]{:S(2)}) collective-permute-start(bf16[128,128]{1,0:T(8,128)(2,1)S(1)} %get-tuple-element.26), channel_id=1, source_target_pairs={{0,2},{2,0},{4,6},{6,4},{1,3},{3,1},{5,7},{7,5},{8,10},{10,8},{12,... | collective-permute-start | bytes 98312 | tf_op jit(solution)/shard_map/ppermute | solution.py:245
  149.7 0.0 collective-permute-done.4.got_p
  149.7 5.6 %collective-permute-done.5.got_q = bf16[128,128]{1,0:T(8,128)(2,1)S(1)} collective-permute-done((bf16[128,128]{1,0:T(8,128)(2,1)S(1)}, bf16[128,128]{1,0:T(8,128)(2,1)S(1)}, u32[]{:S(2)}, u32[]{:S(2)}) %collective-permute-start.5) | collective-permute-done | bytes 32800 | tf_op jit(solution)/shard_map/ppermute | solution.py:245
  155.3 20.9 %all_to_all.33 = bf16[8,32,128]{2,1,0:T(8,128)(2,1)S(1)} all-to-all(bf16[8,32,128]{2,1,0:T(8,128)(2,1)S(1)} %bitcast.26), channel_id=1, replica_groups=mesh['y'=4,'x'=4,'l'=8,'h'=4,'c'=2] {'l'}, dimensions={0} | all-to-all | bytes 131072 | tf_op jit(solution)/shard_map/all_to_all | solution.py:237
  176.2 0.8 shard_map.102
  177.1 7.5 %all-to-all-start.5 = ((bf16[16,16,128]{2,1,0:T(8,128)(2,1)}), bf16[16,16,128]{2,1,0:T(8,128)(2,1)S(1)}, u32[]{:S(2)}, u32[]{:S(2)}) async-start(bf16[16,16,128]{2,1,0:T(8,128)(2,1)} %shard_map.102), calls=%async_computation.5 | async-start | bytes 131072 | tf_op jit(solution)/shard_map/all_to_all | solution.py:237
  184.6 1.9 shard_map.104
  186.5 4.4 %all-to-all-done.5.got = bf16[16,16,128]{2,1,0:T(8,128)(2,1)S(1)} async-done(((bf16[16,16,128]{2,1,0:T(8,128)(2,1)}), bf16[16,16,128]{2,1,0:T(8,128)(2,1)S(1)}, u32[]{:S(2)}, u32[]{:S(2)}) %all-to-all-start.5) | async-done | bytes 65568 | tf_op jit(solution)/shard_map/all_to_all | solution.py:237
  190.9 0.9 shard_map.103
  (7 shorter events, 0.0 us)
Async XLA Ops:
  3.1 53.6 %copy-start = (bf16[1,512,640]{2,1,0:T(8,128)(2,1)S(1)}, bf16[1,512,640]{2,1,0:T(8,128)(2,1)}, u32[]{:S(2)}) copy-start(bf16[1,512,640]{2,1,0:T(8,128)(2,1)} %param.12) | copy-start | bytes 1966084
  3.1 53.6 %copy-start.1 = (bf16[1,640,512]{2,1,0:T(8,128)(2,1)S(1)}, bf16[1,640,512]{2,1,0:T(8,128)(2,1)}, u32[]{:S(2)}) copy-start(bf16[1,640,512]{2,1,0:T(8,128)(2,1)} %param.13) | copy-start | bytes 1966084
  52.9 3.8 %collective-permute-start = (bf16[2,512,256]{2,1,0:T(8,128)(2,1)S(1)}, bf16[2,512,256]{2,1,0:T(8,128)(2,1)S(1)}, u32[]{:S(2)}, u32[]{:S(2)}) collective-permute-start(bf16[2,512,256]{2,1,0:T(8,128)(2,1)S(1)} %shard_map.95.own), channel_id=1, source_target_pairs={{0,1},{1,0},{2,3},{3,2},{4,5},{5,4},{6,7},{7,6},{8,9},{9,8},{10,11... | collective-permute-start | bytes 1572872 | tf_op jit(solution)/shard_map/ppermute | solution.py:241
  92.5 3.4 %collective-permute-start.1 = (bf16[512,256]{1,0:T(8,128)(2,1)S(1)}, bf16[512,256]{1,0:T(8,128)(2,1)S(1)}, u32[]{:S(2)}, u32[]{:S(2)}) collective-permute-start(bf16[512,256]{1,0:T(8,128)(2,1)S(1)} %get-tuple-element.18), channel_id=1, source_target_pairs={{0,1},{1,0},{2,3},{3,2},{4,5},{5,4},{6,7},{7,6},{8,9},{9,8},{10,11... | collective-permute-start | bytes 786440 | tf_op jit(solution)/shard_map/ppermute | solution.py:241
  97.0 37.9 %all-to-all-start.3 = ((bf16[4,128,640]{2,1,0:T(8,128)(2,1)}), bf16[4,128,640]{2,1,0:T(8,128)(2,1)S(1)}, u32[]{:S(2)}, u32[]{:S(2)}) async-start(bf16[4,128,640]{2,1,0:T(8,128)(2,1)} %get-tuple-element.23), calls=%async_computation.3 | async-start | bytes 1310720 | tf_op jit(solution)/shard_map/all_to_all | solution.py:237
  100.5 28.4 %collective-permute-start.2 = (bf16[2,128,128]{2,1,0:T(8,128)(2,1)S(1)}, bf16[2,128,128]{2,1,0:T(8,128)(2,1)S(1)}, u32[]{:S(2)}, u32[]{:S(2)}) collective-permute-start(bf16[2,128,128]{2,1,0:T(8,128)(2,1)S(1)} %get-tuple-element.21), channel_id=1, source_target_pairs={{0,2},{2,0},{4,6},{6,4},{1,3},{3,1},{5,7},{7,5},{8,10},{10,8},{12,... | collective-permute-start | bytes 196616 | tf_op jit(solution)/shard_map/ppermute | solution.py:245
  116.2 18.6 %collective-permute-start.3 = (bf16[2,128,128]{2,1,0:T(8,128)(2,1)S(1)}, bf16[2,128,128]{2,1,0:T(8,128)(2,1)S(1)}, u32[]{:S(2)}, u32[]{:S(2)}) collective-permute-start(bf16[2,128,128]{2,1,0:T(8,128)(2,1)S(1)} %get-tuple-element.22), channel_id=1, source_target_pairs={{0,6},{2,4},{4,2},{6,0},{1,7},{3,5},{5,3},{7,1},{8,14},{10,12},{12... | collective-permute-start | bytes 196616 | tf_op jit(solution)/shard_map/ppermute | solution.py:245
  134.9 14.8 %collective-permute-start.4 = (bf16[128,128]{1,0:T(8,128)(2,1)S(1)}, bf16[128,128]{1,0:T(8,128)(2,1)S(1)}, u32[]{:S(2)}, u32[]{:S(2)}) collective-permute-start(bf16[128,128]{1,0:T(8,128)(2,1)S(1)} %get-tuple-element.25), channel_id=1, source_target_pairs={{0,6},{2,4},{4,2},{6,0},{1,7},{3,5},{5,3},{7,1},{8,14},{10,12},{12... | collective-permute-start | bytes 98312 | tf_op jit(solution)/shard_map/ppermute | solution.py:245
  140.8 14.5 %collective-permute-start.5 = (bf16[128,128]{1,0:T(8,128)(2,1)S(1)}, bf16[128,128]{1,0:T(8,128)(2,1)S(1)}, u32[]{:S(2)}, u32[]{:S(2)}) collective-permute-start(bf16[128,128]{1,0:T(8,128)(2,1)S(1)} %get-tuple-element.26), channel_id=1, source_target_pairs={{0,2},{2,0},{4,6},{6,4},{1,3},{3,1},{5,7},{7,5},{8,10},{10,8},{12,... | collective-permute-start | bytes 98312 | tf_op jit(solution)/shard_map/ppermute | solution.py:245
  176.2 14.7 %copy-start.2 = (s32[128]{0:T(128)S(1)}, s32[128]{0:T(128)}, u32[]{:S(2)}) copy-start(s32[128]{0:T(128)} %param.10) | copy-start | bytes 1540
  176.2 14.7 %copy-start.3 = (s32[128]{0:T(128)S(1)}, s32[128]{0:T(128)}, u32[]{:S(2)}) copy-start(s32[128]{0:T(128)} %param.11) | copy-start | bytes 1540
  177.1 13.9 %all-to-all-start.5 = ((bf16[16,16,128]{2,1,0:T(8,128)(2,1)}), bf16[16,16,128]{2,1,0:T(8,128)(2,1)S(1)}, u32[]{:S(2)}, u32[]{:S(2)}) async-start(bf16[16,16,128]{2,1,0:T(8,128)(2,1)} %shard_map.102), calls=%async_computation.5 | async-start | bytes 131072 | tf_op jit(solution)/shard_map/all_to_all | solution.py:237

commit v3 on v2

v3 whole, which is shorter than its diff:
```python
import jax
import jax.numpy as jnp
from jax import lax
from jax.experimental import pallas as pl
from jax.experimental.pallas import tpu as pltpu
from jax.sharding import Mesh, PartitionSpec as P

tanh_scale = 0.7978845608028654
cubic_coef = 0.044715
f32 = jnp.float32
bf16 = jnp.bfloat16


def gelu_pair(pre_act):
    tanh_arg = tanh_scale * (pre_act + cubic_coef * pre_act * pre_act * pre_act)
    tanh_val = jnp.tanh(tanh_arg)
    gelu_value = 0.5 * pre_act * (1.0 + tanh_val)
    gelu_slope = 0.5 * (1.0 + tanh_val) + 0.5 * pre_act * (
        1.0 - tanh_val * tanh_val
    ) * tanh_scale * (1.0 + 3.0 * cubic_coef * pre_act * pre_act)
    return (gelu_value, gelu_slope)


def dot(a, b, dims):
    return lax.dot_general(a, b, ((dims[0], dims[1]), ((), ())), preferred_element_type=f32)


def size(shape):
    n = 1
    for s in shape:
        n *= s
    return n


def call(kernel, outs, *args, scratch=(), fetch=False, after=(), passed=()):
    moved = sum(a.size * a.dtype.itemsize for a in args) + sum(
        jnp.dtype(d).itemsize * size(s) for s, d in outs
    )
    place = (lax.axis_index("y") * 2 + lax.axis_index("c")).astype(jnp.int32).reshape(1)
    space = pltpu.HBM if fetch else pltpu.VMEM
    return pl.pallas_call(
        kernel,
        out_shape=[jax.ShapeDtypeStruct(s, d) for s, d in outs],
        in_specs=[pl.BlockSpec(memory_space=pltpu.SMEM)]
        + [pl.BlockSpec(memory_space=space)] * len(args)
        + [pl.BlockSpec(memory_space=pl.ANY)] * len(after),
        out_specs=[pl.BlockSpec(memory_space=pltpu.VMEM)] * (len(outs) - len(passed))
        + [pl.BlockSpec(memory_space=pltpu.HBM)] * len(passed),
        scratch_shapes=scratch,
        compiler_params=pltpu.CompilerParams(vmem_limit_bytes=(60 if fetch else 16) * 1024 * 1024),
        cost_estimate=pl.CostEstimate(flops=0, bytes_accessed=moved, transcendentals=0),
    )(place, *args, *after)


def core(place):
    return place[0] & 1


def as_bf16(mask):
    return mask.astype(f32).astype(bf16)


def dispatch_kernel(
    place, eid, slot, gate, tok, cot, w_in, out, w_pass, eid_v, slot_v, gate_v, tok_v, cot_v, sems
):
    quarters, toks, feats = tok_v.shape
    count = out.shape[0] // quarters
    copies = [
        pltpu.make_async_copy(src, dst, sems.at[i])
        for i, (src, dst) in enumerate(((eid, eid_v), (slot, slot_v), (gate, gate_v)))
    ]
    for src, dst in ((tok, tok_v), (cot, cot_v)):
        for q in range(quarters):
            cols = pl.ds(pl.multiple_of((2 * q + core(place)) * feats, feats), feats)
            copies.append(pltpu.make_async_copy(src.at[:, cols], dst.at[q], sems.at[len(copies)]))
    copies.append(pltpu.make_async_copy(w_in, w_pass, sems.at[len(copies)]))
    for copy in copies:
        copy.start()
    for copy in copies[:3]:
        copy.wait()
    row = lax.broadcasted_iota(jnp.int32, (count, toks), 0)
    hit = (row // 8 == eid_v[...]) & (row % 4 == slot_v[...])
    is_x = row % 8 < 4
    take_x = as_bf16(hit & is_x)
    take_dy = as_bf16(hit & ~is_x)
    row_gate = jnp.sum(jnp.where(hit, gate_v[...], 0.0), axis=1, keepdims=True)
    for copy in copies[3:-1]:
        copy.wait()
    for q in range(quarters):
        got_x = dot(take_x, tok_v[q], ((1,), (0,)))
        got_dy = row_gate * dot(take_dy, cot_v[q], ((1,), (0,)))
        out[q * count : (q + 1) * count] = (got_x + got_dy).astype(bf16)
    copies[-1].wait()


def regroup_kernel(place, got, _, __, out):
    rows = out.shape[1] // 4
    count = 2 * rows
    n = lax.broadcasted_iota(jnp.int32, (count, count), 0)
    col = lax.broadcasted_iota(jnp.int32, (count, count), 1)
    which, group, slot = n // rows, (n % rows) // 4, n % 4
    perm = as_bf16(col == group * 8 + which * 4 + slot)
    for y in range(4):
        moved = dot(perm, got[y * count : (y + 1) * count], ((1,), (0,))).astype(bf16)
        out[0, y * rows : (y + 1) * rows] = moved[:rows]
        out[1, y * rows : (y + 1) * rows] = moved[rows:]


def arrange_kernel(place, own, left, right, far_low, far_high, mine, theirs):
    y, c = place[0] >> 1, core(place)
    hs = 4
    f = own.shape[0] // (2 * hs)
    for out, at in ((mine, c), (theirs, 1 - c)):
        for src, q in ((own, y), (left, (y + 3) & 3), (right, (y + 1) & 3), (None, (y + 2) & 3)):
            for h in range(hs):
                ref, h_in = (src, h) if src is not None else ((far_low, far_high)[h // 2], h % 2)
                rows = ref[pl.ds(pl.multiple_of((h_in * 2 + at) * f, f), f), :]
                out[pl.ds(pl.multiple_of((h * 4 + q) * f, f), f), :] = rows


def halves(place, ref, axis):
    n = ref.shape[axis] // 2
    for c in (core(place), 1 - core(place)):
        part = pl.ds(pl.multiple_of(c * n, n), n)
        yield ref[part, :] if axis == 0 else ref[:, part]


def parts_kernel(place, own, other, w_in, w_out, out):
    hid = w_in.shape[1]
    (in_own, in_other), (out_own, out_other) = halves(place, w_in, 0), halves(place, w_out, 1)
    out[:, :hid] = (
        dot(own[0], in_own, ((1,), (0,))) + dot(other[0], in_other, ((1,), (0,)))
    ).astype(bf16)
    out[:, hid:] = (
        dot(own[1], out_own, ((1,), (1,))) + dot(other[1], out_other, ((1,), (1,)))
    ).astype(bf16)


def gelu_kernel(place, got, both):
    hid = both.shape[1] // 2
    total = got[0].astype(f32)
    for q in range(1, got.shape[0]):
        total = total + got[q].astype(f32)
    gelu_value, gelu_slope = gelu_pair(total[:, :hid])
    both[:, :hid] = (total[:, hid:] * gelu_slope).astype(bf16)
    both[:, hid:] = gelu_value.astype(bf16)


def back_kernel(place, both, w_mine, w_theirs, mine, theirs):
    d_hidden = both[:, : both.shape[1] // 2]
    theirs[...] = dot(d_hidden, w_theirs[...], ((1,), (1,))).astype(bf16)
    mine[...] = dot(d_hidden, w_mine[...], ((1,), (1,)))


def pack_kernel(place, mine, got, out):
    n = out.shape[2]
    for h in range(out.shape[0]):
        cols = slice(h * n, (h + 1) * n)
        out[h] = (mine[:, cols] + got[:, cols].astype(f32)).astype(bf16)


def sum_kernel(place, got, out):
    total = got[0].astype(f32)
    for h in range(1, got.shape[0]):
        total = total + got[h].astype(f32)
    total = total.astype(bf16)
    rows, lanes = out.shape
    row = lax.broadcasted_iota(jnp.int32, (rows, total.shape[0]), 0)
    col = lax.broadcasted_iota(jnp.int32, (rows, total.shape[0]), 1)
    source = (row // 8) * 4 + row % 4
    moved = 0.0
    for q_hi in range(2):
        take = as_bf16((source == col) & ((row // 4) % 2 == q_hi))
        moved = moved + dot(take, total[:, q_hi * lanes : (q_hi + 1) * lanes], ((1,), (0,)))
    out[...] = moved.astype(bf16)


def token_kernel(place, eid, slot, got, out):
    quarters, f, toks = out.shape
    row = lax.broadcasted_iota(jnp.int32, (got.shape[0], toks), 0)
    hit = (row // 8 == eid[...]) & (row % 4 == slot[...])
    for q_hi in range(quarters // 2):
        take = as_bf16(hit & ((row // 4) % 2 == q_hi))
        picked = dot(got[...], take, ((0,), (0,))).astype(bf16)
        out[2 * q_hi] = picked[:f]
        out[2 * q_hi + 1] = picked[f:]


def grads_kernel(place, own, other, both, g_in, g_out):
    n, hid = own.shape[2], both.shape[1] // 2
    for src, c in ((own, core(place)), (other, 1 - core(place))):
        part = pl.ds(pl.multiple_of(c * n, n), n)
        g_in[part, :] = dot(src[0], both[:, :hid], ((0,), (0,))).astype(bf16)
        g_out[:, part] = dot(both[:, hid:], src[1], ((0,), (0,))).astype(bf16)


def exchange(x, axes):
    return lax.all_to_all(x, axes, split_axis=0, concat_axis=0, tiled=True)


def other_core(x):
    return lax.ppermute(x, "c", [(0, 1), (1, 0)])


def over_y(x, step):
    return lax.ppermute(x, "y", [(y, (y + step) % 4) for y in range(4)])


def local(tokens, cotangent, gate_value, expert_id, token_slot, w_in, w_out):
    ys, xs, ls, hs = (lax.axis_size(a) for a in ("y", "x", "l", "h"))
    width, hid = w_in.shape[1:]
    toks = tokens.shape[0]
    w_in, w_out = w_in[0], w_out[0]
    eid, slot, gate = (a.reshape(1, toks) for a in (expert_id, token_slot, gate_value))
    groups = ys * xs * ls
    rows, part, f = groups * 4, width // 2, width // 8
    chunk = rows // ys
    sent, w_pass = call(
        dispatch_kernel,
        [((groups * 8, part), bf16), (w_in.shape, bf16)],
        eid,
        slot,
        gate,
        tokens,
        cotangent,
        w_in,
        scratch=[
            pltpu.VMEM((1, toks), jnp.int32),
            pltpu.VMEM((1, toks), jnp.int32),
            pltpu.VMEM((1, toks), f32),
            pltpu.VMEM((ys, toks, part), bf16),
            pltpu.VMEM((ys, toks, part), bf16),
            pltpu.SemaphoreType.DMA((4 + 2 * ys,)),
        ],
        fetch=True,
        passed=(1,),
    )
    got = exchange(sent.reshape(groups, 8, part), ("y", "x", "l")).reshape(groups * 8, part)
    left, right = over_y(w_pass, 1), over_y(w_pass, -1)
    far_low, far_high = over_y(right[:part], -1), over_y(left[part:], 1)
    w_mine, w_theirs = call(
        arrange_kernel, [((ys * part, hid), bf16)] * 2, w_pass, left, right, far_low, far_high
    )
    (own,) = call(regroup_kernel, [((2, rows, part), bf16)], got, after=(w_mine, w_theirs))
    other = other_core(own)
    (parts,) = call(parts_kernel, [((rows, 2 * hid), bf16)], own, other, w_in, w_out)
    got = exchange(parts.reshape(ys, chunk, 2 * hid), "y")
    (both,) = call(gelu_kernel, [((chunk, 2 * hid), bf16)], got)
    mine, theirs = call(
        back_kernel, [((chunk, ys * part), f32), ((chunk, ys * part), bf16)], both, w_mine, w_theirs
    )
    got = other_core(theirs)
    (sent,) = call(pack_kernel, [((hs, chunk, part), bf16)], mine, got)
    got = exchange(sent, "h")
    (sent,) = call(sum_kernel, [((xs * ls * 8, 2 * f), bf16)], got)
    got = exchange(sent.reshape(xs * ls, 8, 2 * f), ("x", "l")).reshape(xs * ls * 8, 2 * f)
    both = lax.all_gather(both, "y", axis=0, tiled=True)
    g_in, g_out = call(grads_kernel, [((width, hid), bf16), ((hid, width), bf16)], own, other, both)
    (grad_t,) = call(token_kernel, [((ys, f, toks), bf16)], eid, slot, got)
    return jnp.transpose(grad_t, (2, 0, 1)), g_in[None], g_out[None]


def solution(mesh):
    dp, expert, mp = mesh.devices.shape
    fine = Mesh(mesh.devices.reshape(dp, 4, expert // 4, mp // 2, 2), ("y", "x", "l", "h", "c"))
    group, ffn = ("y", "x", "l"), ("h", "c")
    in_specs = (
        P(group, None),
        P(group, None),
        P(group),
        P(group),
        P(group),
        P(("x", "l"), "y", ffn),
        P(("x", "l"), ffn, "y"),
    )
    out_specs = (P(group, None, ffn), P(("x", "l"), "y", ffn), P(("x", "l"), ffn, "y"))
    return jax.shard_map(local, mesh=fine, in_specs=in_specs, out_specs=out_specs, check_vma=False)
```

time: 192 us -> 216 us (1.12)
  the two profiles are of different devices: /device:TPU:2 before, /device:TPU:1 now
where the time goes in v3:
time: 216 us; the launch traced here: 215 us
  starting transfers between devices  87.7 us (41%)
  waiting for transfers between devices  59.2 us (27%)
  Pallas kernels  30.9 us (14%)
  blocking collectives  20.1 us (9%)
  between operations  14.2 us (7%)
  local copies, waits for them, and re-layouts  3.23 us (1%)
    all_to_all x3, starting transfers between devices, exchange(): return lax.all_to_all(x, axes, split_axis=0, concat_axis=0, tiled=True)  66.8 us
    all_to_all x3, waiting for transfers between devices, exchange(): return lax.all_to_all(x, axes, split_axis=0, concat_axis=0, tiled=True)  31.9 us
    pallas_call x10, Pallas kernels, call(): pl.pallas_call(kernel, out_shape=[jax.ShapeDtypeStruct(s, d) for s, d in...  30.9 us
    ppermute x4, waiting for transfers between devices, over_y(): return lax.ppermute(x, 'y', [(y, (y + step) % 4) for y in range(4)])  24 us
    all_to_all x1, blocking collectives, exchange(): return lax.all_to_all(x, axes, split_axis=0, concat_axis=0, tiled=True)  20.1 us
    ppermute x4, starting transfers between devices, over_y(): return lax.ppermute(x, 'y', [(y, (y + step) % 4) for y in range(4)])  12.9 us
    ppermute x2, starting transfers between devices, other_core(): return lax.ppermute(x, 'c', [(0, 1), (1, 0)])  8.03 us
  transfers between devices with their start and end apart: 10, of which 7 were waited for; matrix products, arithmetic and copies ran while one was open for 0% of the time, Pallas kernels for 1%

profile of v3, /device:TPU:1, one launch (start us, length us, event | category | flops | bytes accessed | tf_op | source)
XLA Modules:
  0.0 215.4 jit_solution(16180676790328728166)
XLA Ops:
  7.2 21.9 %shard_map.94 = (bf16[1024,256]{1,0:T(8,128)(2,1)}, bf16[512,640]{1,0:T(8,128)(2,1)}) custom-call(s32[1]{0:T(128)} %bitcast.place, s32[1,128]{1,0:T(1,128)} %bitcast.20, s32[1,128]{1,0:T(1,128)} %bitcast.22, f32[1,128]{1,0:T(1,128)} %bitcast.26, bf16[128,2048]{1,0:T(8,128)(2,1)} %tok.1, bf16[128,2048]{1,0:T(8,128)(2,1)} %cot.1, bf16[512,640]{1,0:T(8,128)(2,1)} %bitcast.15), custom_call_target="tpu_custom_call" | custom-call | bytes 2885120 | tf_op jit(solution)/shard_map/pallas_call | solution.py:41
  29.1 20.4 %all-to-all-start = ((bf16[128,8,256]{2,1,0:T(8,128)(2,1)}), bf16[128,8,256]{2,1,0:T(8,128)(2,1)S(1)}, u32[]{:S(2)}, u32[]{:S(2)}) async-start(bf16[128,8,256]{2,1,0:T(8,128)(2,1)} %bitcast.24), calls=%async_computation | async-start | bytes 1048576 | tf_op jit(solution)/shard_map/all_to_all | solution.py:198
  49.5 4.4 %collective-permute-start.1 = (bf16[512,640]{1,0:T(8,128)(2,1)}, bf16[512,640]{1,0:T(8,128)(2,1)S(1)}, u32[]{:S(2)}, u32[]{:S(2)}) collective-permute-start(bf16[512,640]{1,0:T(8,128)(2,1)} %get-tuple-element.12.own), channel_id=1, source_target_pairs={{0,768},{256,0},{512,256},{768,512},{1,769},{257,1},{513,257},{769... | collective-permute-start | bytes 1966088 | tf_op jit(solution)/shard_map/ppermute | solution.py:206
  53.8 1.9 collective-permute-start
  55.8 15.4 %collective-permute-done.1.right = bf16[512,640]{1,0:T(8,128)(2,1)S(1)} collective-permute-done((bf16[512,640]{1,0:T(8,128)(2,1)}, bf16[512,640]{1,0:T(8,128)(2,1)S(1)}, u32[]{:S(2)}, u32[]{:S(2)}) %collective-permute-start.1) | collective-permute-done | bytes 655392 | tf_op jit(solution)/shard_map/ppermute | solution.py:206
  71.2 4.7 %collective-permute-start.2 = (bf16[256,640]{1,0:T(8,128)(2,1)S(1)}, bf16[256,640]{1,0:T(8,128)(2,1)S(1)}, u32[]{:S(2)}, u32[]{:S(2)}) collective-permute-start(bf16[256,640]{1,0:T(8,128)(2,1)S(1)} %slice.8), channel_id=1, source_target_pairs={{0,768},{256,0},{512,256},{768,512},{1,769},{257,1},{513,257},{769... | collective-permute-start | bytes 983048 | tf_op jit(solution)/shard_map/ppermute | solution.py:206
  75.9 1.9 collective-permute-start.3
  77.8 3.8 %collective-permute-done.2.far_low = bf16[256,640]{1,0:T(8,128)(2,1)S(1)} collective-permute-done((bf16[256,640]{1,0:T(8,128)(2,1)S(1)}, bf16[256,640]{1,0:T(8,128)(2,1)S(1)}, u32[]{:S(2)}, u32[]{:S(2)}) %collective-permute-start.2) | collective-permute-done | bytes 327712 | tf_op jit(solution)/shard_map/ppermute | solution.py:206
  81.6 4.8 %collective-permute-done.3.far_high = bf16[256,640]{1,0:T(8,128)(2,1)S(1)} collective-permute-done((bf16[256,640]{1,0:T(8,128)(2,1)S(1)}, bf16[256,640]{1,0:T(8,128)(2,1)S(1)}, u32[]{:S(2)}, u32[]{:S(2)}) %collective-permute-start.3) | collective-permute-done | bytes 327712 | tf_op jit(solution)/shard_map/ppermute | solution.py:206
  86.4 0.4 shard_map.95
  86.9 0.8 copy-done.3
  87.6 1.0 copy-done.4
  88.7 0.3 shard_map.96.own
  89.0 4.8 %collective-permute-start.4 = (bf16[2,512,256]{2,1,0:T(8,128)(2,1)S(1)}, bf16[2,512,256]{2,1,0:T(8,128)(2,1)S(1)}, u32[]{:S(2)}, u32[]{:S(2)}) collective-permute-start(bf16[2,512,256]{2,1,0:T(8,128)(2,1)S(1)} %shard_map.96.own), channel_id=1, source_target_pairs={{0,1},{1,0},{2,3},{3,2},{4,5},{5,4},{6,7},{7,6},{8,9},{9,8},{10,11... | collective-permute-start | bytes 1572872 | tf_op jit(solution)/shard_map/ppermute | solution.py:202
  93.8 1.5 collective-permute-done.4.other
  95.3 1.0 shard_map.97
  96.3 20.1 %all_to_all.20.got = bf16[4,128,1280]{2,1,0:T(8,128)(2,1)S(1)} all-to-all(bf16[4,128,1280]{2,1,0:T(8,128)(2,1)S(1)} %bitcast.14), channel_id=1, replica_groups=mesh['y'=4,'x'=4,'l'=8,'h'=4,'c'=2] {'y'}, dimensions={0} | all-to-all | bytes 2621440 | tf_op jit(solution)/shard_map/all_to_all | solution.py:198
  116.4 1.1 shard_map.98.both
  117.5 1.9 shard_map.99
  119.5 3.2 %collective-permute-start.5 = (bf16[128,1024]{1,0:T(8,128)(2,1)S(1)}, bf16[128,1024]{1,0:T(8,128)(2,1)S(1)}, u32[]{:S(2)}, u32[]{:S(2)}) collective-permute-start(bf16[128,1024]{1,0:T(8,128)(2,1)S(1)} %get-tuple-element.16), channel_id=1, source_target_pairs={{0,1},{1,0},{2,3},{3,2},{4,5},{5,4},{6,7},{7,6},{8,9},{9,8},{10,11... | collective-permute-start | bytes 786440 | tf_op jit(solution)/shard_map/ppermute | solution.py:202
  122.7 1.1 collective-permute-done.5.got
  123.8 0.8 shard_map.100
  124.6 20.6 %all-to-all-start.2 = ((bf16[4,128,256]{2,1,0:T(8,128)(2,1)}), bf16[4,128,256]{2,1,0:T(8,128)(2,1)S(1)}, u32[]{:S(2)}, u32[]{:S(2)}) async-start(bf16[4,128,256]{2,1,0:T(8,128)(2,1)} %shard_map.100), calls=%async_computation.2 | async-start | bytes 524288 | tf_op jit(solution)/shard_map/all_to_all | solution.py:198
  145.2 0.7 all-gather.2.cloned.1.call-update
  145.9 23.6 %all-to-all-done.2.got = bf16[4,128,256]{2,1,0:T(8,128)(2,1)S(1)} async-done(((bf16[4,128,256]{2,1,0:T(8,128)(2,1)}), bf16[4,128,256]{2,1,0:T(8,128)(2,1)S(1)}, u32[]{:S(2)}, u32[]{:S(2)}) %all-to-all-start.2) | async-done | bytes 262176 | tf_op jit(solution)/shard_map/all_to_all | solution.py:198
  169.5 0.9 shard_map.101
  170.4 25.8 %all-to-all-start.3 = ((bf16[32,8,128]{2,1,0:T(8,128)(2,1)}), bf16[32,8,128]{2,1,0:T(8,128)(2,1)S(1)}, u32[]{:S(2)}, u32[]{:S(2)}) async-start(bf16[32,8,128]{2,1,0:T(8,128)(2,1)} %bitcast.9), calls=%async_computation.3 | async-start | bytes 131072 | tf_op jit(solution)/shard_map/all_to_all | solution.py:198
  196.2 0.0 all-gather.2.cloned.1.call-done.both
  196.3 1.3 copy-done.5
  197.6 1.9 shard_map.103
  199.4 8.3 %all-to-all-done.3 = bf16[32,8,128]{2,1,0:T(8,128)(2,1)S(1)} async-done(((bf16[32,8,128]{2,1,0:T(8,128)(2,1)}), bf16[32,8,128]{2,1,0:T(8,128)(2,1)S(1)}, u32[]{:S(2)}, u32[]{:S(2)}) %all-to-all-start.3) | async-done | bytes 65568 | tf_op jit(solution)/shard_map/all_to_all | solution.py:198
  207.7 0.9 shard_map.102
  (22 shorter events, 0.1 us)
Async XLA Ops:
  29.1 57.8 %all-to-all-start = ((bf16[128,8,256]{2,1,0:T(8,128)(2,1)}), bf16[128,8,256]{2,1,0:T(8,128)(2,1)S(1)}, u32[]{:S(2)}, u32[]{:S(2)}) async-start(bf16[128,8,256]{2,1,0:T(8,128)(2,1)} %bitcast.24), calls=%async_computation | async-start | bytes 1048576 | tf_op jit(solution)/shard_map/all_to_all | solution.py:198
  49.5 37.0 %copy-start.6 = (bf16[512,640]{1,0:T(8,128)(2,1)S(1)}, bf16[512,640]{1,0:T(8,128)(2,1)}, u32[]{:S(2)}) copy-start(bf16[512,640]{1,0:T(8,128)(2,1)} %get-tuple-element.12.own) | copy-start | bytes 1966084
  49.5 21.7 %collective-permute-start.1 = (bf16[512,640]{1,0:T(8,128)(2,1)}, bf16[512,640]{1,0:T(8,128)(2,1)S(1)}, u32[]{:S(2)}, u32[]{:S(2)}) collective-permute-start(bf16[512,640]{1,0:T(8,128)(2,1)} %get-tuple-element.12.own), channel_id=1, source_target_pairs={{0,768},{256,0},{512,256},{768,512},{1,769},{257,1},{513,257},{769... | collective-permute-start | bytes 1966088 | tf_op jit(solution)/shard_map/ppermute | solution.py:206
  53.8 22.0 %collective-permute-start = (bf16[512,640]{1,0:T(8,128)(2,1)}, bf16[512,640]{1,0:T(8,128)(2,1)S(1)}, u32[]{:S(2)}, u32[]{:S(2)}) collective-permute-start(bf16[512,640]{1,0:T(8,128)(2,1)} %get-tuple-element.12.own), channel_id=1, source_target_pairs={{0,256},{256,512},{512,768},{768,0},{1,257},{257,513},{513,769},{7... | collective-permute-start | bytes 1966088 | tf_op jit(solution)/shard_map/ppermute | solution.py:206
  71.2 10.5 %collective-permute-start.2 = (bf16[256,640]{1,0:T(8,128)(2,1)S(1)}, bf16[256,640]{1,0:T(8,128)(2,1)S(1)}, u32[]{:S(2)}, u32[]{:S(2)}) collective-permute-start(bf16[256,640]{1,0:T(8,128)(2,1)S(1)} %slice.8), channel_id=1, source_target_pairs={{0,768},{256,0},{512,256},{768,512},{1,769},{257,1},{513,257},{769... | collective-permute-start | bytes 983048 | tf_op jit(solution)/shard_map/ppermute | solution.py:206
  75.9 10.5 %collective-permute-start.3 = (bf16[256,640]{1,0:T(8,128)(2,1)S(1)}, bf16[256,640]{1,0:T(8,128)(2,1)S(1)}, u32[]{:S(2)}, u32[]{:S(2)}) collective-permute-start(bf16[256,640]{1,0:T(8,128)(2,1)S(1)} %slice.9), channel_id=1, source_target_pairs={{0,256},{256,512},{512,768},{768,0},{1,257},{257,513},{513,769},{7... | collective-permute-start | bytes 983048 | tf_op jit(solution)/shard_map/ppermute | solution.py:206
  86.8 0.8 copy-start.3
  87.6 1.0 copy-start.4
  88.7 6.6 %copy-start = (bf16[1,512,640]{2,1,0:T(8,128)(2,1)S(1)}, bf16[1,512,640]{2,1,0:T(8,128)(2,1)}, u32[]{:S(2)}) copy-start(bf16[1,512,640]{2,1,0:T(8,128)(2,1)} %param.12) | copy-start | bytes 1966084
  88.7 6.6 %copy-start.7 = (bf16[1,640,512]{2,1,0:T(8,128)(2,1)S(1)}, bf16[1,640,512]{2,1,0:T(8,128)(2,1)}, u32[]{:S(2)}) copy-start(bf16[1,640,512]{2,1,0:T(8,128)(2,1)} %param.13) | copy-start | bytes 1966084
  89.0 6.3 %collective-permute-start.4 = (bf16[2,512,256]{2,1,0:T(8,128)(2,1)S(1)}, bf16[2,512,256]{2,1,0:T(8,128)(2,1)S(1)}, u32[]{:S(2)}, u32[]{:S(2)}) collective-permute-start(bf16[2,512,256]{2,1,0:T(8,128)(2,1)S(1)} %shard_map.96.own), channel_id=1, source_target_pairs={{0,1},{1,0},{2,3},{3,2},{4,5},{5,4},{6,7},{7,6},{8,9},{9,8},{10,11... | collective-permute-start | bytes 1572872 | tf_op jit(solution)/shard_map/ppermute | solution.py:202
  95.3 1.0 copy-start.1
  119.4 76.8 %copy-start.2 = (bf16[2,512,256]{2,1,0:T(8,128)(2,1)S(1)}, bf16[2,512,256]{2,1,0:T(8,128)(2,1)}, u32[]{:S(2)}) copy-start(bf16[2,512,256]{2,1,0:T(8,128)(2,1)} %copy-done.1) | copy-start | bytes 1572868
  119.5 4.4 %collective-permute-start.5 = (bf16[128,1024]{1,0:T(8,128)(2,1)S(1)}, bf16[128,1024]{1,0:T(8,128)(2,1)S(1)}, u32[]{:S(2)}, u32[]{:S(2)}) collective-permute-start(bf16[128,1024]{1,0:T(8,128)(2,1)S(1)} %get-tuple-element.16), channel_id=1, source_target_pairs={{0,1},{1,0},{2,3},{3,2},{4,5},{5,4},{6,7},{7,6},{8,9},{9,8},{10,11... | collective-permute-start | bytes 786440 | tf_op jit(solution)/shard_map/ppermute | solution.py:202
  124.6 44.9 %all-to-all-start.2 = ((bf16[4,128,256]{2,1,0:T(8,128)(2,1)}), bf16[4,128,256]{2,1,0:T(8,128)(2,1)S(1)}, u32[]{:S(2)}, u32[]{:S(2)}) async-start(bf16[4,128,256]{2,1,0:T(8,128)(2,1)} %shard_map.100), calls=%async_computation.2 | async-start | bytes 524288 | tf_op jit(solution)/shard_map/all_to_all | solution.py:198
  145.2 51.0 %all-gather.2.cloned.1.call-start = ((), (), s32[]{:S(2)}) async-start(), calls=%async_computation.4 | async-start | bytes 1638400 | tf_op jit(solution)/shard_map/all_gather | solution.py:257
  170.4 37.3 %copy-start.8 = (s32[128]{0:T(128)S(1)}, s32[128]{0:T(128)}, u32[]{:S(2)}) copy-start(s32[128]{0:T(128)} %param.10) | copy-start | bytes 1540
  170.4 37.3 %copy-start.9 = (s32[128]{0:T(128)S(1)}, s32[128]{0:T(128)}, u32[]{:S(2)}) copy-start(s32[128]{0:T(128)} %param.11) | copy-start | bytes 1540
  170.4 37.3 %all-to-all-start.3 = ((bf16[32,8,128]{2,1,0:T(8,128)(2,1)}), bf16[32,8,128]{2,1,0:T(8,128)(2,1)S(1)}, u32[]{:S(2)}, u32[]{:S(2)}) async-start(bf16[32,8,128]{2,1,0:T(8,128)(2,1)} %bitcast.9), calls=%async_computation.3 | async-start | bytes 131072 | tf_op jit(solution)/shard_map/all_to_all | solution.py:198
  196.2 1.3 copy-start.5
Sparse Core Ops, SparseCore 0:
  149.3 41.1 all-gather.1

commit v4 on v3

--- a/solution.py
+++ b/solution.py
@@ -32,7 +32,7 @@
     return n
 
 
-def call(kernel, outs, *args, scratch=(), fetch=False, after=(), passed=()):
+def call(kernel, outs, *args, scratch=(), fetch=False, after=()):
     moved = sum(a.size * a.dtype.itemsize for a in args) + sum(
         jnp.dtype(d).itemsize * size(s) for s, d in outs
     )
@@ -44,8 +44,7 @@
         in_specs=[pl.BlockSpec(memory_space=pltpu.SMEM)]
         + [pl.BlockSpec(memory_space=space)] * len(args)
         + [pl.BlockSpec(memory_space=pl.ANY)] * len(after),
-        out_specs=[pl.BlockSpec(memory_space=pltpu.VMEM)] * (len(outs) - len(passed))
-        + [pl.BlockSpec(memory_space=pltpu.HBM)] * len(passed),
+        out_specs=[pl.BlockSpec(memory_space=pltpu.VMEM)] * len(outs),
         scratch_shapes=scratch,
         compiler_params=pltpu.CompilerParams(vmem_limit_bytes=(60 if fetch else 16) * 1024 * 1024),
         cost_estimate=pl.CostEstimate(flops=0, bytes_accessed=moved, transcendentals=0),
@@ -93,20 +92,21 @@
     copies[-1].wait()
 
 
-def regroup_kernel(place, got, _, __, out):
-    rows = out.shape[1] // 4
+def regroup_kernel(place, got, _, out):
+    rows, xs = out.shape[1] // 4, 4
     count = 2 * rows
     n = lax.broadcasted_iota(jnp.int32, (count, count), 0)
     col = lax.broadcasted_iota(jnp.int32, (count, count), 1)
-    which, group, slot = n // rows, (n % rows) // 4, n % 4
-    perm = as_bf16(col == group * 8 + which * 4 + slot)
+    which, at_l, x, slot = n // rows, (n % rows) // (4 * xs), (n // 4) % xs, n % 4
+    perm = as_bf16(col == ((x * (rows // (4 * xs)) + at_l) * 2 + which) * 4 + slot)
     for y in range(4):
         moved = dot(perm, got[y * count : (y + 1) * count], ((1,), (0,))).astype(bf16)
         out[0, y * rows : (y + 1) * rows] = moved[:rows]
         out[1, y * rows : (y + 1) * rows] = moved[rows:]
 
 
-def arrange_kernel(place, own, left, right, far_low, far_high, mine, theirs):
+def arrange_kernel(place, own, left, right, far_low, far_high, mine, theirs, done):
+    done[...] = jnp.zeros_like(done)
     y, c = place[0] >> 1, core(place)
     hs = 4
     f = own.shape[0] // (2 * hs)
@@ -136,62 +136,57 @@
     ).astype(bf16)
 
 
-def gelu_kernel(place, got, both):
-    hid = both.shape[1] // 2
+def gelu_kernel(place, got, dh, act):
+    hid = dh.shape[1]
     total = got[0].astype(f32)
     for q in range(1, got.shape[0]):
         total = total + got[q].astype(f32)
     gelu_value, gelu_slope = gelu_pair(total[:, :hid])
-    both[:, :hid] = (total[:, hid:] * gelu_slope).astype(bf16)
-    both[:, hid:] = gelu_value.astype(bf16)
-
-
-def back_kernel(place, both, w_mine, w_theirs, mine, theirs):
-    d_hidden = both[:, : both.shape[1] // 2]
-    theirs[...] = dot(d_hidden, w_theirs[...], ((1,), (1,))).astype(bf16)
-    mine[...] = dot(d_hidden, w_mine[...], ((1,), (1,)))
+    dh[...] = (total[:, hid:] * gelu_slope).astype(bf16)
+    act[...] = gelu_value.astype(bf16)
+
+
+def back_kernel(place, dh, w_mine, w_theirs, mine, theirs):
+    theirs[...] = dot(dh[...], w_theirs[...], ((1,), (1,))).astype(bf16)
+    mine[...] = dot(dh[...], w_mine[...], ((1,), (1,)))
 
 
 def pack_kernel(place, mine, got, out):
-    n = out.shape[2]
-    for h in range(out.shape[0]):
+    ls, hs, rows, n = out.shape
+    for h in range(hs):
         cols = slice(h * n, (h + 1) * n)
-        out[h] = (mine[:, cols] + got[:, cols].astype(f32)).astype(bf16)
-
-
-def sum_kernel(place, got, out):
-    total = got[0].astype(f32)
-    for h in range(1, got.shape[0]):
-        total = total + got[h].astype(f32)
-    total = total.astype(bf16)
-    rows, lanes = out.shape
-    row = lax.broadcasted_iota(jnp.int32, (rows, total.shape[0]), 0)
-    col = lax.broadcasted_iota(jnp.int32, (rows, total.shape[0]), 1)
-    source = (row // 8) * 4 + row % 4
-    moved = 0.0
-    for q_hi in range(2):
-        take = as_bf16((source == col) & ((row // 4) % 2 == q_hi))
-        moved = moved + dot(take, total[:, q_hi * lanes : (q_hi + 1) * lanes], ((1,), (0,)))
-    out[...] = moved.astype(bf16)
+        both = (mine[:, cols] + got[:, cols].astype(f32)).astype(bf16)
+        out[:, h] = both.reshape(ls, rows, n)
+
+
+def sum_kernel(place, got, _, out):
+    ls, hs, inner, n = got.shape
+    total = got[:, 0].astype(f32)
+    for h in range(1, hs):
+        total = total + got[:, h].astype(f32)
+    rows = ls * inner
+    row = lax.broadcasted_iota(jnp.int32, (rows, rows), 0)
+    col = lax.broadcasted_iota(jnp.int32, (rows, rows), 1)
+    perm = as_bf16(col == (row // 4) % ls * inner + row // (4 * ls) * 4 + row % 4)
+    out[...] = dot(perm, total.astype(bf16).reshape(rows, n), ((1,), (0,))).astype(bf16)
 
 
 def token_kernel(place, eid, slot, got, out):
     quarters, f, toks = out.shape
     row = lax.broadcasted_iota(jnp.int32, (got.shape[0], toks), 0)
-    hit = (row // 8 == eid[...]) & (row % 4 == slot[...])
-    for q_hi in range(quarters // 2):
-        take = as_bf16(hit & ((row // 4) % 2 == q_hi))
-        picked = dot(got[...], take, ((0,), (0,))).astype(bf16)
-        out[2 * q_hi] = picked[:f]
-        out[2 * q_hi + 1] = picked[f:]
-
-
-def grads_kernel(place, own, other, both, g_in, g_out):
-    n, hid = own.shape[2], both.shape[1] // 2
+    take = as_bf16((row // 4 == eid[...]) & (row % 4 == slot[...]))
+    picked = dot(got[...], take, ((0,), (0,))).astype(bf16)
+    for q in range(quarters):
+        out[q] = picked[q * f : (q + 1) * f]
+
+
+def grads_kernel(place, own, other, dh, act, g_in, g_out, done):
+    done[...] = jnp.zeros_like(done)
+    n = own.shape[2]
     for src, c in ((own, core(place)), (other, 1 - core(place))):
         part = pl.ds(pl.multiple_of(c * n, n), n)
-        g_in[part, :] = dot(src[0], both[:, :hid], ((0,), (0,))).astype(bf16)
-        g_out[:, part] = dot(both[:, hid:], src[1], ((0,), (0,))).astype(bf16)
+        g_in[part, :] = dot(src[0], dh[...], ((0,), (0,))).astype(bf16)
+        g_out[:, part] = dot(act[...], src[1], ((0,), (0,))).astype(bf16)
 
 
 def exchange(x, axes):
@@ -233,29 +228,33 @@
             pltpu.SemaphoreType.DMA((4 + 2 * ys,)),
         ],
         fetch=True,
-        passed=(1,),
     )
     got = exchange(sent.reshape(groups, 8, part), ("y", "x", "l")).reshape(groups * 8, part)
     left, right = over_y(w_pass, 1), over_y(w_pass, -1)
     far_low, far_high = over_y(right[:part], -1), over_y(left[part:], 1)
-    w_mine, w_theirs = call(
-        arrange_kernel, [((ys * part, hid), bf16)] * 2, w_pass, left, right, far_low, far_high
-    )
-    (own,) = call(regroup_kernel, [((2, rows, part), bf16)], got, after=(w_mine, w_theirs))
+    token = ((8, 128), f32)
+    w_mine, w_theirs, done = call(
+        arrange_kernel, [((ys * part, hid), bf16)] * 2 + [token], w_pass, left, right, far_low, far_high
+    )
+    (own,) = call(regroup_kernel, [((2, rows, part), bf16)], got, after=(done,))
     other = other_core(own)
     (parts,) = call(parts_kernel, [((rows, 2 * hid), bf16)], own, other, w_in, w_out)
     got = exchange(parts.reshape(ys, chunk, 2 * hid), "y")
-    (both,) = call(gelu_kernel, [((chunk, 2 * hid), bf16)], got)
+    dh, act = call(gelu_kernel, [((chunk, hid), bf16)] * 2, got)
     mine, theirs = call(
-        back_kernel, [((chunk, ys * part), f32), ((chunk, ys * part), bf16)], both, w_mine, w_theirs
+        back_kernel, [((chunk, ys * part), f32), ((chunk, ys * part), bf16)], dh, w_mine, w_theirs
     )
     got = other_core(theirs)
-    (sent,) = call(pack_kernel, [((hs, chunk, part), bf16)], mine, got)
-    got = exchange(sent, "h")
-    (sent,) = call(sum_kernel, [((xs * ls * 8, 2 * f), bf16)], got)
-    got = exchange(sent.reshape(xs * ls, 8, 2 * f), ("x", "l")).reshape(xs * ls * 8, 2 * f)
-    both = lax.all_gather(both, "y", axis=0, tiled=True)
-    g_in, g_out = call(grads_kernel, [((width, hid), bf16), ((hid, width), bf16)], own, other, both)
+    (sent,) = call(pack_kernel, [((ls, hs, xs * 4, part), bf16)], mine, got)
+    got = exchange(sent.reshape(ls * hs, xs * 4, part), ("l", "h"))
+    dh, act = (lax.all_gather(a, "y", axis=0, tiled=True) for a in (dh, act))
+    g_in, g_out, done = call(
+        grads_kernel, [((width, hid), bf16), ((hid, width), bf16), token], own, other, dh, act
+    )
+    (sent,) = call(
+        sum_kernel, [((chunk, part), bf16)], got.reshape(ls, hs, xs * 4, part), after=(done,)
+    )
+    got = exchange(sent.reshape(xs, ls * 4, part), "x").reshape(chunk, part)
     (grad_t,) = call(token_kernel, [((ys, f, toks), bf16)], eid, slot, got)
     return jnp.transpose(grad_t, (2, 0, 1)), g_in[None], g_out[None]
 

time: 216 us -> 166 us (0.77)
  the two profiles are of different devices: /device:TPU:1 before, /device:TPU:32 now
where the time goes in v4:
time: 166 us
  starting transfers between devices  60.5 us (36%)
  blocking collectives  57.3 us (35%)
  waiting for transfers between devices  34.5 us (21%)
  Pallas kernels  9.27 us (6%)
  local copies, waits for them, and re-layouts  3.15 us (2%)
    all_to_all x2, starting transfers between devices, exchange(): return lax.all_to_all(x, axes, split_axis=0, concat_axis=0, tiled=True)  41.9 us
    all_to_all x2, blocking collectives, exchange(): return lax.all_to_all(x, axes, split_axis=0, concat_axis=0, tiled=True)  30.6 us
    all_gather x2, blocking collectives, local(): dh, act = (lax.all_gather(a, 'y', axis=0, tiled=True) for a in (dh, act))  26.7 us
    ppermute x4, waiting for transfers between devices, over_y(): return lax.ppermute(x, 'y', [(y, (y + step) % 4) for y in range(4)])  24.5 us
    ppermute x4, starting transfers between devices, over_y(): return lax.ppermute(x, 'y', [(y, (y + step) % 4) for y in range(4)])  14.7 us
    pallas_call x10, Pallas kernels, call(): pl.pallas_call(kernel, out_shape=[jax.ShapeDtypeStruct(s, d) for s, d in...  9.27 us
    all_to_all x2, waiting for transfers between devices, exchange(): return lax.all_to_all(x, axes, split_axis=0, concat_axis=0, tiled=True)  6.63 us
    ppermute x2, starting transfers between devices, other_core(): return lax.ppermute(x, 'c', [(0, 1), (1, 0)])  3.84 us
  transfers between devices with their start and end apart: 8, of which 6 were waited for; matrix products, arithmetic and copies ran while one was open for 0% of the time, Pallas kernels for 1%

profile of v4, /device:TPU:32, one launch (start us, length us, event | category | flops | bytes accessed | tf_op | source)
XLA Modules:
  0.0 165.6 jit_solution(15822753337295980246)
XLA Ops:
  0.6 2.7 %shard_map.94 = (bf16[1024,256]{1,0:T(8,128)(2,1)}, bf16[512,640]{1,0:T(8,128)(2,1)}) custom-call(s32[1]{0:T(128)} %bitcast.place, s32[1,128]{1,0:T(1,128)} %bitcast.24, s32[1,128]{1,0:T(1,128)} %bitcast.26, f32[1,128]{1,0:T(1,128)} %bitcast.30, bf16[128,2048]{1,0:T(8,128)(2,1)} %tok.1, bf16[128,2048]{1,0:T(8,128)(2,1)} %cot.1, bf16[512,640]{1,0:T(8,128)(2,1)} %bitcast.17), custom_call_target="tpu_custom_call" | custom-call | bytes 2885120 | tf_op jit(solution)/shard_map/pallas_call | solution.py:41
  3.3 19.1 %all-to-all-start = ((bf16[128,8,256]{2,1,0:T(8,128)(2,1)}), bf16[128,8,256]{2,1,0:T(8,128)(2,1)S(1)}, u32[]{:S(2)}, u32[]{:S(2)}) async-start(bf16[128,8,256]{2,1,0:T(8,128)(2,1)} %bitcast.28), calls=%async_computation | async-start | bytes 1048576 | tf_op jit(solution)/shard_map/all_to_all | solution.py:193
  22.4 0.0 copy-start.3
  22.4 5.3 %collective-permute-start.1 = (bf16[512,640]{1,0:T(8,128)(2,1)}, bf16[512,640]{1,0:T(8,128)(2,1)S(1)}, u32[]{:S(2)}, u32[]{:S(2)}) collective-permute-start(bf16[512,640]{1,0:T(8,128)(2,1)} %get-tuple-element.16.own), channel_id=1, source_target_pairs={{0,768},{256,0},{512,256},{768,512},{1,769},{257,1},{513,257},{769... | collective-permute-start | bytes 1966088 | tf_op jit(solution)/shard_map/ppermute | solution.py:201
  27.7 1.9 %collective-permute-start = (bf16[512,640]{1,0:T(8,128)(2,1)}, bf16[512,640]{1,0:T(8,128)(2,1)S(1)}, u32[]{:S(2)}, u32[]{:S(2)}) collective-permute-start(bf16[512,640]{1,0:T(8,128)(2,1)} %get-tuple-element.16.own), channel_id=1, source_target_pairs={{0,256},{256,512},{512,768},{768,0},{1,257},{257,513},{513,769},{7... | collective-permute-start | bytes 1966088 | tf_op jit(solution)/shard_map/ppermute | solution.py:201
  29.6 15.1 %collective-permute-done.1.right = bf16[512,640]{1,0:T(8,128)(2,1)S(1)} collective-permute-done((bf16[512,640]{1,0:T(8,128)(2,1)}, bf16[512,640]{1,0:T(8,128)(2,1)S(1)}, u32[]{:S(2)}, u32[]{:S(2)}) %collective-permute-start.1) | collective-permute-done | bytes 655392 | tf_op jit(solution)/shard_map/ppermute | solution.py:201
  44.7 5.5 %collective-permute-start.2 = (bf16[256,640]{1,0:T(8,128)(2,1)S(1)}, bf16[256,640]{1,0:T(8,128)(2,1)S(1)}, u32[]{:S(2)}, u32[]{:S(2)}) collective-permute-start(bf16[256,640]{1,0:T(8,128)(2,1)S(1)} %slice.8), channel_id=1, source_target_pairs={{0,768},{256,0},{512,256},{768,512},{1,769},{257,1},{513,257},{769... | collective-permute-start | bytes 983048 | tf_op jit(solution)/shard_map/ppermute | solution.py:201
  50.3 2.1 %collective-permute-start.3 = (bf16[256,640]{1,0:T(8,128)(2,1)S(1)}, bf16[256,640]{1,0:T(8,128)(2,1)S(1)}, u32[]{:S(2)}, u32[]{:S(2)}) collective-permute-start(bf16[256,640]{1,0:T(8,128)(2,1)S(1)} %slice.9), channel_id=1, source_target_pairs={{0,256},{256,512},{512,768},{768,0},{1,257},{257,513},{513,769},{7... | collective-permute-start | bytes 983048 | tf_op jit(solution)/shard_map/ppermute | solution.py:201
  52.4 3.9 %collective-permute-done.2.far_low = bf16[256,640]{1,0:T(8,128)(2,1)S(1)} collective-permute-done((bf16[256,640]{1,0:T(8,128)(2,1)S(1)}, bf16[256,640]{1,0:T(8,128)(2,1)S(1)}, u32[]{:S(2)}, u32[]{:S(2)}) %collective-permute-start.2) | collective-permute-done | bytes 327712 | tf_op jit(solution)/shard_map/ppermute | solution.py:201
  56.3 5.5 %collective-permute-done.3.far_high = bf16[256,640]{1,0:T(8,128)(2,1)S(1)} collective-permute-done((bf16[256,640]{1,0:T(8,128)(2,1)S(1)}, bf16[256,640]{1,0:T(8,128)(2,1)S(1)}, u32[]{:S(2)}, u32[]{:S(2)}) %collective-permute-start.3) | collective-permute-done | bytes 327712 | tf_op jit(solution)/shard_map/ppermute | solution.py:201
  61.8 0.4 shard_map.95
  62.2 1.1 copy-done.1
  63.2 0.3 shard_map.96.own
  63.6 1.9 %collective-permute-start.4 = (bf16[2,512,256]{2,1,0:T(8,128)(2,1)S(1)}, bf16[2,512,256]{2,1,0:T(8,128)(2,1)S(1)}, u32[]{:S(2)}, u32[]{:S(2)}) collective-permute-start(bf16[2,512,256]{2,1,0:T(8,128)(2,1)S(1)} %shard_map.96.own), channel_id=1, source_target_pairs={{0,1},{1,0},{2,3},{3,2},{4,5},{5,4},{6,7},{7,6},{8,9},{9,8},{10,11... | collective-permute-start | bytes 1572872 | tf_op jit(solution)/shard_map/ppermute | solution.py:197
  65.5 1.9 %collective-permute-done.4.other = bf16[2,512,256]{2,1,0:T(8,128)(2,1)S(1)} collective-permute-done((bf16[2,512,256]{2,1,0:T(8,128)(2,1)S(1)}, bf16[2,512,256]{2,1,0:T(8,128)(2,1)S(1)}, u32[]{:S(2)}, u32[]{:S(2)}) %collective-permute-start.4) | collective-permute-done | bytes 524320 | tf_op jit(solution)/shard_map/ppermute | solution.py:197
  67.4 1.1 copy-done.4
  68.4 1.0 shard_map.97
  69.4 20.9 %all_to_all.20.got = bf16[4,128,1280]{2,1,0:T(8,128)(2,1)S(1)} all-to-all(bf16[4,128,1280]{2,1,0:T(8,128)(2,1)S(1)} %bitcast.16), channel_id=1, replica_groups=mesh['y'=4,'x'=4,'l'=8,'h'=4,'c'=2] {'y'}, dimensions={0} | all-to-all | bytes 2621440 | tf_op jit(solution)/shard_map/all_to_all | solution.py:193
  90.4 0.4 shard_map.98
  90.8 0.9 copy-done.2
  91.7 0.9 shard_map.99
  92.6 1.9 %collective-permute-start.5 = (bf16[128,1024]{1,0:T(8,128)(2,1)S(1)}, bf16[128,1024]{1,0:T(8,128)(2,1)S(1)}, u32[]{:S(2)}, u32[]{:S(2)}) collective-permute-start(bf16[128,1024]{1,0:T(8,128)(2,1)S(1)} %get-tuple-element.22), channel_id=1, source_target_pairs={{0,1},{1,0},{2,3},{3,2},{4,5},{5,4},{6,7},{7,6},{8,9},{9,8},{10,11... | collective-permute-start | bytes 786440 | tf_op jit(solution)/shard_map/ppermute | solution.py:197
  94.6 1.5 collective-permute-done.5.got
  96.1 0.7 shard_map.100
  96.8 22.8 %all-to-all-start.2 = ((bf16[32,16,256]{2,1,0:T(8,128)(2,1)}), bf16[32,16,256]{2,1,0:T(8,128)(2,1)S(1)}, u32[]{:S(2)}, u32[]{:S(2)}) async-start(bf16[32,16,256]{2,1,0:T(8,128)(2,1)} %bitcast.9), calls=%async_computation.2 | async-start | bytes 524288 | tf_op jit(solution)/shard_map/all_to_all | solution.py:193
  119.7 13.7 %all_gather.6.dh = bf16[512,640]{1,0:T(8,128)(2,1)S(1)} all-gather(bf16[128,640]{1,0:T(8,128)(2,1)S(1)} %get-tuple-element.18.dh), channel_id=1, replica_groups=mesh['y'=4,'x'=4,'l'=8,'h'=4,'c'=2] {'y'}, dimensions={0}, use_global_device_ids=true | all-gather | bytes 819200 | tf_op jit(solution)/shard_map/all_gather | solution.py:250
  133.3 13.0 %all_gather.7.act = bf16[512,640]{1,0:T(8,128)(2,1)S(1)} all-gather(bf16[128,640]{1,0:T(8,128)(2,1)S(1)} %get-tuple-element.23), channel_id=1, replica_groups=mesh['y'=4,'x'=4,'l'=8,'h'=4,'c'=2] {'y'}, dimensions={0}, use_global_device_ids=true | all-gather | bytes 819200 | tf_op jit(solution)/shard_map/all_gather | solution.py:250
  146.4 1.9 %shard_map.101 = (bf16[512,640]{1,0:T(8,128)(2,1)}, bf16[640,512]{1,0:T(8,128)(2,1)}, f32[8,128]{1,0:T(8,128)S(1)}) custom-call(s32[1]{0:T(128)} %bitcast.place, bf16[2,512,256]{2,1,0:T(8,128)(2,1)S(1)} %shard_map.96.own, bf16[2,512,256]{2,1,0:T(8,128)(2,1)S(1)} %collective-permute-done.4.other, bf16[512,640]{1,0:T(8,128)(2,1)S(1)} %all_gather.6.dh, ...), custom_call_target="tpu_custom_call" | custom-call | bytes 3674112 | tf_op jit(solution)/shard_map/pallas_call | solution.py:41
  148.2 6.6 %all-to-all-done.2 = bf16[32,16,256]{2,1,0:T(8,128)(2,1)S(1)} async-done(((bf16[32,16,256]{2,1,0:T(8,128)(2,1)}), bf16[32,16,256]{2,1,0:T(8,128)(2,1)S(1)}, u32[]{:S(2)}, u32[]{:S(2)}) %all-to-all-start.2) | async-done | bytes 262176 | tf_op jit(solution)/shard_map/all_to_all | solution.py:193
  154.9 0.2 shard_map.102
  155.0 9.7 %all_to_all.21 = bf16[4,32,256]{2,1,0:T(8,128)(2,1)S(1)} all-to-all(bf16[4,32,256]{2,1,0:T(8,128)(2,1)S(1)} %bitcast.23), channel_id=1, replica_groups=mesh['y'=4,'x'=4,'l'=8,'h'=4,'c'=2] {'x'}, dimensions={0} | all-to-all | bytes 131072 | tf_op jit(solution)/shard_map/all_to_all | solution.py:193
  164.7 0.8 shard_map.103
  (14 shorter events, 0.1 us)
Async XLA Ops:
  3.3 59.9 %all-to-all-start = ((bf16[128,8,256]{2,1,0:T(8,128)(2,1)}), bf16[128,8,256]{2,1,0:T(8,128)(2,1)S(1)}, u32[]{:S(2)}, u32[]{:S(2)}) async-start(bf16[128,8,256]{2,1,0:T(8,128)(2,1)} %bitcast.28), calls=%async_computation | async-start | bytes 1048576 | tf_op jit(solution)/shard_map/all_to_all | solution.py:193
  22.4 39.4 %copy-start.3 = (bf16[512,640]{1,0:T(8,128)(2,1)S(1)}, bf16[512,640]{1,0:T(8,128)(2,1)}, u32[]{:S(2)}) copy-start(bf16[512,640]{1,0:T(8,128)(2,1)} %get-tuple-element.16.own) | copy-start | bytes 1966084
  22.4 22.3 %collective-permute-start.1 = (bf16[512,640]{1,0:T(8,128)(2,1)}, bf16[512,640]{1,0:T(8,128)(2,1)S(1)}, u32[]{:S(2)}, u32[]{:S(2)}) collective-permute-start(bf16[512,640]{1,0:T(8,128)(2,1)} %get-tuple-element.16.own), channel_id=1, source_target_pairs={{0,768},{256,0},{512,256},{768,512},{1,769},{257,1},{513,257},{769... | collective-permute-start | bytes 1966088 | tf_op jit(solution)/shard_map/ppermute | solution.py:201
  27.7 22.6 %collective-permute-start = (bf16[512,640]{1,0:T(8,128)(2,1)}, bf16[512,640]{1,0:T(8,128)(2,1)S(1)}, u32[]{:S(2)}, u32[]{:S(2)}) collective-permute-start(bf16[512,640]{1,0:T(8,128)(2,1)} %get-tuple-element.16.own), channel_id=1, source_target_pairs={{0,256},{256,512},{512,768},{768,0},{1,257},{257,513},{513,769},{7... | collective-permute-start | bytes 1966088 | tf_op jit(solution)/shard_map/ppermute | solution.py:201
  44.7 11.6 %collective-permute-start.2 = (bf16[256,640]{1,0:T(8,128)(2,1)S(1)}, bf16[256,640]{1,0:T(8,128)(2,1)S(1)}, u32[]{:S(2)}, u32[]{:S(2)}) collective-permute-start(bf16[256,640]{1,0:T(8,128)(2,1)S(1)} %slice.8), channel_id=1, source_target_pairs={{0,768},{256,0},{512,256},{768,512},{1,769},{257,1},{513,257},{769... | collective-permute-start | bytes 983048 | tf_op jit(solution)/shard_map/ppermute | solution.py:201
  50.3 17.1 %copy-start = (bf16[1,512,640]{2,1,0:T(8,128)(2,1)S(1)}, bf16[1,512,640]{2,1,0:T(8,128)(2,1)}, u32[]{:S(2)}) copy-start(bf16[1,512,640]{2,1,0:T(8,128)(2,1)} %param.12) | copy-start | bytes 1966084
  50.3 11.5 %collective-permute-start.3 = (bf16[256,640]{1,0:T(8,128)(2,1)S(1)}, bf16[256,640]{1,0:T(8,128)(2,1)S(1)}, u32[]{:S(2)}, u32[]{:S(2)}) collective-permute-start(bf16[256,640]{1,0:T(8,128)(2,1)S(1)} %slice.9), channel_id=1, source_target_pairs={{0,256},{256,512},{512,768},{768,0},{1,257},{257,513},{513,769},{7... | collective-permute-start | bytes 983048 | tf_op jit(solution)/shard_map/ppermute | solution.py:201
  62.2 1.1 copy-start.1
  63.6 3.8 %collective-permute-start.4 = (bf16[2,512,256]{2,1,0:T(8,128)(2,1)S(1)}, bf16[2,512,256]{2,1,0:T(8,128)(2,1)S(1)}, u32[]{:S(2)}, u32[]{:S(2)}) collective-permute-start(bf16[2,512,256]{2,1,0:T(8,128)(2,1)S(1)} %shard_map.96.own), channel_id=1, source_target_pairs={{0,1},{1,0},{2,3},{3,2},{4,5},{5,4},{6,7},{7,6},{8,9},{9,8},{10,11... | collective-permute-start | bytes 1572872 | tf_op jit(solution)/shard_map/ppermute | solution.py:197
  67.4 1.1 copy-start.4
  90.4 1.3 copy-start.2
  92.6 3.4 %collective-permute-start.5 = (bf16[128,1024]{1,0:T(8,128)(2,1)S(1)}, bf16[128,1024]{1,0:T(8,128)(2,1)S(1)}, u32[]{:S(2)}, u32[]{:S(2)}) collective-permute-start(bf16[128,1024]{1,0:T(8,128)(2,1)S(1)} %get-tuple-element.22), channel_id=1, source_target_pairs={{0,1},{1,0},{2,3},{3,2},{4,5},{5,4},{6,7},{7,6},{8,9},{9,8},{10,11... | collective-permute-start | bytes 786440 | tf_op jit(solution)/shard_map/ppermute | solution.py:197
  96.8 58.0 %all-to-all-start.2 = ((bf16[32,16,256]{2,1,0:T(8,128)(2,1)}), bf16[32,16,256]{2,1,0:T(8,128)(2,1)S(1)}, u32[]{:S(2)}, u32[]{:S(2)}) async-start(bf16[32,16,256]{2,1,0:T(8,128)(2,1)} %bitcast.9), calls=%async_computation.2 | async-start | bytes 524288 | tf_op jit(solution)/shard_map/all_to_all | solution.py:193
  146.4 18.4 %copy-start.5 = (s32[128]{0:T(128)S(1)}, s32[128]{0:T(128)}, u32[]{:S(2)}) copy-start(s32[128]{0:T(128)} %param.10) | copy-start | bytes 1540
  146.4 18.4 %copy-start.6 = (s32[128]{0:T(128)S(1)}, s32[128]{0:T(128)}, u32[]{:S(2)}) copy-start(s32[128]{0:T(128)} %param.11) | copy-start | bytes 1540

commit v5 on v4

--- a/solution.py
+++ b/solution.py
@@ -92,7 +92,7 @@
     copies[-1].wait()
 
 
-def regroup_kernel(place, got, _, out):
+def regroup_kernel(place, got, _, __, out):
     rows, xs = out.shape[1] // 4, 4
     count = 2 * rows
     n = lax.broadcasted_iota(jnp.int32, (count, count), 0)
@@ -105,19 +105,6 @@
         out[1, y * rows : (y + 1) * rows] = moved[rows:]
 
 
-def arrange_kernel(place, own, left, right, far_low, far_high, mine, theirs, done):
-    done[...] = jnp.zeros_like(done)
-    y, c = place[0] >> 1, core(place)
-    hs = 4
-    f = own.shape[0] // (2 * hs)
-    for out, at in ((mine, c), (theirs, 1 - c)):
-        for src, q in ((own, y), (left, (y + 3) & 3), (right, (y + 1) & 3), (None, (y + 2) & 3)):
-            for h in range(hs):
-                ref, h_in = (src, h) if src is not None else ((far_low, far_high)[h // 2], h % 2)
-                rows = ref[pl.ds(pl.multiple_of((h_in * 2 + at) * f, f), f), :]
-                out[pl.ds(pl.multiple_of((h * 4 + q) * f, f), f), :] = rows
-
-
 def halves(place, ref, axis):
     n = ref.shape[axis] // 2
     for c in (core(place), 1 - core(place)):
@@ -146,9 +133,16 @@
     act[...] = gelu_value.astype(bf16)
 
 
-def back_kernel(place, dh, w_mine, w_theirs, mine, theirs):
-    theirs[...] = dot(dh[...], w_theirs[...], ((1,), (1,))).astype(bf16)
-    mine[...] = dot(dh[...], w_mine[...], ((1,), (1,)))
+def back_kernel(place, dh, own, left, right, far, mine, theirs, w):
+    y, c = place[0] >> 1, core(place)
+    hs = 4
+    f = own.shape[0] // (2 * hs)
+    for out, at in ((theirs, 1 - c), (mine, c)):
+        for src, q in ((own, y), (left, (y + 3) & 3), (right, (y + 1) & 3), (far, (y + 2) & 3)):
+            for h in range(hs):
+                rows = src[pl.ds(pl.multiple_of((h * 2 + at) * f, f), f), :]
+                w[pl.ds(pl.multiple_of((h * 4 + q) * f, f), f), :] = rows
+        out[...] = dot(dh[...], w[...], ((1,), (1,))).astype(out.dtype)
 
 
 def pack_kernel(place, mine, got, out):
@@ -231,25 +225,34 @@
     )
     got = exchange(sent.reshape(groups, 8, part), ("y", "x", "l")).reshape(groups * 8, part)
     left, right = over_y(w_pass, 1), over_y(w_pass, -1)
-    far_low, far_high = over_y(right[:part], -1), over_y(left[part:], 1)
-    token = ((8, 128), f32)
-    w_mine, w_theirs, done = call(
-        arrange_kernel, [((ys * part, hid), bf16)] * 2 + [token], w_pass, left, right, far_low, far_high
-    )
-    (own,) = call(regroup_kernel, [((2, rows, part), bf16)], got, after=(done,))
+    far = over_y(right, -1)
+    arrived = tuple(a[:16, :128] for a in (left, right))
+    (own,) = call(regroup_kernel, [((2, rows, part), bf16)], got, after=arrived)
     other = other_core(own)
     (parts,) = call(parts_kernel, [((rows, 2 * hid), bf16)], own, other, w_in, w_out)
     got = exchange(parts.reshape(ys, chunk, 2 * hid), "y")
     dh, act = call(gelu_kernel, [((chunk, hid), bf16)] * 2, got)
     mine, theirs = call(
-        back_kernel, [((chunk, ys * part), f32), ((chunk, ys * part), bf16)], dh, w_mine, w_theirs
+        back_kernel,
+        [((chunk, ys * part), f32), ((chunk, ys * part), bf16)],
+        dh,
+        w_in,
+        left,
+        right,
+        far,
+        scratch=[pltpu.VMEM((ys * part, hid), bf16)],
     )
     got = other_core(theirs)
     (sent,) = call(pack_kernel, [((ls, hs, xs * 4, part), bf16)], mine, got)
     got = exchange(sent.reshape(ls * hs, xs * 4, part), ("l", "h"))
     dh, act = (lax.all_gather(a, "y", axis=0, tiled=True) for a in (dh, act))
     g_in, g_out, done = call(
-        grads_kernel, [((width, hid), bf16), ((hid, width), bf16), token], own, other, dh, act
+        grads_kernel,
+        [((width, hid), bf16), ((hid, width), bf16), ((8, 128), f32)],
+        own,
+        other,
+        dh,
+        act,
     )
     (sent,) = call(
         sum_kernel, [((chunk, part), bf16)], got.reshape(ls, hs, xs * 4, part), after=(done,)

time: 166 us -> 168 us (1.012)
  waiting for transfers between devices: 34.5 us -> 57.9 us
  blocking collectives: 57.3 us -> 34.6 us
  Pallas kernels: 9.27 us -> 11.3 us
    all_to_all x2 -> x1, blocking collectives: 30.6 us -> 7.99 us  [exchange(): return lax.all_to_all(x, axes, split_axis=0, concat_axis=0, tiled=True)]
    all_to_all x2 -> x3, waiting for transfers between devices: 6.63 us -> 25.7 us  [exchange(): return lax.all_to_all(x, axes, split_axis=0, concat_axis=0, tiled=True)]
    ppermute x4 -> x3, waiting for transfers between devices: 24.5 us -> 28.8 us  [over_y(): return lax.ppermute(x, 'y', [(y, (y + step) % 4) for y in range(4)])]
    all_to_all x2 -> x3, starting transfers between devices: 41.9 us -> 45.7 us  [exchange(): return lax.all_to_all(x, axes, split_axis=0, concat_axis=0, tiled=True)]
    ppermute x4 -> x3, starting transfers between devices: 14.7 us -> 12.2 us  [over_y(): return lax.ppermute(x, 'y', [(y, (y + step) % 4) for y in range(4)])]
    pallas_call x10 -> x9, Pallas kernels: 9.27 us -> 11.3 us  [call(): pl.pallas_call(kernel, out_shape=[jax.ShapeDtypeStruct(s, d) for s, d in...]
  transfers between devices with their start and end apart: 8 -> 8, of which waited for: 6 -> 8; matrix products, arithmetic and copies ran while one was open for 0% -> 0% of each run, Pallas kernels for 1% -> 1%
where the time goes in v5:
time: 168 us
  starting transfers between devices  61.7 us (37%)
  waiting for transfers between devices  57.9 us (34%)
  blocking collectives  34.6 us (21%)
  Pallas kernels  11.3 us (7%)
  local copies, waits for them, and re-layouts  1.7 us (1%)
    all_to_all x3, starting transfers between devices, exchange(): return lax.all_to_all(x, axes, split_axis=0, concat_axis=0, tiled=True)  45.7 us
    ppermute x3, waiting for transfers between devices, over_y(): return lax.ppermute(x, 'y', [(y, (y + step) % 4) for y in range(4)])  28.8 us
    all_gather x2, blocking collectives, local(): dh, act = (lax.all_gather(a, 'y', axis=0, tiled=True) for a in (dh, act))  26.6 us
    all_to_all x3, waiting for transfers between devices, exchange(): return lax.all_to_all(x, axes, split_axis=0, concat_axis=0, tiled=True)  25.7 us
    ppermute x3, starting transfers between devices, over_y(): return lax.ppermute(x, 'y', [(y, (y + step) % 4) for y in range(4)])  12.2 us
    pallas_call x9, Pallas kernels, call(): pl.pallas_call(kernel, out_shape=[jax.ShapeDtypeStruct(s, d) for s, d in...  11.3 us
    all_to_all x1, blocking collectives, exchange(): return lax.all_to_all(x, axes, split_axis=0, concat_axis=0, tiled=True)  7.99 us
    ppermute x2, starting transfers between devices, other_core(): return lax.ppermute(x, 'c', [(0, 1), (1, 0)])  3.84 us
  transfers between devices with their start and end apart: 8, of which 8 were waited for; matrix products, arithmetic and copies ran while one was open for 0% of the time, Pallas kernels for 1%

profile of v5, /device:TPU:32, one launch (start us, length us, event | category | flops | bytes accessed | tf_op | source)
XLA Modules:
  0.0 167.9 jit_solution(8134318875674853614)
XLA Ops:
  0.6 2.7 %shard_map.94 = (bf16[1024,256]{1,0:T(8,128)(2,1)}, bf16[512,640]{1,0:T(8,128)(2,1)}) custom-call(s32[1]{0:T(128)} %bitcast.place, s32[1,128]{1,0:T(1,128)} %bitcast.24, s32[1,128]{1,0:T(1,128)} %bitcast.26, f32[1,128]{1,0:T(1,128)} %bitcast.30, bf16[128,2048]{1,0:T(8,128)(2,1)} %tok.1, bf16[128,2048]{1,0:T(8,128)(2,1)} %cot.1, bf16[512,640]{1,0:T(8,128)(2,1)} %bitcast.16), custom_call_target="tpu_custom_call" | custom-call | bytes 2885120 | tf_op jit(solution)/shard_map/pallas_call | solution.py:41
  3.3 0.0 copy-start
  3.3 0.0 copy-start.5
  3.3 19.2 %all-to-all-start = ((bf16[128,8,256]{2,1,0:T(8,128)(2,1)}), bf16[128,8,256]{2,1,0:T(8,128)(2,1)S(1)}, u32[]{:S(2)}, u32[]{:S(2)}) async-start(bf16[128,8,256]{2,1,0:T(8,128)(2,1)} %bitcast.28), calls=%async_computation | async-start | bytes 1048576 | tf_op jit(solution)/shard_map/all_to_all | solution.py:187
  22.5 3.5 %collective-permute-start = (bf16[512,640]{1,0:T(8,128)(2,1)}, bf16[512,640]{1,0:T(8,128)(2,1)S(1)}, u32[]{:S(2)}, u32[]{:S(2)}) collective-permute-start(bf16[512,640]{1,0:T(8,128)(2,1)} %get-tuple-element.13), channel_id=1, source_target_pairs={{0,256},{256,512},{512,768},{768,0},{1,257},{257,513},{513,769},{7... | collective-permute-start | bytes 1966088 | tf_op jit(solution)/shard_map/ppermute | solution.py:195
  26.0 3.6 %collective-permute-start.1 = (bf16[512,640]{1,0:T(8,128)(2,1)}, bf16[512,640]{1,0:T(8,128)(2,1)S(1)}, u32[]{:S(2)}, u32[]{:S(2)}) collective-permute-start(bf16[512,640]{1,0:T(8,128)(2,1)} %get-tuple-element.13), channel_id=1, source_target_pairs={{0,768},{256,0},{512,256},{768,512},{1,769},{257,1},{513,257},{769... | collective-permute-start | bytes 1966088 | tf_op jit(solution)/shard_map/ppermute | solution.py:195
  29.6 16.4 %collective-permute-done.left = bf16[512,640]{1,0:T(8,128)(2,1)S(1)} collective-permute-done((bf16[512,640]{1,0:T(8,128)(2,1)}, bf16[512,640]{1,0:T(8,128)(2,1)S(1)}, u32[]{:S(2)}, u32[]{:S(2)}) %collective-permute-start) | collective-permute-done | bytes 655392 | tf_op jit(solution)/shard_map/ppermute | solution.py:195
  46.0 0.8 copy-done.1
  46.9 0.1 collective-permute-done.1.right
  47.0 0.8 copy-done.3
  47.8 5.6 %all-to-all-done = bf16[128,8,256]{2,1,0:T(8,128)(2,1)S(1)} async-done(((bf16[128,8,256]{2,1,0:T(8,128)(2,1)}), bf16[128,8,256]{2,1,0:T(8,128)(2,1)S(1)}, u32[]{:S(2)}, u32[]{:S(2)}) %all-to-all-start) | async-done | bytes 524320 | tf_op jit(solution)/shard_map/all_to_all | solution.py:187
  53.4 0.3 shard_map.95.own
  53.7 1.9 %collective-permute-start.2 = (bf16[2,512,256]{2,1,0:T(8,128)(2,1)S(1)}, bf16[2,512,256]{2,1,0:T(8,128)(2,1)S(1)}, u32[]{:S(2)}, u32[]{:S(2)}) collective-permute-start(bf16[2,512,256]{2,1,0:T(8,128)(2,1)S(1)} %shard_map.95.own), channel_id=1, source_target_pairs={{0,1},{1,0},{2,3},{3,2},{4,5},{5,4},{6,7},{7,6},{8,9},{9,8},{10,11... | collective-permute-start | bytes 1572872 | tf_op jit(solution)/shard_map/ppermute | solution.py:191
  55.6 1.9 %collective-permute-done.2.other = bf16[2,512,256]{2,1,0:T(8,128)(2,1)S(1)} collective-permute-done((bf16[2,512,256]{2,1,0:T(8,128)(2,1)S(1)}, bf16[2,512,256]{2,1,0:T(8,128)(2,1)S(1)}, u32[]{:S(2)}, u32[]{:S(2)}) %collective-permute-start.2) | collective-permute-done | bytes 524320 | tf_op jit(solution)/shard_map/ppermute | solution.py:191
  57.5 2.1 %shard_map.96 = bf16[512,1280]{1,0:T(8,128)(2,1)} custom-call(s32[1]{0:T(128)} %bitcast.place, bf16[2,512,256]{2,1,0:T(8,128)(2,1)S(1)} %shard_map.95.own, bf16[2,512,256]{2,1,0:T(8,128)(2,1)S(1)} %collective-permute-done.2.other, bf16[512,640]{1,0:T(8,128)(2,1)S(1)} %bitcast.17, bf16[640,512]{1,0:T(8,128)(2,1)S(1)} %bitcast.21), custom_call_target="tpu_custom_call" | custom-call | bytes 3670016 | tf_op jit(solution)/shard_map/pallas_call | solution.py:41
  59.6 3.5 %all-to-all-start.1 = ((bf16[4,128,1280]{2,1,0:T(8,128)(2,1)}), bf16[4,128,1280]{2,1,0:T(8,128)(2,1)S(1)}, u32[]{:S(2)}, u32[]{:S(2)}) async-start(bf16[4,128,1280]{2,1,0:T(8,128)(2,1)} %bitcast.8), calls=%async_computation.1 | async-start | bytes 2621440 | tf_op jit(solution)/shard_map/all_to_all | solution.py:187
  63.1 5.1 %collective-permute-start.3 = (bf16[512,640]{1,0:T(8,128)(2,1)}, bf16[512,640]{1,0:T(8,128)(2,1)}, u32[]{:S(2)}, u32[]{:S(2)}) collective-permute-start(bf16[512,640]{1,0:T(8,128)(2,1)} %copy-done.3), channel_id=1, source_target_pairs={{0,768},{256,0},{512,256},{768,512},{1,769},{257,1},{513,257},{769... | collective-permute-start | bytes 1966088 | tf_op jit(solution)/shard_map/ppermute | solution.py:195
  68.2 13.3 %all-to-all-done.1.got = bf16[4,128,1280]{2,1,0:T(8,128)(2,1)S(1)} async-done(((bf16[4,128,1280]{2,1,0:T(8,128)(2,1)}), bf16[4,128,1280]{2,1,0:T(8,128)(2,1)S(1)}, u32[]{:S(2)}, u32[]{:S(2)}) %all-to-all-start.1) | async-done | bytes 1310752 | tf_op jit(solution)/shard_map/all_to_all | solution.py:187
  81.6 0.4 shard_map.97
  82.0 12.3 %collective-permute-done.3.far = bf16[512,640]{1,0:T(8,128)(2,1)} collective-permute-done((bf16[512,640]{1,0:T(8,128)(2,1)}, bf16[512,640]{1,0:T(8,128)(2,1)}, u32[]{:S(2)}, u32[]{:S(2)}) %collective-permute-start.3) | collective-permute-done | bytes 655392 | tf_op jit(solution)/shard_map/ppermute | solution.py:195
  94.3 2.3 %shard_map.98 = (f32[128,1024]{1,0:T(8,128)S(1)}, bf16[128,1024]{1,0:T(8,128)(2,1)S(1)}) custom-call(s32[1]{0:T(128)} %bitcast.place, bf16[128,640]{1,0:T(8,128)(2,1)S(1)} %get-tuple-element.14.dh, bf16[512,640]{1,0:T(8,128)(2,1)S(1)} %bitcast.18, bf16[512,640]{1,0:T(8,128)(2,1)S(1)} %copy-done.2, bf16[512,640]{1,0:T(8,128)(2,1)S(1)} %copy-done.4, ...), custom_call_target="tpu_custom_call" | custom-call | bytes 3571712 | tf_op jit(solution)/shard_map/pallas_call | solution.py:41
  96.6 1.9 %collective-permute-start.4 = (bf16[128,1024]{1,0:T(8,128)(2,1)S(1)}, bf16[128,1024]{1,0:T(8,128)(2,1)S(1)}, u32[]{:S(2)}, u32[]{:S(2)}) collective-permute-start(bf16[128,1024]{1,0:T(8,128)(2,1)S(1)} %get-tuple-element.16), channel_id=1, source_target_pairs={{0,1},{1,0},{2,3},{3,2},{4,5},{5,4},{6,7},{7,6},{8,9},{9,8},{10,11... | collective-permute-start | bytes 786440 | tf_op jit(solution)/shard_map/ppermute | solution.py:191
  98.5 1.5 collective-permute-done.4.got
  100.0 0.7 shard_map.99
  100.7 22.9 %all-to-all-start.2 = ((bf16[32,16,256]{2,1,0:T(8,128)(2,1)}), bf16[32,16,256]{2,1,0:T(8,128)(2,1)S(1)}, u32[]{:S(2)}, u32[]{:S(2)}) async-start(bf16[32,16,256]{2,1,0:T(8,128)(2,1)} %bitcast.9), calls=%async_computation.2 | async-start | bytes 524288 | tf_op jit(solution)/shard_map/all_to_all | solution.py:187
  123.7 13.5 %all_gather.6.dh = bf16[512,640]{1,0:T(8,128)(2,1)S(1)} all-gather(bf16[128,640]{1,0:T(8,128)(2,1)S(1)} %get-tuple-element.14.dh), channel_id=1, replica_groups=mesh['y'=4,'x'=4,'l'=8,'h'=4,'c'=2] {'y'}, dimensions={0}, use_global_device_ids=true | all-gather | bytes 819200 | tf_op jit(solution)/shard_map/all_gather | solution.py:248
  137.2 13.0 %all_gather.7.act = bf16[512,640]{1,0:T(8,128)(2,1)S(1)} all-gather(bf16[128,640]{1,0:T(8,128)(2,1)S(1)} %get-tuple-element.17), channel_id=1, replica_groups=mesh['y'=4,'x'=4,'l'=8,'h'=4,'c'=2] {'y'}, dimensions={0}, use_global_device_ids=true | all-gather | bytes 819200 | tf_op jit(solution)/shard_map/all_gather | solution.py:248
  150.3 1.9 %shard_map.100 = (bf16[512,640]{1,0:T(8,128)(2,1)}, bf16[640,512]{1,0:T(8,128)(2,1)}, f32[8,128]{1,0:T(8,128)S(1)}) custom-call(s32[1]{0:T(128)} %bitcast.place, bf16[2,512,256]{2,1,0:T(8,128)(2,1)S(1)} %shard_map.95.own, bf16[2,512,256]{2,1,0:T(8,128)(2,1)S(1)} %collective-permute-done.2.other, bf16[512,640]{1,0:T(8,128)(2,1)S(1)} %all_gather.6.dh, ...), custom_call_target="tpu_custom_call" | custom-call | bytes 3674112 | tf_op jit(solution)/shard_map/pallas_call | solution.py:41
  152.1 6.8 %all-to-all-done.2 = bf16[32,16,256]{2,1,0:T(8,128)(2,1)S(1)} async-done(((bf16[32,16,256]{2,1,0:T(8,128)(2,1)}), bf16[32,16,256]{2,1,0:T(8,128)(2,1)S(1)}, u32[]{:S(2)}, u32[]{:S(2)}) %all-to-all-start.2) | async-done | bytes 262176 | tf_op jit(solution)/shard_map/all_to_all | solution.py:187
  158.9 0.2 shard_map.101
  159.1 8.0 %all_to_all.20 = bf16[4,32,256]{2,1,0:T(8,128)(2,1)S(1)} all-to-all(bf16[4,32,256]{2,1,0:T(8,128)(2,1)S(1)} %bitcast.23), channel_id=1, replica_groups=mesh['y'=4,'x'=4,'l'=8,'h'=4,'c'=2] {'x'}, dimensions={0} | all-to-all | bytes 131072 | tf_op jit(solution)/shard_map/all_to_all | solution.py:187
  167.1 0.8 shard_map.102
  (14 shorter events, 0.0 us)
Async XLA Ops:
  3.3 54.2 %copy-start = (bf16[1,512,640]{2,1,0:T(8,128)(2,1)S(1)}, bf16[1,512,640]{2,1,0:T(8,128)(2,1)}, u32[]{:S(2)}) copy-start(bf16[1,512,640]{2,1,0:T(8,128)(2,1)} %param.12) | copy-start | bytes 1966084
  3.3 54.2 %copy-start.5 = (bf16[1,640,512]{2,1,0:T(8,128)(2,1)S(1)}, bf16[1,640,512]{2,1,0:T(8,128)(2,1)}, u32[]{:S(2)}) copy-start(bf16[1,640,512]{2,1,0:T(8,128)(2,1)} %param.13) | copy-start | bytes 1966084
  3.3 50.1 %all-to-all-start = ((bf16[128,8,256]{2,1,0:T(8,128)(2,1)}), bf16[128,8,256]{2,1,0:T(8,128)(2,1)S(1)}, u32[]{:S(2)}, u32[]{:S(2)}) async-start(bf16[128,8,256]{2,1,0:T(8,128)(2,1)} %bitcast.28), calls=%async_computation | async-start | bytes 1048576 | tf_op jit(solution)/shard_map/all_to_all | solution.py:187
  22.5 23.5 %collective-permute-start = (bf16[512,640]{1,0:T(8,128)(2,1)}, bf16[512,640]{1,0:T(8,128)(2,1)S(1)}, u32[]{:S(2)}, u32[]{:S(2)}) collective-permute-start(bf16[512,640]{1,0:T(8,128)(2,1)} %get-tuple-element.13), channel_id=1, source_target_pairs={{0,256},{256,512},{512,768},{768,0},{1,257},{257,513},{513,769},{7... | collective-permute-start | bytes 1966088 | tf_op jit(solution)/shard_map/ppermute | solution.py:195
  26.0 21.0 %collective-permute-start.1 = (bf16[512,640]{1,0:T(8,128)(2,1)}, bf16[512,640]{1,0:T(8,128)(2,1)S(1)}, u32[]{:S(2)}, u32[]{:S(2)}) collective-permute-start(bf16[512,640]{1,0:T(8,128)(2,1)} %get-tuple-element.13), channel_id=1, source_target_pairs={{0,768},{256,0},{512,256},{768,512},{1,769},{257,1},{513,257},{769... | collective-permute-start | bytes 1966088 | tf_op jit(solution)/shard_map/ppermute | solution.py:195
  46.0 0.8 copy-start.1
  47.0 0.8 copy-start.3
  53.7 3.8 %collective-permute-start.2 = (bf16[2,512,256]{2,1,0:T(8,128)(2,1)S(1)}, bf16[2,512,256]{2,1,0:T(8,128)(2,1)S(1)}, u32[]{:S(2)}, u32[]{:S(2)}) collective-permute-start(bf16[2,512,256]{2,1,0:T(8,128)(2,1)S(1)} %shard_map.95.own), channel_id=1, source_target_pairs={{0,1},{1,0},{2,3},{3,2},{4,5},{5,4},{6,7},{7,6},{8,9},{9,8},{10,11... | collective-permute-start | bytes 1572872 | tf_op jit(solution)/shard_map/ppermute | solution.py:191
  59.6 22.0 %all-to-all-start.1 = ((bf16[4,128,1280]{2,1,0:T(8,128)(2,1)}), bf16[4,128,1280]{2,1,0:T(8,128)(2,1)S(1)}, u32[]{:S(2)}, u32[]{:S(2)}) async-start(bf16[4,128,1280]{2,1,0:T(8,128)(2,1)} %bitcast.8), calls=%async_computation.1 | async-start | bytes 2621440 | tf_op jit(solution)/shard_map/all_to_all | solution.py:187
  63.1 31.1 %collective-permute-start.3 = (bf16[512,640]{1,0:T(8,128)(2,1)}, bf16[512,640]{1,0:T(8,128)(2,1)}, u32[]{:S(2)}, u32[]{:S(2)}) collective-permute-start(bf16[512,640]{1,0:T(8,128)(2,1)} %copy-done.3), channel_id=1, source_target_pairs={{0,768},{256,0},{512,256},{768,512},{1,769},{257,1},{513,257},{769... | collective-permute-start | bytes 1966088 | tf_op jit(solution)/shard_map/ppermute | solution.py:195
  81.6 12.7 %copy-start.2 = (bf16[512,640]{1,0:T(8,128)(2,1)S(1)}, bf16[512,640]{1,0:T(8,128)(2,1)}, u32[]{:S(2)}) copy-start(bf16[512,640]{1,0:T(8,128)(2,1)} %copy-done.1) | copy-start | bytes 1966084
  81.6 12.7 %copy-start.4 = (bf16[512,640]{1,0:T(8,128)(2,1)S(1)}, bf16[512,640]{1,0:T(8,128)(2,1)}, u32[]{:S(2)}) copy-start(bf16[512,640]{1,0:T(8,128)(2,1)} %copy-done.3) | copy-start | bytes 1966084
  96.6 3.4 %collective-permute-start.4 = (bf16[128,1024]{1,0:T(8,128)(2,1)S(1)}, bf16[128,1024]{1,0:T(8,128)(2,1)S(1)}, u32[]{:S(2)}, u32[]{:S(2)}) collective-permute-start(bf16[128,1024]{1,0:T(8,128)(2,1)S(1)} %get-tuple-element.16), channel_id=1, source_target_pairs={{0,1},{1,0},{2,3},{3,2},{4,5},{5,4},{6,7},{7,6},{8,9},{9,8},{10,11... | collective-permute-start | bytes 786440 | tf_op jit(solution)/shard_map/ppermute | solution.py:191
  100.7 58.1 %all-to-all-start.2 = ((bf16[32,16,256]{2,1,0:T(8,128)(2,1)}), bf16[32,16,256]{2,1,0:T(8,128)(2,1)S(1)}, u32[]{:S(2)}, u32[]{:S(2)}) async-start(bf16[32,16,256]{2,1,0:T(8,128)(2,1)} %bitcast.9), calls=%async_computation.2 | async-start | bytes 524288 | tf_op jit(solution)/shard_map/all_to_all | solution.py:187
  150.3 16.8 %copy-start.6 = (s32[128]{0:T(128)S(1)}, s32[128]{0:T(128)}, u32[]{:S(2)}) copy-start(s32[128]{0:T(128)} %param.10) | copy-start | bytes 1540
  150.3 16.8 %copy-start.7 = (s32[128]{0:T(128)S(1)}, s32[128]{0:T(128)}, u32[]{:S(2)}) copy-start(s32[128]{0:T(128)} %param.11) | copy-start | bytes 1540

commit v6 on v5

--- a/solution.py
+++ b/solution.py
@@ -112,7 +112,7 @@
         yield ref[part, :] if axis == 0 else ref[:, part]
 
 
-def parts_kernel(place, own, other, w_in, w_out, out):
+def parts_kernel(place, own, other, w_in, w_out, _, out):
     hid = w_in.shape[1]
     (in_own, in_other), (out_own, out_other) = halves(place, w_in, 0), halves(place, w_out, 1)
     out[:, :hid] = (
@@ -229,7 +229,9 @@
     arrived = tuple(a[:16, :128] for a in (left, right))
     (own,) = call(regroup_kernel, [((2, rows, part), bf16)], got, after=arrived)
     other = other_core(own)
-    (parts,) = call(parts_kernel, [((rows, 2 * hid), bf16)], own, other, w_in, w_out)
+    (parts,) = call(
+        parts_kernel, [((rows, 2 * hid), bf16)], own, other, w_in, w_out, after=(far[:16, :128],)
+    )
     got = exchange(parts.reshape(ys, chunk, 2 * hid), "y")
     dh, act = call(gelu_kernel, [((chunk, hid), bf16)] * 2, got)
     mine, theirs = call(

time: 168 us -> 163 us (0.970)
  waiting for transfers between devices: 57.9 us -> 34 us
  blocking collectives: 34.6 us -> 57.2 us
  starting transfers between devices: 61.7 us -> 58.4 us
    all_to_all x1 -> x2, blocking collectives: 7.99 us -> 30.5 us  [exchange(): return lax.all_to_all(x, axes, split_axis=0, concat_axis=0, tiled=True)]
    all_to_all x3 -> x2, waiting for transfers between devices: 25.7 us -> 9.74 us  [exchange(): return lax.all_to_all(x, axes, split_axis=0, concat_axis=0, tiled=True)]
    ppermute x3, waiting for transfers between devices: 28.8 us -> 22.8 us  [over_y(): return lax.ppermute(x, 'y', [(y, (y + step) % 4) for y in range(4)])]
    all_to_all x3 -> x2, starting transfers between devices: 45.7 us -> 42 us  [exchange(): return lax.all_to_all(x, axes, split_axis=0, concat_axis=0, tiled=True)]
    ppermute x2, waiting for transfers between devices: 3.38 us -> 1.5 us  [other_core(): return lax.ppermute(x, 'c', [(0, 1), (1, 0)])]
  transfers between devices with their start and end apart: 8 -> 7, of which waited for: 8 -> 5; matrix products, arithmetic and copies ran while one was open for 0% -> 0% of each run, Pallas kernels for 1% -> 1%
where the time goes in v6:
time: 163 us; the launch traced here: 162 us
  starting transfers between devices  58.4 us (36%)
  blocking collectives  57.2 us (35%)
  waiting for transfers between devices  34 us (21%)
  Pallas kernels  10.2 us (6%)
  local copies, waits for them, and re-layouts  1.79 us (1%)
    all_to_all x2, starting transfers between devices, exchange(): return lax.all_to_all(x, axes, split_axis=0, concat_axis=0, tiled=True)  42 us
    all_to_all x2, blocking collectives, exchange(): return lax.all_to_all(x, axes, split_axis=0, concat_axis=0, tiled=True)  30.5 us
    all_gather x2, blocking collectives, local(): dh, act = (lax.all_gather(a, 'y', axis=0, tiled=True) for a in (dh, act))  26.7 us
    ppermute x3, waiting for transfers between devices, over_y(): return lax.ppermute(x, 'y', [(y, (y + step) % 4) for y in range(4)])  22.8 us
    ppermute x3, starting transfers between devices, over_y(): return lax.ppermute(x, 'y', [(y, (y + step) % 4) for y in range(4)])  12.5 us
    pallas_call x9, Pallas kernels, call(): pl.pallas_call(kernel, out_shape=[jax.ShapeDtypeStruct(s, d) for s, d in...  10.2 us
    all_to_all x2, waiting for transfers between devices, exchange(): return lax.all_to_all(x, axes, split_axis=0, concat_axis=0, tiled=True)  9.74 us
    ppermute x2, starting transfers between devices, other_core(): return lax.ppermute(x, 'c', [(0, 1), (1, 0)])  3.84 us
  transfers between devices with their start and end apart: 7, of which 5 were waited for; matrix products, arithmetic and copies ran while one was open for 0% of the time, Pallas kernels for 1%

profile of v6, /device:TPU:32, one launch (start us, length us, event | category | flops | bytes accessed | tf_op | source)
XLA Modules:
  0.0 162.4 jit_solution(897700429032514256)
XLA Ops:
  0.6 2.7 %shard_map.94 = (bf16[1024,256]{1,0:T(8,128)(2,1)}, bf16[512,640]{1,0:T(8,128)(2,1)}) custom-call(s32[1]{0:T(128)} %bitcast.place, s32[1,128]{1,0:T(1,128)} %bitcast.25, s32[1,128]{1,0:T(1,128)} %bitcast.27, f32[1,128]{1,0:T(1,128)} %bitcast.31, bf16[128,2048]{1,0:T(8,128)(2,1)} %tok.1, bf16[128,2048]{1,0:T(8,128)(2,1)} %cot.1, bf16[512,640]{1,0:T(8,128)(2,1)} %bitcast.16), custom_call_target="tpu_custom_call" | custom-call | bytes 2885120 | tf_op jit(solution)/shard_map/pallas_call | solution.py:41
  3.3 0.0 copy-start
  3.3 19.2 %all-to-all-start = ((bf16[128,8,256]{2,1,0:T(8,128)(2,1)}), bf16[128,8,256]{2,1,0:T(8,128)(2,1)S(1)}, u32[]{:S(2)}, u32[]{:S(2)}) async-start(bf16[128,8,256]{2,1,0:T(8,128)(2,1)} %bitcast.29), calls=%async_computation | async-start | bytes 1048576 | tf_op jit(solution)/shard_map/all_to_all | solution.py:187
  22.5 5.1 %collective-permute-start.1 = (bf16[512,640]{1,0:T(8,128)(2,1)}, bf16[512,640]{1,0:T(8,128)(2,1)S(1)}, u32[]{:S(2)}, u32[]{:S(2)}) collective-permute-start(bf16[512,640]{1,0:T(8,128)(2,1)} %get-tuple-element.13), channel_id=1, source_target_pairs={{0,768},{256,0},{512,256},{768,512},{1,769},{257,1},{513,257},{769... | collective-permute-start | bytes 1966088 | tf_op jit(solution)/shard_map/ppermute | solution.py:195
  27.7 1.9 %collective-permute-start = (bf16[512,640]{1,0:T(8,128)(2,1)}, bf16[512,640]{1,0:T(8,128)(2,1)S(1)}, u32[]{:S(2)}, u32[]{:S(2)}) collective-permute-start(bf16[512,640]{1,0:T(8,128)(2,1)} %get-tuple-element.13), channel_id=1, source_target_pairs={{0,256},{256,512},{512,768},{768,0},{1,257},{257,513},{513,769},{7... | collective-permute-start | bytes 1966088 | tf_op jit(solution)/shard_map/ppermute | solution.py:195
  29.6 15.2 %collective-permute-done.1.right = bf16[512,640]{1,0:T(8,128)(2,1)S(1)} collective-permute-done((bf16[512,640]{1,0:T(8,128)(2,1)}, bf16[512,640]{1,0:T(8,128)(2,1)S(1)}, u32[]{:S(2)}, u32[]{:S(2)}) %collective-permute-start.1) | collective-permute-done | bytes 655392 | tf_op jit(solution)/shard_map/ppermute | solution.py:195
  44.7 5.5 %collective-permute-start.3 = (bf16[512,640]{1,0:T(8,128)(2,1)S(1)}, bf16[512,640]{1,0:T(8,128)(2,1)}, u32[]{:S(2)}, u32[]{:S(2)}) collective-permute-start(bf16[512,640]{1,0:T(8,128)(2,1)S(1)} %collective-permute-done.1.right), channel_id=1, source_target_pairs={{0,768},{256,0},{512,256},{768,512},{1,769},{257,1},{513,257},{769... | collective-permute-start | bytes 1966088 | tf_op jit(solution)/shard_map/ppermute | solution.py:195
  50.2 0.0 collective-permute-done.left
  50.3 3.1 %all-to-all-done = bf16[128,8,256]{2,1,0:T(8,128)(2,1)S(1)} async-done(((bf16[128,8,256]{2,1,0:T(8,128)(2,1)}), bf16[128,8,256]{2,1,0:T(8,128)(2,1)S(1)}, u32[]{:S(2)}, u32[]{:S(2)}) %all-to-all-start) | async-done | bytes 524320 | tf_op jit(solution)/shard_map/all_to_all | solution.py:187
  53.4 0.3 shard_map.95.own
  53.7 1.9 %collective-permute-start.2 = (bf16[2,512,256]{2,1,0:T(8,128)(2,1)S(1)}, bf16[2,512,256]{2,1,0:T(8,128)(2,1)S(1)}, u32[]{:S(2)}, u32[]{:S(2)}) collective-permute-start(bf16[2,512,256]{2,1,0:T(8,128)(2,1)S(1)} %shard_map.95.own), channel_id=1, source_target_pairs={{0,1},{1,0},{2,3},{3,2},{4,5},{5,4},{6,7},{7,6},{8,9},{9,8},{10,11... | collective-permute-start | bytes 1572872 | tf_op jit(solution)/shard_map/ppermute | solution.py:191
  55.6 7.6 %collective-permute-done.3.far = bf16[512,640]{1,0:T(8,128)(2,1)} collective-permute-done((bf16[512,640]{1,0:T(8,128)(2,1)S(1)}, bf16[512,640]{1,0:T(8,128)(2,1)}, u32[]{:S(2)}, u32[]{:S(2)}) %collective-permute-start.3) | collective-permute-done | bytes 655392 | tf_op jit(solution)/shard_map/ppermute | solution.py:195
  63.2 0.7 slice.14._
  63.9 0.0 collective-permute-done.2.other
  63.9 0.0 copy-done
  63.9 1.1 copy-done.1
  65.0 1.0 shard_map.96
  66.0 20.9 %all_to_all.20.got = bf16[4,128,1280]{2,1,0:T(8,128)(2,1)S(1)} all-to-all(bf16[4,128,1280]{2,1,0:T(8,128)(2,1)S(1)} %bitcast.19), channel_id=1, replica_groups=mesh['y'=4,'x'=4,'l'=8,'h'=4,'c'=2] {'y'}, dimensions={0} | all-to-all | bytes 2621440 | tf_op jit(solution)/shard_map/all_to_all | solution.py:187
  86.9 0.4 shard_map.97
  87.3 2.3 %shard_map.98 = (f32[128,1024]{1,0:T(8,128)S(1)}, bf16[128,1024]{1,0:T(8,128)(2,1)S(1)}) custom-call(s32[1]{0:T(128)} %bitcast.place, bf16[128,640]{1,0:T(8,128)(2,1)S(1)} %get-tuple-element.14.dh, bf16[512,640]{1,0:T(8,128)(2,1)S(1)} %bitcast.18, bf16[512,640]{1,0:T(8,128)(2,1)S(1)} %collective-permute-done.left, ...), custom_call_target="tpu_custom_call" | custom-call | bytes 3571712 | tf_op jit(solution)/shard_map/pallas_call | solution.py:41
  89.6 1.9 %collective-permute-start.4 = (bf16[128,1024]{1,0:T(8,128)(2,1)S(1)}, bf16[128,1024]{1,0:T(8,128)(2,1)S(1)}, u32[]{:S(2)}, u32[]{:S(2)}) collective-permute-start(bf16[128,1024]{1,0:T(8,128)(2,1)S(1)} %get-tuple-element.16), channel_id=1, source_target_pairs={{0,1},{1,0},{2,3},{3,2},{4,5},{5,4},{6,7},{7,6},{8,9},{9,8},{10,11... | collective-permute-start | bytes 786440 | tf_op jit(solution)/shard_map/ppermute | solution.py:191
  91.5 1.5 collective-permute-done.4.got
  93.0 0.7 shard_map.99
  93.7 22.8 %all-to-all-start.2 = ((bf16[32,16,256]{2,1,0:T(8,128)(2,1)}), bf16[32,16,256]{2,1,0:T(8,128)(2,1)S(1)}, u32[]{:S(2)}, u32[]{:S(2)}) async-start(bf16[32,16,256]{2,1,0:T(8,128)(2,1)} %bitcast.9), calls=%async_computation.2 | async-start | bytes 524288 | tf_op jit(solution)/shard_map/all_to_all | solution.py:187
  116.6 13.7 %all_gather.6.dh = bf16[512,640]{1,0:T(8,128)(2,1)S(1)} all-gather(bf16[128,640]{1,0:T(8,128)(2,1)S(1)} %get-tuple-element.14.dh), channel_id=1, replica_groups=mesh['y'=4,'x'=4,'l'=8,'h'=4,'c'=2] {'y'}, dimensions={0}, use_global_device_ids=true | all-gather | bytes 819200 | tf_op jit(solution)/shard_map/all_gather | solution.py:250
  130.2 13.0 %all_gather.7.act = bf16[512,640]{1,0:T(8,128)(2,1)S(1)} all-gather(bf16[128,640]{1,0:T(8,128)(2,1)S(1)} %get-tuple-element.17), channel_id=1, replica_groups=mesh['y'=4,'x'=4,'l'=8,'h'=4,'c'=2] {'y'}, dimensions={0}, use_global_device_ids=true | all-gather | bytes 819200 | tf_op jit(solution)/shard_map/all_gather | solution.py:250
  143.3 1.9 %shard_map.100 = (bf16[512,640]{1,0:T(8,128)(2,1)}, bf16[640,512]{1,0:T(8,128)(2,1)}, f32[8,128]{1,0:T(8,128)S(1)}) custom-call(s32[1]{0:T(128)} %bitcast.place, bf16[2,512,256]{2,1,0:T(8,128)(2,1)S(1)} %shard_map.95.own, bf16[2,512,256]{2,1,0:T(8,128)(2,1)S(1)} %collective-permute-done.2.other, bf16[512,640]{1,0:T(8,128)(2,1)S(1)} %all_gather.6.dh, ...), custom_call_target="tpu_custom_call" | custom-call | bytes 3674112 | tf_op jit(solution)/shard_map/pallas_call | solution.py:41
  145.1 6.6 %all-to-all-done.2 = bf16[32,16,256]{2,1,0:T(8,128)(2,1)S(1)} async-done(((bf16[32,16,256]{2,1,0:T(8,128)(2,1)}), bf16[32,16,256]{2,1,0:T(8,128)(2,1)S(1)}, u32[]{:S(2)}, u32[]{:S(2)}) %all-to-all-start.2) | async-done | bytes 262176 | tf_op jit(solution)/shard_map/all_to_all | solution.py:187
  151.8 0.2 shard_map.101
  151.9 9.6 %all_to_all.21 = bf16[4,32,256]{2,1,0:T(8,128)(2,1)S(1)} all-to-all(bf16[4,32,256]{2,1,0:T(8,128)(2,1)S(1)} %bitcast.24), channel_id=1, replica_groups=mesh['y'=4,'x'=4,'l'=8,'h'=4,'c'=2] {'x'}, dimensions={0} | all-to-all | bytes 131072 | tf_op jit(solution)/shard_map/all_to_all | solution.py:187
  161.6 0.0 copy-done.2
  161.6 0.8 shard_map.102
  (6 shorter events, 0.0 us)
Async XLA Ops:
  3.3 60.6 %copy-start = (bf16[1,512,640]{2,1,0:T(8,128)(2,1)S(1)}, bf16[1,512,640]{2,1,0:T(8,128)(2,1)}, u32[]{:S(2)}) copy-start(bf16[1,512,640]{2,1,0:T(8,128)(2,1)} %param.12) | copy-start | bytes 1966084
  3.3 50.1 %all-to-all-start = ((bf16[128,8,256]{2,1,0:T(8,128)(2,1)}), bf16[128,8,256]{2,1,0:T(8,128)(2,1)S(1)}, u32[]{:S(2)}, u32[]{:S(2)}) async-start(bf16[128,8,256]{2,1,0:T(8,128)(2,1)} %bitcast.29), calls=%async_computation | async-start | bytes 1048576 | tf_op jit(solution)/shard_map/all_to_all | solution.py:187
  22.5 22.2 %collective-permute-start.1 = (bf16[512,640]{1,0:T(8,128)(2,1)}, bf16[512,640]{1,0:T(8,128)(2,1)S(1)}, u32[]{:S(2)}, u32[]{:S(2)}) collective-permute-start(bf16[512,640]{1,0:T(8,128)(2,1)} %get-tuple-element.13), channel_id=1, source_target_pairs={{0,768},{256,0},{512,256},{768,512},{1,769},{257,1},{513,257},{769... | collective-permute-start | bytes 1966088 | tf_op jit(solution)/shard_map/ppermute | solution.py:195
  27.7 22.6 %collective-permute-start = (bf16[512,640]{1,0:T(8,128)(2,1)}, bf16[512,640]{1,0:T(8,128)(2,1)S(1)}, u32[]{:S(2)}, u32[]{:S(2)}) collective-permute-start(bf16[512,640]{1,0:T(8,128)(2,1)} %get-tuple-element.13), channel_id=1, source_target_pairs={{0,256},{256,512},{512,768},{768,0},{1,257},{257,513},{513,769},{7... | collective-permute-start | bytes 1966088 | tf_op jit(solution)/shard_map/ppermute | solution.py:195
  44.7 18.5 %collective-permute-start.3 = (bf16[512,640]{1,0:T(8,128)(2,1)S(1)}, bf16[512,640]{1,0:T(8,128)(2,1)}, u32[]{:S(2)}, u32[]{:S(2)}) collective-permute-start(bf16[512,640]{1,0:T(8,128)(2,1)S(1)} %collective-permute-done.1.right), channel_id=1, source_target_pairs={{0,768},{256,0},{512,256},{768,512},{1,769},{257,1},{513,257},{769... | collective-permute-start | bytes 1966088 | tf_op jit(solution)/shard_map/ppermute | solution.py:195
  53.7 10.2 %collective-permute-start.2 = (bf16[2,512,256]{2,1,0:T(8,128)(2,1)S(1)}, bf16[2,512,256]{2,1,0:T(8,128)(2,1)S(1)}, u32[]{:S(2)}, u32[]{:S(2)}) collective-permute-start(bf16[2,512,256]{2,1,0:T(8,128)(2,1)S(1)} %shard_map.95.own), channel_id=1, source_target_pairs={{0,1},{1,0},{2,3},{3,2},{4,5},{5,4},{6,7},{7,6},{8,9},{9,8},{10,11... | collective-permute-start | bytes 1572872 | tf_op jit(solution)/shard_map/ppermute | solution.py:191
  63.9 1.1 copy-start.1
  89.6 3.4 %collective-permute-start.4 = (bf16[128,1024]{1,0:T(8,128)(2,1)S(1)}, bf16[128,1024]{1,0:T(8,128)(2,1)S(1)}, u32[]{:S(2)}, u32[]{:S(2)}) collective-permute-start(bf16[128,1024]{1,0:T(8,128)(2,1)S(1)} %get-tuple-element.16), channel_id=1, source_target_pairs={{0,1},{1,0},{2,3},{3,2},{4,5},{5,4},{6,7},{7,6},{8,9},{9,8},{10,11... | collective-permute-start | bytes 786440 | tf_op jit(solution)/shard_map/ppermute | solution.py:191
  93.7 58.0 %all-to-all-start.2 = ((bf16[32,16,256]{2,1,0:T(8,128)(2,1)}), bf16[32,16,256]{2,1,0:T(8,128)(2,1)S(1)}, u32[]{:S(2)}, u32[]{:S(2)}) async-start(bf16[32,16,256]{2,1,0:T(8,128)(2,1)} %bitcast.9), calls=%async_computation.2 | async-start | bytes 524288 | tf_op jit(solution)/shard_map/all_to_all | solution.py:187
  143.3 18.3 %copy-start.2 = (s32[128]{0:T(128)S(1)}, s32[128]{0:T(128)}, u32[]{:S(2)}) copy-start(s32[128]{0:T(128)} %param.10) | copy-start | bytes 1540
  143.3 18.3 %copy-start.3 = (s32[128]{0:T(128)S(1)}, s32[128]{0:T(128)}, u32[]{:S(2)}) copy-start(s32[128]{0:T(128)} %param.11) | copy-start | bytes 1540

commit v7 on v5

--- a/solution.py
+++ b/solution.py
@@ -225,7 +225,7 @@
     )
     got = exchange(sent.reshape(groups, 8, part), ("y", "x", "l")).reshape(groups * 8, part)
     left, right = over_y(w_pass, 1), over_y(w_pass, -1)
-    far = over_y(right, -1)
+    far = over_y(left, 1)
     arrived = tuple(a[:16, :128] for a in (left, right))
     (own,) = call(regroup_kernel, [((2, rows, part), bf16)], got, after=arrived)
     other = other_core(own)

time: 168 us -> 170 us (1.012)
  waiting for transfers between devices: 57.9 us -> 60.8 us
    all_to_all x3, waiting for transfers between devices: 25.7 us -> 27.4 us  [exchange(): return lax.all_to_all(x, axes, split_axis=0, concat_axis=0, tiled=True)]
where the time goes in v7:
time: 170 us; the launch traced here: 169 us
  waiting for transfers between devices  60.8 us (36%)
  starting transfers between devices  60.5 us (36%)
  blocking collectives  34.9 us (21%)
  Pallas kernels  11.3 us (7%)
    all_to_all x3, starting transfers between devices, exchange(): return lax.all_to_all(x, axes, split_axis=0, concat_axis=0, tiled=True)  45.7 us
    ppermute x3, waiting for transfers between devices, over_y(): return lax.ppermute(x, 'y', [(y, (y + step) % 4) for y in range(4)])  30 us
    all_to_all x3, waiting for transfers between devices, exchange(): return lax.all_to_all(x, axes, split_axis=0, concat_axis=0, tiled=True)  27.4 us
    all_gather x2, blocking collectives, local(): dh, act = (lax.all_gather(a, 'y', axis=0, tiled=True) for a in (dh, act))  26.9 us
    pallas_call x9, Pallas kernels, call(): pl.pallas_call(kernel, out_shape=[jax.ShapeDtypeStruct(s, d) for s, d in...  11.3 us
    ppermute x3, starting transfers between devices, over_y(): return lax.ppermute(x, 'y', [(y, (y + step) % 4) for y in range(4)])  10.9 us
    all_to_all x1, blocking collectives, exchange(): return lax.all_to_all(x, axes, split_axis=0, concat_axis=0, tiled=True)  7.99 us
    ppermute x2, starting transfers between devices, other_core(): return lax.ppermute(x, 'c', [(0, 1), (1, 0)])  3.84 us
  transfers between devices with their start and end apart: 8, of which 8 were waited for; matrix products, arithmetic and copies ran while one was open for 0% of the time, Pallas kernels for 1%

profile of v7, /device:TPU:32, one launch (start us, length us, event | category | flops | bytes accessed | tf_op | source)
XLA Modules:
  0.0 169.1 jit_solution(13170243892804184626)
XLA Ops:
  0.6 2.7 %shard_map.94 = (bf16[1024,256]{1,0:T(8,128)(2,1)}, bf16[512,640]{1,0:T(8,128)(2,1)}) custom-call(s32[1]{0:T(128)} %bitcast.place, s32[1,128]{1,0:T(1,128)} %bitcast.24, s32[1,128]{1,0:T(1,128)} %bitcast.26, f32[1,128]{1,0:T(1,128)} %bitcast.30, bf16[128,2048]{1,0:T(8,128)(2,1)} %tok.1, bf16[128,2048]{1,0:T(8,128)(2,1)} %cot.1, bf16[512,640]{1,0:T(8,128)(2,1)} %bitcast.16), custom_call_target="tpu_custom_call" | custom-call | bytes 2885120 | tf_op jit(solution)/shard_map/pallas_call | solution.py:41
  3.3 0.0 copy-start
  3.3 0.0 copy-start.5
  3.3 19.2 %all-to-all-start = ((bf16[128,8,256]{2,1,0:T(8,128)(2,1)}), bf16[128,8,256]{2,1,0:T(8,128)(2,1)S(1)}, u32[]{:S(2)}, u32[]{:S(2)}) async-start(bf16[128,8,256]{2,1,0:T(8,128)(2,1)} %bitcast.28), calls=%async_computation | async-start | bytes 1048576 | tf_op jit(solution)/shard_map/all_to_all | solution.py:187
  22.5 3.5 %collective-permute-start = (bf16[512,640]{1,0:T(8,128)(2,1)}, bf16[512,640]{1,0:T(8,128)(2,1)S(1)}, u32[]{:S(2)}, u32[]{:S(2)}) collective-permute-start(bf16[512,640]{1,0:T(8,128)(2,1)} %get-tuple-element.13), channel_id=1, source_target_pairs={{0,256},{256,512},{512,768},{768,0},{1,257},{257,513},{513,769},{7... | collective-permute-start | bytes 1966088 | tf_op jit(solution)/shard_map/ppermute | solution.py:195
  26.0 3.6 %collective-permute-start.1 = (bf16[512,640]{1,0:T(8,128)(2,1)}, bf16[512,640]{1,0:T(8,128)(2,1)S(1)}, u32[]{:S(2)}, u32[]{:S(2)}) collective-permute-start(bf16[512,640]{1,0:T(8,128)(2,1)} %get-tuple-element.13), channel_id=1, source_target_pairs={{0,768},{256,0},{512,256},{768,512},{1,769},{257,1},{513,257},{769... | collective-permute-start | bytes 1966088 | tf_op jit(solution)/shard_map/ppermute | solution.py:195
  29.6 16.4 %collective-permute-done.left = bf16[512,640]{1,0:T(8,128)(2,1)S(1)} collective-permute-done((bf16[512,640]{1,0:T(8,128)(2,1)}, bf16[512,640]{1,0:T(8,128)(2,1)S(1)}, u32[]{:S(2)}, u32[]{:S(2)}) %collective-permute-start) | collective-permute-done | bytes 655392 | tf_op jit(solution)/shard_map/ppermute | solution.py:195
  46.0 0.9 collective-permute-done.1.right
  47.0 0.0 copy-done.1
  47.0 0.8 copy-done.3
  47.8 5.6 %all-to-all-done = bf16[128,8,256]{2,1,0:T(8,128)(2,1)S(1)} async-done(((bf16[128,8,256]{2,1,0:T(8,128)(2,1)}), bf16[128,8,256]{2,1,0:T(8,128)(2,1)S(1)}, u32[]{:S(2)}, u32[]{:S(2)}) %all-to-all-start) | async-done | bytes 524320 | tf_op jit(solution)/shard_map/all_to_all | solution.py:187
  53.4 0.3 shard_map.95.own
  53.7 1.9 %collective-permute-start.2 = (bf16[2,512,256]{2,1,0:T(8,128)(2,1)S(1)}, bf16[2,512,256]{2,1,0:T(8,128)(2,1)S(1)}, u32[]{:S(2)}, u32[]{:S(2)}) collective-permute-start(bf16[2,512,256]{2,1,0:T(8,128)(2,1)S(1)} %shard_map.95.own), channel_id=1, source_target_pairs={{0,1},{1,0},{2,3},{3,2},{4,5},{5,4},{6,7},{7,6},{8,9},{9,8},{10,11... | collective-permute-start | bytes 1572872 | tf_op jit(solution)/shard_map/ppermute | solution.py:191
  55.6 1.9 %collective-permute-done.2.other = bf16[2,512,256]{2,1,0:T(8,128)(2,1)S(1)} collective-permute-done((bf16[2,512,256]{2,1,0:T(8,128)(2,1)S(1)}, bf16[2,512,256]{2,1,0:T(8,128)(2,1)S(1)}, u32[]{:S(2)}, u32[]{:S(2)}) %collective-permute-start.2) | collective-permute-done | bytes 524320 | tf_op jit(solution)/shard_map/ppermute | solution.py:191
  57.5 2.1 %shard_map.96 = bf16[512,1280]{1,0:T(8,128)(2,1)} custom-call(s32[1]{0:T(128)} %bitcast.place, bf16[2,512,256]{2,1,0:T(8,128)(2,1)S(1)} %shard_map.95.own, bf16[2,512,256]{2,1,0:T(8,128)(2,1)S(1)} %collective-permute-done.2.other, bf16[512,640]{1,0:T(8,128)(2,1)S(1)} %bitcast.17, bf16[640,512]{1,0:T(8,128)(2,1)S(1)} %bitcast.21), custom_call_target="tpu_custom_call" | custom-call | bytes 3670016 | tf_op jit(solution)/shard_map/pallas_call | solution.py:41
  59.6 3.5 %all-to-all-start.1 = ((bf16[4,128,1280]{2,1,0:T(8,128)(2,1)}), bf16[4,128,1280]{2,1,0:T(8,128)(2,1)S(1)}, u32[]{:S(2)}, u32[]{:S(2)}) async-start(bf16[4,128,1280]{2,1,0:T(8,128)(2,1)} %bitcast.8), calls=%async_computation.1 | async-start | bytes 2621440 | tf_op jit(solution)/shard_map/all_to_all | solution.py:187
  63.1 3.9 %collective-permute-start.3 = (bf16[512,640]{1,0:T(8,128)(2,1)}, bf16[512,640]{1,0:T(8,128)(2,1)}, u32[]{:S(2)}, u32[]{:S(2)}) collective-permute-start(bf16[512,640]{1,0:T(8,128)(2,1)} %copy-done.1), channel_id=1, source_target_pairs={{0,256},{256,512},{512,768},{768,0},{1,257},{257,513},{513,769},{7... | collective-permute-start | bytes 1966088 | tf_op jit(solution)/shard_map/ppermute | solution.py:195
  67.0 15.4 %all-to-all-done.1.got = bf16[4,128,1280]{2,1,0:T(8,128)(2,1)S(1)} async-done(((bf16[4,128,1280]{2,1,0:T(8,128)(2,1)}), bf16[4,128,1280]{2,1,0:T(8,128)(2,1)S(1)}, u32[]{:S(2)}, u32[]{:S(2)}) %all-to-all-start.1) | async-done | bytes 1310752 | tf_op jit(solution)/shard_map/all_to_all | solution.py:187
  82.4 0.4 shard_map.97
  82.8 12.6 %collective-permute-done.3.far = bf16[512,640]{1,0:T(8,128)(2,1)} collective-permute-done((bf16[512,640]{1,0:T(8,128)(2,1)}, bf16[512,640]{1,0:T(8,128)(2,1)}, u32[]{:S(2)}, u32[]{:S(2)}) %collective-permute-start.3) | collective-permute-done | bytes 655392 | tf_op jit(solution)/shard_map/ppermute | solution.py:195
  95.4 2.3 %shard_map.98 = (f32[128,1024]{1,0:T(8,128)S(1)}, bf16[128,1024]{1,0:T(8,128)(2,1)S(1)}) custom-call(s32[1]{0:T(128)} %bitcast.place, bf16[128,640]{1,0:T(8,128)(2,1)S(1)} %get-tuple-element.14.dh, bf16[512,640]{1,0:T(8,128)(2,1)S(1)} %bitcast.18, bf16[512,640]{1,0:T(8,128)(2,1)S(1)} %copy-done.2, bf16[512,640]{1,0:T(8,128)(2,1)S(1)} %copy-done.4, ...), custom_call_target="tpu_custom_call" | custom-call | bytes 3571712 | tf_op jit(solution)/shard_map/pallas_call | solution.py:41
  97.7 1.9 %collective-permute-start.4 = (bf16[128,1024]{1,0:T(8,128)(2,1)S(1)}, bf16[128,1024]{1,0:T(8,128)(2,1)S(1)}, u32[]{:S(2)}, u32[]{:S(2)}) collective-permute-start(bf16[128,1024]{1,0:T(8,128)(2,1)S(1)} %get-tuple-element.16), channel_id=1, source_target_pairs={{0,1},{1,0},{2,3},{3,2},{4,5},{5,4},{6,7},{7,6},{8,9},{9,8},{10,11... | collective-permute-start | bytes 786440 | tf_op jit(solution)/shard_map/ppermute | solution.py:191
  99.7 1.5 collective-permute-done.4.got
  101.2 0.7 shard_map.99
  101.9 22.9 %all-to-all-start.2 = ((bf16[32,16,256]{2,1,0:T(8,128)(2,1)}), bf16[32,16,256]{2,1,0:T(8,128)(2,1)S(1)}, u32[]{:S(2)}, u32[]{:S(2)}) async-start(bf16[32,16,256]{2,1,0:T(8,128)(2,1)} %bitcast.9), calls=%async_computation.2 | async-start | bytes 524288 | tf_op jit(solution)/shard_map/all_to_all | solution.py:187
  124.9 13.9 %all_gather.6.dh = bf16[512,640]{1,0:T(8,128)(2,1)S(1)} all-gather(bf16[128,640]{1,0:T(8,128)(2,1)S(1)} %get-tuple-element.14.dh), channel_id=1, replica_groups=mesh['y'=4,'x'=4,'l'=8,'h'=4,'c'=2] {'y'}, dimensions={0}, use_global_device_ids=true | all-gather | bytes 819200 | tf_op jit(solution)/shard_map/all_gather | solution.py:248
  138.7 13.0 %all_gather.7.act = bf16[512,640]{1,0:T(8,128)(2,1)S(1)} all-gather(bf16[128,640]{1,0:T(8,128)(2,1)S(1)} %get-tuple-element.17), channel_id=1, replica_groups=mesh['y'=4,'x'=4,'l'=8,'h'=4,'c'=2] {'y'}, dimensions={0}, use_global_device_ids=true | all-gather | bytes 819200 | tf_op jit(solution)/shard_map/all_gather | solution.py:248
  151.8 1.9 %shard_map.100 = (bf16[512,640]{1,0:T(8,128)(2,1)}, bf16[640,512]{1,0:T(8,128)(2,1)}, f32[8,128]{1,0:T(8,128)S(1)}) custom-call(s32[1]{0:T(128)} %bitcast.place, bf16[2,512,256]{2,1,0:T(8,128)(2,1)S(1)} %shard_map.95.own, bf16[2,512,256]{2,1,0:T(8,128)(2,1)S(1)} %collective-permute-done.2.other, bf16[512,640]{1,0:T(8,128)(2,1)S(1)} %all_gather.6.dh, ...), custom_call_target="tpu_custom_call" | custom-call | bytes 3674112 | tf_op jit(solution)/shard_map/pallas_call | solution.py:41
  153.6 6.4 %all-to-all-done.2 = bf16[32,16,256]{2,1,0:T(8,128)(2,1)S(1)} async-done(((bf16[32,16,256]{2,1,0:T(8,128)(2,1)}), bf16[32,16,256]{2,1,0:T(8,128)(2,1)S(1)}, u32[]{:S(2)}, u32[]{:S(2)}) %all-to-all-start.2) | async-done | bytes 262176 | tf_op jit(solution)/shard_map/all_to_all | solution.py:187
  160.1 0.2 shard_map.101
  160.2 8.0 %all_to_all.20 = bf16[4,32,256]{2,1,0:T(8,128)(2,1)S(1)} all-to-all(bf16[4,32,256]{2,1,0:T(8,128)(2,1)S(1)} %bitcast.23), channel_id=1, replica_groups=mesh['y'=4,'x'=4,'l'=8,'h'=4,'c'=2] {'x'}, dimensions={0} | all-to-all | bytes 131072 | tf_op jit(solution)/shard_map/all_to_all | solution.py:187
  168.2 0.8 shard_map.102
  (14 shorter events, 0.0 us)
Async XLA Ops:
  3.3 54.2 %copy-start = (bf16[1,512,640]{2,1,0:T(8,128)(2,1)S(1)}, bf16[1,512,640]{2,1,0:T(8,128)(2,1)}, u32[]{:S(2)}) copy-start(bf16[1,512,640]{2,1,0:T(8,128)(2,1)} %param.12) | copy-start | bytes 1966084
  3.3 54.2 %copy-start.5 = (bf16[1,640,512]{2,1,0:T(8,128)(2,1)S(1)}, bf16[1,640,512]{2,1,0:T(8,128)(2,1)}, u32[]{:S(2)}) copy-start(bf16[1,640,512]{2,1,0:T(8,128)(2,1)} %param.13) | copy-start | bytes 1966084
  3.3 50.1 %all-to-all-start = ((bf16[128,8,256]{2,1,0:T(8,128)(2,1)}), bf16[128,8,256]{2,1,0:T(8,128)(2,1)S(1)}, u32[]{:S(2)}, u32[]{:S(2)}) async-start(bf16[128,8,256]{2,1,0:T(8,128)(2,1)} %bitcast.28), calls=%async_computation | async-start | bytes 1048576 | tf_op jit(solution)/shard_map/all_to_all | solution.py:187
  22.5 23.5 %collective-permute-start = (bf16[512,640]{1,0:T(8,128)(2,1)}, bf16[512,640]{1,0:T(8,128)(2,1)S(1)}, u32[]{:S(2)}, u32[]{:S(2)}) collective-permute-start(bf16[512,640]{1,0:T(8,128)(2,1)} %get-tuple-element.13), channel_id=1, source_target_pairs={{0,256},{256,512},{512,768},{768,0},{1,257},{257,513},{513,769},{7... | collective-permute-start | bytes 1966088 | tf_op jit(solution)/shard_map/ppermute | solution.py:195
  26.0 21.0 %collective-permute-start.1 = (bf16[512,640]{1,0:T(8,128)(2,1)}, bf16[512,640]{1,0:T(8,128)(2,1)S(1)}, u32[]{:S(2)}, u32[]{:S(2)}) collective-permute-start(bf16[512,640]{1,0:T(8,128)(2,1)} %get-tuple-element.13), channel_id=1, source_target_pairs={{0,768},{256,0},{512,256},{768,512},{1,769},{257,1},{513,257},{769... | collective-permute-start | bytes 1966088 | tf_op jit(solution)/shard_map/ppermute | solution.py:195
  46.0 0.9 copy-start.1
  47.0 0.8 copy-start.3
  53.7 3.8 %collective-permute-start.2 = (bf16[2,512,256]{2,1,0:T(8,128)(2,1)S(1)}, bf16[2,512,256]{2,1,0:T(8,128)(2,1)S(1)}, u32[]{:S(2)}, u32[]{:S(2)}) collective-permute-start(bf16[2,512,256]{2,1,0:T(8,128)(2,1)S(1)} %shard_map.95.own), channel_id=1, source_target_pairs={{0,1},{1,0},{2,3},{3,2},{4,5},{5,4},{6,7},{7,6},{8,9},{9,8},{10,11... | collective-permute-start | bytes 1572872 | tf_op jit(solution)/shard_map/ppermute | solution.py:191
  59.6 22.8 %all-to-all-start.1 = ((bf16[4,128,1280]{2,1,0:T(8,128)(2,1)}), bf16[4,128,1280]{2,1,0:T(8,128)(2,1)S(1)}, u32[]{:S(2)}, u32[]{:S(2)}) async-start(bf16[4,128,1280]{2,1,0:T(8,128)(2,1)} %bitcast.8), calls=%async_computation.1 | async-start | bytes 2621440 | tf_op jit(solution)/shard_map/all_to_all | solution.py:187
  63.1 32.3 %collective-permute-start.3 = (bf16[512,640]{1,0:T(8,128)(2,1)}, bf16[512,640]{1,0:T(8,128)(2,1)}, u32[]{:S(2)}, u32[]{:S(2)}) collective-permute-start(bf16[512,640]{1,0:T(8,128)(2,1)} %copy-done.1), channel_id=1, source_target_pairs={{0,256},{256,512},{512,768},{768,0},{1,257},{257,513},{513,769},{7... | collective-permute-start | bytes 1966088 | tf_op jit(solution)/shard_map/ppermute | solution.py:195
  82.4 13.0 %copy-start.2 = (bf16[512,640]{1,0:T(8,128)(2,1)S(1)}, bf16[512,640]{1,0:T(8,128)(2,1)}, u32[]{:S(2)}) copy-start(bf16[512,640]{1,0:T(8,128)(2,1)} %copy-done.1) | copy-start | bytes 1966084
  82.4 13.0 %copy-start.4 = (bf16[512,640]{1,0:T(8,128)(2,1)S(1)}, bf16[512,640]{1,0:T(8,128)(2,1)}, u32[]{:S(2)}) copy-start(bf16[512,640]{1,0:T(8,128)(2,1)} %copy-done.3) | copy-start | bytes 1966084
  97.7 3.4 %collective-permute-start.4 = (bf16[128,1024]{1,0:T(8,128)(2,1)S(1)}, bf16[128,1024]{1,0:T(8,128)(2,1)S(1)}, u32[]{:S(2)}, u32[]{:S(2)}) collective-permute-start(bf16[128,1024]{1,0:T(8,128)(2,1)S(1)} %get-tuple-element.16), channel_id=1, source_target_pairs={{0,1},{1,0},{2,3},{3,2},{4,5},{5,4},{6,7},{7,6},{8,9},{9,8},{10,11... | collective-permute-start | bytes 786440 | tf_op jit(solution)/shard_map/ppermute | solution.py:191
  101.9 58.2 %all-to-all-start.2 = ((bf16[32,16,256]{2,1,0:T(8,128)(2,1)}), bf16[32,16,256]{2,1,0:T(8,128)(2,1)S(1)}, u32[]{:S(2)}, u32[]{:S(2)}) async-start(bf16[32,16,256]{2,1,0:T(8,128)(2,1)} %bitcast.9), calls=%async_computation.2 | async-start | bytes 524288 | tf_op jit(solution)/shard_map/all_to_all | solution.py:187
  151.8 16.5 %copy-start.6 = (s32[128]{0:T(128)S(1)}, s32[128]{0:T(128)}, u32[]{:S(2)}) copy-start(s32[128]{0:T(128)} %param.10) | copy-start | bytes 1540
  151.8 16.5 %copy-start.7 = (s32[128]{0:T(128)S(1)}, s32[128]{0:T(128)}, u32[]{:S(2)}) copy-start(s32[128]{0:T(128)} %param.11) | copy-start | bytes 1540

commit v8 on v6

--- a/solution.py
+++ b/solution.py
@@ -92,7 +92,7 @@
     copies[-1].wait()
 
 
-def regroup_kernel(place, got, _, __, out):
+def regroup_kernel(place, got, _, __, ___, out):
     rows, xs = out.shape[1] // 4, 4
     count = 2 * rows
     n = lax.broadcasted_iota(jnp.int32, (count, count), 0)
@@ -114,16 +114,17 @@
 
 def parts_kernel(place, own, other, w_in, w_out, _, out):
     hid = w_in.shape[1]
-    (in_own, in_other), (out_own, out_other) = halves(place, w_in, 0), halves(place, w_out, 1)
+    in_own, in_other = halves(place, w_in, 0)
     out[:, :hid] = (
         dot(own[0], in_own, ((1,), (0,))) + dot(other[0], in_other, ((1,), (0,)))
     ).astype(bf16)
+    out_own, out_other = halves(place, w_out, 1)
     out[:, hid:] = (
         dot(own[1], out_own, ((1,), (1,))) + dot(other[1], out_other, ((1,), (1,)))
     ).astype(bf16)
 
 
-def gelu_kernel(place, got, dh, act):
+def back_kernel(place, got, own, left, right, far, mine, theirs, dh, act, w):
     hid = dh.shape[1]
     total = got[0].astype(f32)
     for q in range(1, got.shape[0]):
@@ -131,9 +132,6 @@
     gelu_value, gelu_slope = gelu_pair(total[:, :hid])
     dh[...] = (total[:, hid:] * gelu_slope).astype(bf16)
     act[...] = gelu_value.astype(bf16)
-
-
-def back_kernel(place, dh, own, left, right, far, mine, theirs, w):
     y, c = place[0] >> 1, core(place)
     hs = 4
     f = own.shape[0] // (2 * hs)
@@ -226,18 +224,24 @@
     got = exchange(sent.reshape(groups, 8, part), ("y", "x", "l")).reshape(groups * 8, part)
     left, right = over_y(w_pass, 1), over_y(w_pass, -1)
     far = over_y(right, -1)
-    arrived = tuple(a[:16, :128] for a in (left, right))
+    arrived = tuple(a[:16, :128] for a in (left, right)) + (w_out,)
     (own,) = call(regroup_kernel, [((2, rows, part), bf16)], got, after=arrived)
     other = other_core(own)
     (parts,) = call(
-        parts_kernel, [((rows, 2 * hid), bf16)], own, other, w_in, w_out, after=(far[:16, :128],)
+        parts_kernel,
+        [((rows, 2 * hid), bf16)],
+        own,
+        other,
+        w_in,
+        w_out,
+        after=(far,),
     )
     got = exchange(parts.reshape(ys, chunk, 2 * hid), "y")
-    dh, act = call(gelu_kernel, [((chunk, hid), bf16)] * 2, got)
-    mine, theirs = call(
+    block = ((chunk, hid), bf16)
+    mine, theirs, dh, act = call(
         back_kernel,
-        [((chunk, ys * part), f32), ((chunk, ys * part), bf16)],
-        dh,
+        [((chunk, ys * part), f32), ((chunk, ys * part), bf16), block, block],
+        got,
         w_in,
         left,
         right,

time: 163 us -> 161 us (0.988)
    pallas_call x9 -> x8, Pallas kernels: 10.2 us -> 10.1 us  [call(): pl.pallas_call(kernel, out_shape=[jax.ShapeDtypeStruct(s, d) for s, d in...]
where the time goes in v8:
time: 161 us
  starting transfers between devices  58.5 us (36%)
  blocking collectives  57.1 us (35%)
  waiting for transfers between devices  32.8 us (20%)
  Pallas kernels  10.1 us (6%)
    all_to_all x2, starting transfers between devices, exchange(): return lax.all_to_all(x, axes, split_axis=0, concat_axis=0, tiled=True)  42 us
    all_to_all x2, blocking collectives, exchange(): return lax.all_to_all(x, axes, split_axis=0, concat_axis=0, tiled=True)  30.4 us
    all_gather x2, blocking collectives, local(): dh, act = (lax.all_gather(a, 'y', axis=0, tiled=True) for a in (dh, act))  26.7 us
    ppermute x3, waiting for transfers between devices, over_y(): return lax.ppermute(x, 'y', [(y, (y + step) % 4) for y in range(4)])  23.2 us
    ppermute x3, starting transfers between devices, over_y(): return lax.ppermute(x, 'y', [(y, (y + step) % 4) for y in range(4)])  12.6 us
    pallas_call x8, Pallas kernels, call(): pl.pallas_call(kernel, out_shape=[jax.ShapeDtypeStruct(s, d) for s, d in...  10.1 us
    all_to_all x2, waiting for transfers between devices, exchange(): return lax.all_to_all(x, axes, split_axis=0, concat_axis=0, tiled=True)  8.11 us
    ppermute x2, starting transfers between devices, other_core(): return lax.ppermute(x, 'c', [(0, 1), (1, 0)])  3.84 us
  transfers between devices with their start and end apart: 7, of which 5 were waited for; matrix products, arithmetic and copies ran while one was open for 0% of the time, Pallas kernels for 1%

profile of v8, /device:TPU:32, one launch (start us, length us, event | category | flops | bytes accessed | tf_op | source)
XLA Modules:
  0.0 160.9 jit_solution(3282065392403689425)
XLA Ops:
  0.6 0.0 copy-start.1
  0.6 2.7 %shard_map.94 = (bf16[1024,256]{1,0:T(8,128)(2,1)}, bf16[512,640]{1,0:T(8,128)(2,1)}) custom-call(s32[1]{0:T(128)} %bitcast.place, s32[1,128]{1,0:T(1,128)} %bitcast.26, s32[1,128]{1,0:T(1,128)} %bitcast.28, f32[1,128]{1,0:T(1,128)} %bitcast.32, bf16[128,2048]{1,0:T(8,128)(2,1)} %tok.1, bf16[128,2048]{1,0:T(8,128)(2,1)} %cot.1, bf16[512,640]{1,0:T(8,128)(2,1)} %bitcast.16), custom_call_target="tpu_custom_call" | custom-call | bytes 2885120 | tf_op jit(solution)/shard_map/pallas_call | solution.py:41
  3.4 0.0 copy-start
  3.4 19.2 %all-to-all-start = ((bf16[128,8,256]{2,1,0:T(8,128)(2,1)}), bf16[128,8,256]{2,1,0:T(8,128)(2,1)S(1)}, u32[]{:S(2)}, u32[]{:S(2)}) async-start(bf16[128,8,256]{2,1,0:T(8,128)(2,1)} %bitcast.30), calls=%async_computation | async-start | bytes 1048576 | tf_op jit(solution)/shard_map/all_to_all | solution.py:185
  22.6 5.1 %collective-permute-start.1 = (bf16[512,640]{1,0:T(8,128)(2,1)}, bf16[512,640]{1,0:T(8,128)(2,1)}, u32[]{:S(2)}, u32[]{:S(2)}) collective-permute-start(bf16[512,640]{1,0:T(8,128)(2,1)} %get-tuple-element.13), channel_id=1, source_target_pairs={{0,768},{256,0},{512,256},{768,512},{1,769},{257,1},{513,257},{769... | collective-permute-start | bytes 1966088 | tf_op jit(solution)/shard_map/ppermute | solution.py:193
  27.7 1.9 %collective-permute-start = (bf16[512,640]{1,0:T(8,128)(2,1)}, bf16[512,640]{1,0:T(8,128)(2,1)S(1)}, u32[]{:S(2)}, u32[]{:S(2)}) collective-permute-start(bf16[512,640]{1,0:T(8,128)(2,1)} %get-tuple-element.13), channel_id=1, source_target_pairs={{0,256},{256,512},{512,768},{768,0},{1,257},{257,513},{513,769},{7... | collective-permute-start | bytes 1966088 | tf_op jit(solution)/shard_map/ppermute | solution.py:193
  29.7 15.1 %collective-permute-done.1.right = bf16[512,640]{1,0:T(8,128)(2,1)} collective-permute-done((bf16[512,640]{1,0:T(8,128)(2,1)}, bf16[512,640]{1,0:T(8,128)(2,1)}, u32[]{:S(2)}, u32[]{:S(2)}) %collective-permute-start.1) | collective-permute-done | bytes 655392 | tf_op jit(solution)/shard_map/ppermute | solution.py:193
  44.8 5.6 %collective-permute-start.3 = (bf16[512,640]{1,0:T(8,128)(2,1)}, bf16[512,640]{1,0:T(8,128)(2,1)S(1)}, u32[]{:S(2)}, u32[]{:S(2)}) collective-permute-start(bf16[512,640]{1,0:T(8,128)(2,1)} %collective-permute-done.1.right), channel_id=1, source_target_pairs={{0,768},{256,0},{512,256},{768,512},{1,769},{257,1},{513,257},{769... | collective-permute-start | bytes 1966088 | tf_op jit(solution)/shard_map/ppermute | solution.py:193
  50.4 0.7 slice.9.__
  51.1 0.0 collective-permute-done.left
  51.1 0.8 copy-done.2
  52.0 1.5 all-to-all-done
  53.5 0.3 shard_map.95.own
  53.8 1.9 %collective-permute-start.2 = (bf16[2,512,256]{2,1,0:T(8,128)(2,1)S(1)}, bf16[2,512,256]{2,1,0:T(8,128)(2,1)S(1)}, u32[]{:S(2)}, u32[]{:S(2)}) collective-permute-start(bf16[2,512,256]{2,1,0:T(8,128)(2,1)S(1)} %shard_map.95.own), channel_id=1, source_target_pairs={{0,1},{1,0},{2,3},{3,2},{4,5},{5,4},{6,7},{7,6},{8,9},{9,8},{10,11... | collective-permute-start | bytes 1572872 | tf_op jit(solution)/shard_map/ppermute | solution.py:189
  55.7 8.0 %collective-permute-done.3._.far = bf16[512,640]{1,0:T(8,128)(2,1)S(1)} collective-permute-done((bf16[512,640]{1,0:T(8,128)(2,1)}, bf16[512,640]{1,0:T(8,128)(2,1)S(1)}, u32[]{:S(2)}, u32[]{:S(2)}) %collective-permute-start.3) | collective-permute-done | bytes 655392 | tf_op jit(solution)/shard_map/ppermute | solution.py:193
  63.7 0.0 collective-permute-done.2.other
  63.7 1.0 shard_map.96
  64.7 0.0 copy-start.3
  64.7 20.8 %all_to_all.20.got = bf16[4,128,1280]{2,1,0:T(8,128)(2,1)S(1)} all-to-all(bf16[4,128,1280]{2,1,0:T(8,128)(2,1)S(1)} %bitcast.19), channel_id=1, replica_groups=mesh['y'=4,'x'=4,'l'=8,'h'=4,'c'=2] {'y'}, dimensions={0} | all-to-all | bytes 2621440 | tf_op jit(solution)/shard_map/all_to_all | solution.py:185
  85.5 0.0 copy-done.3
  85.5 2.5 %shard_map.97 = (f32[128,1024]{1,0:T(8,128)S(1)}, bf16[128,1024]{1,0:T(8,128)(2,1)S(1)}, bf16[128,640]{1,0:T(8,128)(2,1)S(1)}, bf16[128,640]{1,0:T(8,128)(2,1)S(1)}) custom-call(s32[1]{0:T(128)} %bitcast.place, bf16[4,128,1280]{2,1,0:T(8,128)(2,1)S(1)} %all_to_all.20.got, bf16[512,640]{1,0:T(8,128)(2,1)S(1)} %bitcast.18, bf16[512,640]{1,0:T(8,128)(2,1)S(1)} %copy-done.3, ...), custom_call_target="tpu_custom_call" | custom-call | bytes 5046272 | tf_op jit(solution)/shard_map/pallas_call | solution.py:41
  88.0 1.9 %collective-permute-start.4 = (bf16[128,1024]{1,0:T(8,128)(2,1)S(1)}, bf16[128,1024]{1,0:T(8,128)(2,1)S(1)}, u32[]{:S(2)}, u32[]{:S(2)}) collective-permute-start(bf16[128,1024]{1,0:T(8,128)(2,1)S(1)} %get-tuple-element.15), channel_id=1, source_target_pairs={{0,1},{1,0},{2,3},{3,2},{4,5},{5,4},{6,7},{7,6},{8,9},{9,8},{10,11... | collective-permute-start | bytes 786440 | tf_op jit(solution)/shard_map/ppermute | solution.py:189
  90.0 1.5 collective-permute-done.4.got
  91.5 0.7 shard_map.98
  92.2 22.8 %all-to-all-start.2 = ((bf16[32,16,256]{2,1,0:T(8,128)(2,1)}), bf16[32,16,256]{2,1,0:T(8,128)(2,1)S(1)}, u32[]{:S(2)}, u32[]{:S(2)}) async-start(bf16[32,16,256]{2,1,0:T(8,128)(2,1)} %bitcast.9), calls=%async_computation.2 | async-start | bytes 524288 | tf_op jit(solution)/shard_map/all_to_all | solution.py:185
  115.0 13.7 %all_gather.6.dh = bf16[512,640]{1,0:T(8,128)(2,1)S(1)} all-gather(bf16[128,640]{1,0:T(8,128)(2,1)S(1)} %get-tuple-element.16), channel_id=1, replica_groups=mesh['y'=4,'x'=4,'l'=8,'h'=4,'c'=2] {'y'}, dimensions={0}, use_global_device_ids=true | all-gather | bytes 819200 | tf_op jit(solution)/shard_map/all_gather | solution.py:254
  128.7 13.0 %all_gather.7.act = bf16[512,640]{1,0:T(8,128)(2,1)S(1)} all-gather(bf16[128,640]{1,0:T(8,128)(2,1)S(1)} %get-tuple-element.17), channel_id=1, replica_groups=mesh['y'=4,'x'=4,'l'=8,'h'=4,'c'=2] {'y'}, dimensions={0}, use_global_device_ids=true | all-gather | bytes 819200 | tf_op jit(solution)/shard_map/all_gather | solution.py:254
  141.8 1.9 %shard_map.99 = (bf16[512,640]{1,0:T(8,128)(2,1)}, bf16[640,512]{1,0:T(8,128)(2,1)}, f32[8,128]{1,0:T(8,128)S(1)}) custom-call(s32[1]{0:T(128)} %bitcast.place, bf16[2,512,256]{2,1,0:T(8,128)(2,1)S(1)} %shard_map.95.own, bf16[2,512,256]{2,1,0:T(8,128)(2,1)S(1)} %collective-permute-done.2.other, bf16[512,640]{1,0:T(8,128)(2,1)S(1)} %all_gather.6.dh, ...), custom_call_target="tpu_custom_call" | custom-call | bytes 3674112 | tf_op jit(solution)/shard_map/pallas_call | solution.py:41
  143.6 6.6 %all-to-all-done.2 = bf16[32,16,256]{2,1,0:T(8,128)(2,1)S(1)} async-done(((bf16[32,16,256]{2,1,0:T(8,128)(2,1)}), bf16[32,16,256]{2,1,0:T(8,128)(2,1)S(1)}, u32[]{:S(2)}, u32[]{:S(2)}) %all-to-all-start.2) | async-done | bytes 262176 | tf_op jit(solution)/shard_map/all_to_all | solution.py:185
  150.2 0.2 shard_map.100
  150.4 9.6 %all_to_all.21 = bf16[4,32,256]{2,1,0:T(8,128)(2,1)S(1)} all-to-all(bf16[4,32,256]{2,1,0:T(8,128)(2,1)S(1)} %bitcast.25), channel_id=1, replica_groups=mesh['y'=4,'x'=4,'l'=8,'h'=4,'c'=2] {'x'}, dimensions={0} | all-to-all | bytes 131072 | tf_op jit(solution)/shard_map/all_to_all | solution.py:185
  160.1 0.8 shard_map.101
  (8 shorter events, 0.0 us)
Async XLA Ops:
  0.6 52.8 %copy-start.1 = (bf16[1,640,512]{2,1,0:T(8,128)(2,1)S(1)}, bf16[1,640,512]{2,1,0:T(8,128)(2,1)}, u32[]{:S(2)}) copy-start(bf16[1,640,512]{2,1,0:T(8,128)(2,1)} %param.13) | copy-start | bytes 1966084
  3.4 60.4 %copy-start = (bf16[1,512,640]{2,1,0:T(8,128)(2,1)S(1)}, bf16[1,512,640]{2,1,0:T(8,128)(2,1)}, u32[]{:S(2)}) copy-start(bf16[1,512,640]{2,1,0:T(8,128)(2,1)} %param.12) | copy-start | bytes 1966084
  3.4 50.1 %all-to-all-start = ((bf16[128,8,256]{2,1,0:T(8,128)(2,1)}), bf16[128,8,256]{2,1,0:T(8,128)(2,1)S(1)}, u32[]{:S(2)}, u32[]{:S(2)}) async-start(bf16[128,8,256]{2,1,0:T(8,128)(2,1)} %bitcast.30), calls=%async_computation | async-start | bytes 1048576 | tf_op jit(solution)/shard_map/all_to_all | solution.py:185
  22.6 22.2 %collective-permute-start.1 = (bf16[512,640]{1,0:T(8,128)(2,1)}, bf16[512,640]{1,0:T(8,128)(2,1)}, u32[]{:S(2)}, u32[]{:S(2)}) collective-permute-start(bf16[512,640]{1,0:T(8,128)(2,1)} %get-tuple-element.13), channel_id=1, source_target_pairs={{0,768},{256,0},{512,256},{768,512},{1,769},{257,1},{513,257},{769... | collective-permute-start | bytes 1966088 | tf_op jit(solution)/shard_map/ppermute | solution.py:193
  27.7 23.4 %collective-permute-start = (bf16[512,640]{1,0:T(8,128)(2,1)}, bf16[512,640]{1,0:T(8,128)(2,1)S(1)}, u32[]{:S(2)}, u32[]{:S(2)}) collective-permute-start(bf16[512,640]{1,0:T(8,128)(2,1)} %get-tuple-element.13), channel_id=1, source_target_pairs={{0,256},{256,512},{512,768},{768,0},{1,257},{257,513},{513,769},{7... | collective-permute-start | bytes 1966088 | tf_op jit(solution)/shard_map/ppermute | solution.py:193
  44.8 18.9 %collective-permute-start.3 = (bf16[512,640]{1,0:T(8,128)(2,1)}, bf16[512,640]{1,0:T(8,128)(2,1)S(1)}, u32[]{:S(2)}, u32[]{:S(2)}) collective-permute-start(bf16[512,640]{1,0:T(8,128)(2,1)} %collective-permute-done.1.right), channel_id=1, source_target_pairs={{0,768},{256,0},{512,256},{768,512},{1,769},{257,1},{513,257},{769... | collective-permute-start | bytes 1966088 | tf_op jit(solution)/shard_map/ppermute | solution.py:193
  51.1 0.8 copy-start.2
  53.8 10.0 %collective-permute-start.2 = (bf16[2,512,256]{2,1,0:T(8,128)(2,1)S(1)}, bf16[2,512,256]{2,1,0:T(8,128)(2,1)S(1)}, u32[]{:S(2)}, u32[]{:S(2)}) collective-permute-start(bf16[2,512,256]{2,1,0:T(8,128)(2,1)S(1)} %shard_map.95.own), channel_id=1, source_target_pairs={{0,1},{1,0},{2,3},{3,2},{4,5},{5,4},{6,7},{7,6},{8,9},{9,8},{10,11... | collective-permute-start | bytes 1572872 | tf_op jit(solution)/shard_map/ppermute | solution.py:189
  64.7 20.8 %copy-start.3 = (bf16[512,640]{1,0:T(8,128)(2,1)S(1)}, bf16[512,640]{1,0:T(8,128)(2,1)}, u32[]{:S(2)}) copy-start(bf16[512,640]{1,0:T(8,128)(2,1)} %copy-done.2) | copy-start | bytes 1966084
  88.0 3.4 %collective-permute-start.4 = (bf16[128,1024]{1,0:T(8,128)(2,1)S(1)}, bf16[128,1024]{1,0:T(8,128)(2,1)S(1)}, u32[]{:S(2)}, u32[]{:S(2)}) collective-permute-start(bf16[128,1024]{1,0:T(8,128)(2,1)S(1)} %get-tuple-element.15), channel_id=1, source_target_pairs={{0,1},{1,0},{2,3},{3,2},{4,5},{5,4},{6,7},{7,6},{8,9},{9,8},{10,11... | collective-permute-start | bytes 786440 | tf_op jit(solution)/shard_map/ppermute | solution.py:189
  92.2 58.0 %all-to-all-start.2 = ((bf16[32,16,256]{2,1,0:T(8,128)(2,1)}), bf16[32,16,256]{2,1,0:T(8,128)(2,1)S(1)}, u32[]{:S(2)}, u32[]{:S(2)}) async-start(bf16[32,16,256]{2,1,0:T(8,128)(2,1)} %bitcast.9), calls=%async_computation.2 | async-start | bytes 524288 | tf_op jit(solution)/shard_map/all_to_all | solution.py:185
  141.8 18.3 %copy-start.4 = (s32[128]{0:T(128)S(1)}, s32[128]{0:T(128)}, u32[]{:S(2)}) copy-start(s32[128]{0:T(128)} %param.10) | copy-start | bytes 1540
  141.8 18.3 %copy-start.5 = (s32[128]{0:T(128)S(1)}, s32[128]{0:T(128)}, u32[]{:S(2)}) copy-start(s32[128]{0:T(128)} %param.11) | copy-start | bytes 1540

commit v9 on v8

--- a/solution.py
+++ b/solution.py
@@ -60,7 +60,7 @@
 
 
 def dispatch_kernel(
-    place, eid, slot, gate, tok, cot, w_in, out, w_pass, eid_v, slot_v, gate_v, tok_v, cot_v, sems
+    place, eid, slot, gate, tok, cot, w_in, out, w_low, w_high, eid_v, slot_v, gate_v, tok_v, cot_v, sems
 ):
     quarters, toks, feats = tok_v.shape
     count = out.shape[0] // quarters
@@ -72,7 +72,10 @@
         for q in range(quarters):
             cols = pl.ds(pl.multiple_of((2 * q + core(place)) * feats, feats), feats)
             copies.append(pltpu.make_async_copy(src.at[:, cols], dst.at[q], sems.at[len(copies)]))
-    copies.append(pltpu.make_async_copy(w_in, w_pass, sems.at[len(copies)]))
+    half = w_in.shape[0] // 2
+    for i, dst in enumerate((w_low, w_high)):
+        src = w_in.at[i * half : (i + 1) * half]
+        copies.append(pltpu.make_async_copy(src, dst, sems.at[len(copies)]))
     for copy in copies:
         copy.start()
     for copy in copies[:3]:
@@ -83,16 +86,18 @@
     take_x = as_bf16(hit & is_x)
     take_dy = as_bf16(hit & ~is_x)
     row_gate = jnp.sum(jnp.where(hit, gate_v[...], 0.0), axis=1, keepdims=True)
-    for copy in copies[3:-1]:
+    for copy in copies[3:-2]:
         copy.wait()
     for q in range(quarters):
         got_x = dot(take_x, tok_v[q], ((1,), (0,)))
         got_dy = row_gate * dot(take_dy, cot_v[q], ((1,), (0,)))
         out[q * count : (q + 1) * count] = (got_x + got_dy).astype(bf16)
-    copies[-1].wait()
-
-
-def regroup_kernel(place, got, _, __, ___, out):
+    for copy in copies[-2:]:
+        copy.wait()
+
+
+def regroup_kernel(place, got, *refs):
+    out = refs[-1]
     rows, xs = out.shape[1] // 4, 4
     count = 2 * rows
     n = lax.broadcasted_iota(jnp.int32, (count, count), 0)
@@ -112,7 +117,7 @@
         yield ref[part, :] if axis == 0 else ref[:, part]
 
 
-def parts_kernel(place, own, other, w_in, w_out, _, out):
+def parts_kernel(place, own, other, w_in, w_out, out):
     hid = w_in.shape[1]
     in_own, in_other = halves(place, w_in, 0)
     out[:, :hid] = (
@@ -124,7 +129,9 @@
     ).astype(bf16)
 
 
-def back_kernel(place, got, own, left, right, far, mine, theirs, dh, act, w):
+def back_kernel(
+    place, got, own, left_a, left_b, right_a, right_b, far_a, far_b, mine, theirs, dh, act, w
+):
     hid = dh.shape[1]
     total = got[0].astype(f32)
     for q in range(1, got.shape[0]):
@@ -136,9 +143,16 @@
     hs = 4
     f = own.shape[0] // (2 * hs)
     for out, at in ((theirs, 1 - c), (mine, c)):
-        for src, q in ((own, y), (left, (y + 3) & 3), (right, (y + 1) & 3), (far, (y + 2) & 3)):
+        for src, q in (
+            ((own, own), y),
+            ((left_a, left_b), (y + 3) & 3),
+            ((right_a, right_b), (y + 1) & 3),
+            ((far_a, far_b), (y + 2) & 3),
+        ):
             for h in range(hs):
-                rows = src[pl.ds(pl.multiple_of((h * 2 + at) * f, f), f), :]
+                ref = src[h // 2]
+                start = ((h if ref is own else h % 2) * 2 + at) * f
+                rows = ref[pl.ds(pl.multiple_of(start, f), f), :]
                 w[pl.ds(pl.multiple_of((h * 4 + q) * f, f), f), :] = rows
         out[...] = dot(dh[...], w[...], ((1,), (1,))).astype(out.dtype)
 
@@ -202,9 +216,9 @@
     groups = ys * xs * ls
     rows, part, f = groups * 4, width // 2, width // 8
     chunk = rows // ys
-    sent, w_pass = call(
+    sent, w_low, w_high = call(
         dispatch_kernel,
-        [((groups * 8, part), bf16), (w_in.shape, bf16)],
+        [((groups * 8, part), bf16)] + [((part, hid), bf16)] * 2,
         eid,
         slot,
         gate,
@@ -217,25 +231,19 @@
             pltpu.VMEM((1, toks), f32),
             pltpu.VMEM((ys, toks, part), bf16),
             pltpu.VMEM((ys, toks, part), bf16),
-            pltpu.SemaphoreType.DMA((4 + 2 * ys,)),
+            pltpu.SemaphoreType.DMA((5 + 2 * ys,)),
         ],
         fetch=True,
     )
     got = exchange(sent.reshape(groups, 8, part), ("y", "x", "l")).reshape(groups * 8, part)
-    left, right = over_y(w_pass, 1), over_y(w_pass, -1)
-    far = over_y(right, -1)
-    arrived = tuple(a[:16, :128] for a in (left, right)) + (w_out,)
+    right_low, left_high = over_y(w_low, -1), over_y(w_high, 1)
+    right_high, left_low = over_y(w_high, -1), over_y(w_low, 1)
+    far_low, far_high = over_y(right_low, -1), over_y(left_high, 1)
+    gathered = (left_low, left_high, right_low, right_high, far_low, far_high)
+    arrived = tuple(a[:16, :128] for a in (left_low, right_high, far_low, far_high)) + (w_out,)
     (own,) = call(regroup_kernel, [((2, rows, part), bf16)], got, after=arrived)
     other = other_core(own)
-    (parts,) = call(
-        parts_kernel,
-        [((rows, 2 * hid), bf16)],
-        own,
-        other,
-        w_in,
-        w_out,
-        after=(far,),
-    )
+    (parts,) = call(parts_kernel, [((rows, 2 * hid), bf16)], own, other, w_in, w_out)
     got = exchange(parts.reshape(ys, chunk, 2 * hid), "y")
     block = ((chunk, hid), bf16)
     mine, theirs, dh, act = call(
@@ -243,9 +251,7 @@
         [((chunk, ys * part), f32), ((chunk, ys * part), bf16), block, block],
         got,
         w_in,
-        left,
-        right,
-        far,
+        *gathered,
         scratch=[pltpu.VMEM((ys * part, hid), bf16)],
     )
     got = other_core(theirs)

time: 161 us -> 159 us (0.988)
  waiting for transfers between devices: 32.8 us -> 21.5 us
  starting transfers between devices: 58.5 us -> 67.1 us
    ppermute x3 -> x6, waiting for transfers between devices: 23.2 us -> 11.7 us  [over_y(): return lax.ppermute(x, 'y', [(y, (y + step) % 4) for y in range(4)])]
    ppermute x3 -> x6, starting transfers between devices: 12.6 us -> 21.2 us  [over_y(): return lax.ppermute(x, 'y', [(y, (y + step) % 4) for y in range(4)])]
    ppermute x2, waiting for transfers between devices: 1.5 us -> 3.38 us  [other_core(): return lax.ppermute(x, 'c', [(0, 1), (1, 0)])]
    all_to_all x2, waiting for transfers between devices: 8.11 us -> 6.47 us  [exchange(): return lax.all_to_all(x, axes, split_axis=0, concat_axis=0, tiled=True)]
  transfers between devices with their start and end apart: 7 -> 10, of which waited for: 5 -> 7; matrix products, arithmetic and copies ran while one was open for 0% -> 0% of each run, Pallas kernels for 1% -> 1%
where the time goes in v9:
time: 159 us; the launch traced here: 158 us
  starting transfers between devices  67.1 us (42%)
  blocking collectives  57.4 us (36%)
  waiting for transfers between devices  21.5 us (14%)
  Pallas kernels  9.03 us (6%)
  local copies, waits for them, and re-layouts  2.2 us (1%)
    all_to_all x2, starting transfers between devices, exchange(): return lax.all_to_all(x, axes, split_axis=0, concat_axis=0, tiled=True)  42 us
    all_to_all x2, blocking collectives, exchange(): return lax.all_to_all(x, axes, split_axis=0, concat_axis=0, tiled=True)  30.5 us
    all_gather x2, blocking collectives, local(): dh, act = (lax.all_gather(a, 'y', axis=0, tiled=True) for a in (dh, act))  26.9 us
    ppermute x6, starting transfers between devices, over_y(): return lax.ppermute(x, 'y', [(y, (y + step) % 4) for y in range(4)])  21.2 us
    ppermute x6, waiting for transfers between devices, over_y(): return lax.ppermute(x, 'y', [(y, (y + step) % 4) for y in range(4)])  11.7 us
    pallas_call x8, Pallas kernels, call(): pl.pallas_call(kernel, out_shape=[jax.ShapeDtypeStruct(s, d) for s, d in...  9.03 us
    all_to_all x2, waiting for transfers between devices, exchange(): return lax.all_to_all(x, axes, split_axis=0, concat_axis=0, tiled=True)  6.47 us
    ppermute x2, starting transfers between devices, other_core(): return lax.ppermute(x, 'c', [(0, 1), (1, 0)])  3.84 us
  transfers between devices with their start and end apart: 10, of which 7 were waited for; matrix products, arithmetic and copies ran while one was open for 0% of the time, Pallas kernels for 1%

profile of v9, /device:TPU:32, one launch (start us, length us, event | category | flops | bytes accessed | tf_op | source)
XLA Modules:
  0.0 158.1 jit_solution(14300527934246252232)
XLA Ops:
  0.6 2.7 %shard_map.94 = (bf16[1024,256]{1,0:T(8,128)(2,1)}, bf16[256,640]{1,0:T(8,128)(2,1)}, bf16[256,640]{1,0:T(8,128)(2,1)}) custom-call(s32[1]{0:T(128)} %bitcast.place, s32[1,128]{1,0:T(1,128)} %bitcast.26, s32[1,128]{1,0:T(1,128)} %bitcast.28, f32[1,128]{1,0:T(1,128)} %bitcast.32, bf16[128,2048]{1,0:T(8,128)(2,1)} %tok.1, bf16[128,2048]{1,0:T(8,128)(2,1)} %cot.1, ...), custom_call_target="tpu_custom_call" | custom-call | bytes 2885120 | tf_op jit(solution)/shard_map/pallas_call | solution.py:41
  3.4 19.2 %all-to-all-start = ((bf16[128,8,256]{2,1,0:T(8,128)(2,1)}), bf16[128,8,256]{2,1,0:T(8,128)(2,1)S(1)}, u32[]{:S(2)}, u32[]{:S(2)}) async-start(bf16[128,8,256]{2,1,0:T(8,128)(2,1)} %bitcast.30), calls=%async_computation | async-start | bytes 1048576 | tf_op jit(solution)/shard_map/all_to_all | solution.py:199
  22.6 5.1 %collective-permute-start.2 = (bf16[256,640]{1,0:T(8,128)(2,1)}, bf16[256,640]{1,0:T(8,128)(2,1)S(1)}, u32[]{:S(2)}, u32[]{:S(2)}) collective-permute-start(bf16[256,640]{1,0:T(8,128)(2,1)} %get-tuple-element.14), channel_id=1, source_target_pairs={{0,768},{256,0},{512,256},{768,512},{1,769},{257,1},{513,257},{769... | collective-permute-start | bytes 983048 | tf_op jit(solution)/shard_map/ppermute | solution.py:207
  27.7 1.9 %collective-permute-start.4 = (bf16[256,640]{1,0:T(8,128)(2,1)}, bf16[256,640]{1,0:T(8,128)(2,1)S(1)}, u32[]{:S(2)}, u32[]{:S(2)}) collective-permute-start(bf16[256,640]{1,0:T(8,128)(2,1)} %get-tuple-element.15), channel_id=1, source_target_pairs={{0,256},{256,512},{512,768},{768,0},{1,257},{257,513},{513,769},{7... | collective-permute-start | bytes 983048 | tf_op jit(solution)/shard_map/ppermute | solution.py:207
  29.7 2.3 %collective-permute-start = (bf16[256,640]{1,0:T(8,128)(2,1)}, bf16[256,640]{1,0:T(8,128)(2,1)S(1)}, u32[]{:S(2)}, u32[]{:S(2)}) collective-permute-start(bf16[256,640]{1,0:T(8,128)(2,1)} %get-tuple-element.14), channel_id=1, source_target_pairs={{0,256},{256,512},{512,768},{768,0},{1,257},{257,513},{513,769},{7... | collective-permute-start | bytes 983048 | tf_op jit(solution)/shard_map/ppermute | solution.py:207
  31.9 4.8 %collective-permute-start.1 = (bf16[256,640]{1,0:T(8,128)(2,1)}, bf16[256,640]{1,0:T(8,128)(2,1)S(1)}, u32[]{:S(2)}, u32[]{:S(2)}) collective-permute-start(bf16[256,640]{1,0:T(8,128)(2,1)} %get-tuple-element.15), channel_id=1, source_target_pairs={{0,768},{256,0},{512,256},{768,512},{1,769},{257,1},{513,257},{769... | collective-permute-start | bytes 983048 | tf_op jit(solution)/shard_map/ppermute | solution.py:207
  36.7 1.1 collective-permute-done.2.right_a
  37.8 5.2 %collective-permute-start.3 = (bf16[256,640]{1,0:T(8,128)(2,1)S(1)}, bf16[256,640]{1,0:T(8,128)(2,1)S(1)}, u32[]{:S(2)}, u32[]{:S(2)}) collective-permute-start(bf16[256,640]{1,0:T(8,128)(2,1)S(1)} %collective-permute-done.2.right_a), channel_id=1, source_target_pairs={{0,768},{256,0},{512,256},{768,512},{1,769},{257,1},{513,257},{769... | collective-permute-start | bytes 983048 | tf_op jit(solution)/shard_map/ppermute | solution.py:207
  43.0 0.7 copy-done.4
  43.8 1.9 %collective-permute-start.5 = (bf16[256,640]{1,0:T(8,128)(2,1)S(1)}, bf16[256,640]{1,0:T(8,128)(2,1)S(1)}, u32[]{:S(2)}, u32[]{:S(2)}) collective-permute-start(bf16[256,640]{1,0:T(8,128)(2,1)S(1)} %collective-permute-done.4.left_b), channel_id=1, source_target_pairs={{0,256},{256,512},{512,768},{768,0},{1,257},{257,513},{513,769},{7... | collective-permute-start | bytes 983048 | tf_op jit(solution)/shard_map/ppermute | solution.py:207
  45.7 0.7 copy-done.6
  46.4 4.6 %collective-permute-done.left_a = bf16[256,640]{1,0:T(8,128)(2,1)S(1)} collective-permute-done((bf16[256,640]{1,0:T(8,128)(2,1)}, bf16[256,640]{1,0:T(8,128)(2,1)S(1)}, u32[]{:S(2)}, u32[]{:S(2)}) %collective-permute-start) | collective-permute-done | bytes 327712 | tf_op jit(solution)/shard_map/ppermute | solution.py:207
  51.0 1.4 collective-permute-done.3.far_a
  52.5 4.5 %collective-permute-done.5.far_b = bf16[256,640]{1,0:T(8,128)(2,1)S(1)} collective-permute-done((bf16[256,640]{1,0:T(8,128)(2,1)S(1)}, bf16[256,640]{1,0:T(8,128)(2,1)S(1)}, u32[]{:S(2)}, u32[]{:S(2)}) %collective-permute-start.5) | collective-permute-done | bytes 327712 | tf_op jit(solution)/shard_map/ppermute | solution.py:207
  57.0 0.7 copy-done.2
  57.7 0.3 shard_map.95.own
  58.0 1.9 %collective-permute-start.6 = (bf16[2,512,256]{2,1,0:T(8,128)(2,1)S(1)}, bf16[2,512,256]{2,1,0:T(8,128)(2,1)S(1)}, u32[]{:S(2)}, u32[]{:S(2)}) collective-permute-start(bf16[2,512,256]{2,1,0:T(8,128)(2,1)S(1)} %shard_map.95.own), channel_id=1, source_target_pairs={{0,1},{1,0},{2,3},{3,2},{4,5},{5,4},{6,7},{7,6},{8,9},{9,8},{10,11... | collective-permute-start | bytes 1572872 | tf_op jit(solution)/shard_map/ppermute | solution.py:203
  60.0 1.9 %collective-permute-done.6.other = bf16[2,512,256]{2,1,0:T(8,128)(2,1)S(1)} collective-permute-done((bf16[2,512,256]{2,1,0:T(8,128)(2,1)S(1)}, bf16[2,512,256]{2,1,0:T(8,128)(2,1)S(1)}, u32[]{:S(2)}, u32[]{:S(2)}) %collective-permute-start.6) | collective-permute-done | bytes 524320 | tf_op jit(solution)/shard_map/ppermute | solution.py:203
  61.8 1.0 shard_map.96
  62.9 21.0 %all_to_all.20.got = bf16[4,128,1280]{2,1,0:T(8,128)(2,1)S(1)} all-to-all(bf16[4,128,1280]{2,1,0:T(8,128)(2,1)S(1)} %bitcast.19), channel_id=1, replica_groups=mesh['y'=4,'x'=4,'l'=8,'h'=4,'c'=2] {'y'}, dimensions={0} | all-to-all | bytes 2621440 | tf_op jit(solution)/shard_map/all_to_all | solution.py:199
  83.9 1.4 shard_map.97
  85.4 1.9 %collective-permute-start.7 = (bf16[128,1024]{1,0:T(8,128)(2,1)S(1)}, bf16[128,1024]{1,0:T(8,128)(2,1)S(1)}, u32[]{:S(2)}, u32[]{:S(2)}) collective-permute-start(bf16[128,1024]{1,0:T(8,128)(2,1)S(1)} %get-tuple-element.17), channel_id=1, source_target_pairs={{0,1},{1,0},{2,3},{3,2},{4,5},{5,4},{6,7},{7,6},{8,9},{9,8},{10,11... | collective-permute-start | bytes 786440 | tf_op jit(solution)/shard_map/ppermute | solution.py:203
  87.3 1.5 collective-permute-done.7.got
  88.8 0.8 shard_map.98
  89.5 22.8 %all-to-all-start.2 = ((bf16[32,16,256]{2,1,0:T(8,128)(2,1)}), bf16[32,16,256]{2,1,0:T(8,128)(2,1)S(1)}, u32[]{:S(2)}, u32[]{:S(2)}) async-start(bf16[32,16,256]{2,1,0:T(8,128)(2,1)} %bitcast.9), calls=%async_computation.2 | async-start | bytes 524288 | tf_op jit(solution)/shard_map/all_to_all | solution.py:199
  112.4 13.8 %all_gather.6.dh = bf16[512,640]{1,0:T(8,128)(2,1)S(1)} all-gather(bf16[128,640]{1,0:T(8,128)(2,1)} %copy-done.8), channel_id=1, replica_groups=mesh['y'=4,'x'=4,'l'=8,'h'=4,'c'=2] {'y'}, dimensions={0}, use_global_device_ids=true | all-gather | bytes 819200 | tf_op jit(solution)/shard_map/all_gather | solution.py:260
  126.2 13.0 %all_gather.7.act = bf16[512,640]{1,0:T(8,128)(2,1)S(1)} all-gather(bf16[128,640]{1,0:T(8,128)(2,1)S(1)} %get-tuple-element.19), channel_id=1, replica_groups=mesh['y'=4,'x'=4,'l'=8,'h'=4,'c'=2] {'y'}, dimensions={0}, use_global_device_ids=true | all-gather | bytes 819200 | tf_op jit(solution)/shard_map/all_gather | solution.py:260
  139.2 1.9 %shard_map.99 = (bf16[512,640]{1,0:T(8,128)(2,1)}, bf16[640,512]{1,0:T(8,128)(2,1)}, f32[8,128]{1,0:T(8,128)S(1)}) custom-call(s32[1]{0:T(128)} %bitcast.place, bf16[2,512,256]{2,1,0:T(8,128)(2,1)S(1)} %shard_map.95.own, bf16[2,512,256]{2,1,0:T(8,128)(2,1)S(1)} %collective-permute-done.6.other, bf16[512,640]{1,0:T(8,128)(2,1)S(1)} %all_gather.6.dh, ...), custom_call_target="tpu_custom_call" | custom-call | bytes 3674112 | tf_op jit(solution)/shard_map/pallas_call | solution.py:41
  141.1 6.5 %all-to-all-done.2 = bf16[32,16,256]{2,1,0:T(8,128)(2,1)S(1)} async-done(((bf16[32,16,256]{2,1,0:T(8,128)(2,1)}), bf16[32,16,256]{2,1,0:T(8,128)(2,1)S(1)}, u32[]{:S(2)}, u32[]{:S(2)}) %all-to-all-start.2) | async-done | bytes 262176 | tf_op jit(solution)/shard_map/all_to_all | solution.py:199
  147.6 0.2 shard_map.100
  147.7 9.5 %all_to_all.21 = bf16[4,32,256]{2,1,0:T(8,128)(2,1)S(1)} all-to-all(bf16[4,32,256]{2,1,0:T(8,128)(2,1)S(1)} %bitcast.25), channel_id=1, replica_groups=mesh['y'=4,'x'=4,'l'=8,'h'=4,'c'=2] {'x'}, dimensions={0} | all-to-all | bytes 131072 | tf_op jit(solution)/shard_map/all_to_all | solution.py:199
  157.2 0.8 shard_map.101
  (26 shorter events, 0.1 us)
Async XLA Ops:
  0.6 57.1 %copy-start.1 = (bf16[1,640,512]{2,1,0:T(8,128)(2,1)S(1)}, bf16[1,640,512]{2,1,0:T(8,128)(2,1)}, u32[]{:S(2)}) copy-start(bf16[1,640,512]{2,1,0:T(8,128)(2,1)} %param.13) | copy-start | bytes 1966084
  3.4 58.5 %copy-start = (bf16[1,512,640]{2,1,0:T(8,128)(2,1)S(1)}, bf16[1,512,640]{2,1,0:T(8,128)(2,1)}, u32[]{:S(2)}) copy-start(bf16[1,512,640]{2,1,0:T(8,128)(2,1)} %param.12) | copy-start | bytes 1966084
  3.4 54.3 %all-to-all-start = ((bf16[128,8,256]{2,1,0:T(8,128)(2,1)}), bf16[128,8,256]{2,1,0:T(8,128)(2,1)S(1)}, u32[]{:S(2)}, u32[]{:S(2)}) async-start(bf16[128,8,256]{2,1,0:T(8,128)(2,1)} %bitcast.30), calls=%async_computation | async-start | bytes 1048576 | tf_op jit(solution)/shard_map/all_to_all | solution.py:199
  22.6 15.2 %collective-permute-start.2 = (bf16[256,640]{1,0:T(8,128)(2,1)}, bf16[256,640]{1,0:T(8,128)(2,1)S(1)}, u32[]{:S(2)}, u32[]{:S(2)}) collective-permute-start(bf16[256,640]{1,0:T(8,128)(2,1)} %get-tuple-element.14), channel_id=1, source_target_pairs={{0,768},{256,0},{512,256},{768,512},{1,769},{257,1},{513,257},{769... | collective-permute-start | bytes 983048 | tf_op jit(solution)/shard_map/ppermute | solution.py:207
  27.7 16.0 %collective-permute-start.4 = (bf16[256,640]{1,0:T(8,128)(2,1)}, bf16[256,640]{1,0:T(8,128)(2,1)S(1)}, u32[]{:S(2)}, u32[]{:S(2)}) collective-permute-start(bf16[256,640]{1,0:T(8,128)(2,1)} %get-tuple-element.15), channel_id=1, source_target_pairs={{0,256},{256,512},{512,768},{768,0},{1,257},{257,513},{513,769},{7... | collective-permute-start | bytes 983048 | tf_op jit(solution)/shard_map/ppermute | solution.py:207
  29.7 21.4 %collective-permute-start = (bf16[256,640]{1,0:T(8,128)(2,1)}, bf16[256,640]{1,0:T(8,128)(2,1)S(1)}, u32[]{:S(2)}, u32[]{:S(2)}) collective-permute-start(bf16[256,640]{1,0:T(8,128)(2,1)} %get-tuple-element.14), channel_id=1, source_target_pairs={{0,256},{256,512},{512,768},{768,0},{1,257},{257,513},{513,769},{7... | collective-permute-start | bytes 983048 | tf_op jit(solution)/shard_map/ppermute | solution.py:207
  31.9 19.1 %collective-permute-start.1 = (bf16[256,640]{1,0:T(8,128)(2,1)}, bf16[256,640]{1,0:T(8,128)(2,1)S(1)}, u32[]{:S(2)}, u32[]{:S(2)}) collective-permute-start(bf16[256,640]{1,0:T(8,128)(2,1)} %get-tuple-element.15), channel_id=1, source_target_pairs={{0,768},{256,0},{512,256},{768,512},{1,769},{257,1},{513,257},{769... | collective-permute-start | bytes 983048 | tf_op jit(solution)/shard_map/ppermute | solution.py:207
  37.8 14.7 %collective-permute-start.3 = (bf16[256,640]{1,0:T(8,128)(2,1)S(1)}, bf16[256,640]{1,0:T(8,128)(2,1)S(1)}, u32[]{:S(2)}, u32[]{:S(2)}) collective-permute-start(bf16[256,640]{1,0:T(8,128)(2,1)S(1)} %collective-permute-done.2.right_a), channel_id=1, source_target_pairs={{0,768},{256,0},{512,256},{768,512},{1,769},{257,1},{513,257},{769... | collective-permute-start | bytes 983048 | tf_op jit(solution)/shard_map/ppermute | solution.py:207
  43.0 0.7 copy-start.4
  43.8 13.2 %collective-permute-start.5 = (bf16[256,640]{1,0:T(8,128)(2,1)S(1)}, bf16[256,640]{1,0:T(8,128)(2,1)S(1)}, u32[]{:S(2)}, u32[]{:S(2)}) collective-permute-start(bf16[256,640]{1,0:T(8,128)(2,1)S(1)} %collective-permute-done.4.left_b), channel_id=1, source_target_pairs={{0,256},{256,512},{512,768},{768,0},{1,257},{257,513},{513,769},{7... | collective-permute-start | bytes 983048 | tf_op jit(solution)/shard_map/ppermute | solution.py:207
  45.7 0.7 copy-start.6
  57.0 0.7 copy-start.2
  58.0 3.8 %collective-permute-start.6 = (bf16[2,512,256]{2,1,0:T(8,128)(2,1)S(1)}, bf16[2,512,256]{2,1,0:T(8,128)(2,1)S(1)}, u32[]{:S(2)}, u32[]{:S(2)}) collective-permute-start(bf16[2,512,256]{2,1,0:T(8,128)(2,1)S(1)} %shard_map.95.own), channel_id=1, source_target_pairs={{0,1},{1,0},{2,3},{3,2},{4,5},{5,4},{6,7},{7,6},{8,9},{9,8},{10,11... | collective-permute-start | bytes 1572872 | tf_op jit(solution)/shard_map/ppermute | solution.py:203
  62.8 21.1 %copy-start.3 = (bf16[256,640]{1,0:T(8,128)(2,1)S(1)}, bf16[256,640]{1,0:T(8,128)(2,1)}, u32[]{:S(2)}) copy-start(bf16[256,640]{1,0:T(8,128)(2,1)} %copy-done.2) | copy-start | bytes 983044
  62.9 21.1 %copy-start.5 = (bf16[256,640]{1,0:T(8,128)(2,1)S(1)}, bf16[256,640]{1,0:T(8,128)(2,1)}, u32[]{:S(2)}) copy-start(bf16[256,640]{1,0:T(8,128)(2,1)} %copy-done.4) | copy-start | bytes 983044
  62.9 21.1 %copy-start.7 = (bf16[256,640]{1,0:T(8,128)(2,1)S(1)}, bf16[256,640]{1,0:T(8,128)(2,1)}, u32[]{:S(2)}) copy-start(bf16[256,640]{1,0:T(8,128)(2,1)} %copy-done.6) | copy-start | bytes 983044
  85.3 4.2 %copy-start.8 = (bf16[128,640]{1,0:T(8,128)(2,1)}, bf16[128,640]{1,0:T(8,128)(2,1)S(1)}, u32[]{:S(2)}) copy-start(bf16[128,640]{1,0:T(8,128)(2,1)S(1)} %get-tuple-element.18) | copy-start | bytes 491524
  85.4 3.4 %collective-permute-start.7 = (bf16[128,1024]{1,0:T(8,128)(2,1)S(1)}, bf16[128,1024]{1,0:T(8,128)(2,1)S(1)}, u32[]{:S(2)}, u32[]{:S(2)}) collective-permute-start(bf16[128,1024]{1,0:T(8,128)(2,1)S(1)} %get-tuple-element.17), channel_id=1, source_target_pairs={{0,1},{1,0},{2,3},{3,2},{4,5},{5,4},{6,7},{7,6},{8,9},{9,8},{10,11... | collective-permute-start | bytes 786440 | tf_op jit(solution)/shard_map/ppermute | solution.py:203
  89.5 58.0 %all-to-all-start.2 = ((bf16[32,16,256]{2,1,0:T(8,128)(2,1)}), bf16[32,16,256]{2,1,0:T(8,128)(2,1)S(1)}, u32[]{:S(2)}, u32[]{:S(2)}) async-start(bf16[32,16,256]{2,1,0:T(8,128)(2,1)} %bitcast.9), calls=%async_computation.2 | async-start | bytes 524288 | tf_op jit(solution)/shard_map/all_to_all | solution.py:199
  139.2 18.0 %copy-start.9 = (s32[128]{0:T(128)S(1)}, s32[128]{0:T(128)}, u32[]{:S(2)}) copy-start(s32[128]{0:T(128)} %param.10) | copy-start | bytes 1540
  139.2 18.0 %copy-start.10 = (s32[128]{0:T(128)S(1)}, s32[128]{0:T(128)}, u32[]{:S(2)}) copy-start(s32[128]{0:T(128)} %param.11) | copy-start | bytes 1540

commit v10 on v9

--- a/solution.py
+++ b/solution.py
@@ -32,7 +32,7 @@
     return n
 
 
-def call(kernel, outs, *args, scratch=(), fetch=False, after=()):
+def call(kernel, outs, *args, scratch=(), fetch=False, lazy=(), after=()):
     moved = sum(a.size * a.dtype.itemsize for a in args) + sum(
         jnp.dtype(d).itemsize * size(s) for s, d in outs
     )
@@ -43,12 +43,13 @@
         out_shape=[jax.ShapeDtypeStruct(s, d) for s, d in outs],
         in_specs=[pl.BlockSpec(memory_space=pltpu.SMEM)]
         + [pl.BlockSpec(memory_space=space)] * len(args)
+        + [pl.BlockSpec(memory_space=pltpu.HBM)] * len(lazy)
         + [pl.BlockSpec(memory_space=pl.ANY)] * len(after),
-        out_specs=[pl.BlockSpec(memory_space=pltpu.VMEM)] * len(outs),
+        out_specs=[pl.BlockSpec(memory_space=space)] * len(outs),
         scratch_shapes=scratch,
         compiler_params=pltpu.CompilerParams(vmem_limit_bytes=(60 if fetch else 16) * 1024 * 1024),
         cost_estimate=pl.CostEstimate(flops=0, bytes_accessed=moved, transcendentals=0),
-    )(place, *args, *after)
+    )(place, *args, *lazy, *after)
 
 
 def core(place):
@@ -60,7 +61,8 @@
 
 
 def dispatch_kernel(
-    place, eid, slot, gate, tok, cot, w_in, out, w_low, w_high, eid_v, slot_v, gate_v, tok_v, cot_v, sems
+    place, eid, slot, gate, tok, cot, w_in, out, w_low, w_high,
+    eid_v, slot_v, gate_v, tok_v, cot_v, w_v, out_v, sems, out_sems,
 ):
     quarters, toks, feats = tok_v.shape
     count = out.shape[0] // quarters
@@ -68,14 +70,11 @@
         pltpu.make_async_copy(src, dst, sems.at[i])
         for i, (src, dst) in enumerate(((eid, eid_v), (slot, slot_v), (gate, gate_v)))
     ]
-    for src, dst in ((tok, tok_v), (cot, cot_v)):
-        for q in range(quarters):
-            cols = pl.ds(pl.multiple_of((2 * q + core(place)) * feats, feats), feats)
+    for q in range(quarters):
+        cols = pl.ds(pl.multiple_of((2 * q + core(place)) * feats, feats), feats)
+        for src, dst in ((tok, tok_v), (cot, cot_v)):
             copies.append(pltpu.make_async_copy(src.at[:, cols], dst.at[q], sems.at[len(copies)]))
-    half = w_in.shape[0] // 2
-    for i, dst in enumerate((w_low, w_high)):
-        src = w_in.at[i * half : (i + 1) * half]
-        copies.append(pltpu.make_async_copy(src, dst, sems.at[len(copies)]))
+    copies.append(pltpu.make_async_copy(w_in, w_v, sems.at[len(copies)]))
     for copy in copies:
         copy.start()
     for copy in copies[:3]:
@@ -86,13 +85,23 @@
     take_x = as_bf16(hit & is_x)
     take_dy = as_bf16(hit & ~is_x)
     row_gate = jnp.sum(jnp.where(hit, gate_v[...], 0.0), axis=1, keepdims=True)
-    for copy in copies[3:-2]:
-        copy.wait()
+    results = []
     for q in range(quarters):
+        for copy in copies[3 + 2 * q : 5 + 2 * q]:
+            copy.wait()
         got_x = dot(take_x, tok_v[q], ((1,), (0,)))
         got_dy = row_gate * dot(take_dy, cot_v[q], ((1,), (0,)))
-        out[q * count : (q + 1) * count] = (got_x + got_dy).astype(bf16)
-    for copy in copies[-2:]:
+        out_v[q] = (got_x + got_dy).astype(bf16)
+        dst = out.at[q * count : (q + 1) * count]
+        results.append(pltpu.make_async_copy(out_v.at[q], dst, out_sems.at[q]))
+        results[-1].start()
+    copies[-1].wait()
+    half = w_in.shape[0] // 2
+    for i, dst in enumerate((w_low, w_high)):
+        src = w_v.at[i * half : (i + 1) * half]
+        results.append(pltpu.make_async_copy(src, dst, out_sems.at[quarters + i]))
+        results[-1].start()
+    for copy in results:
         copy.wait()
 
 
@@ -130,19 +139,13 @@
 
 
 def back_kernel(
-    place, got, own, left_a, left_b, right_a, right_b, far_a, far_b, mine, theirs, dh, act, w
+    place, got, own, left_a, left_b, right_a, right_b, far_a, far_b, mine, theirs, dh, act, w, sems
 ):
-    hid = dh.shape[1]
-    total = got[0].astype(f32)
-    for q in range(1, got.shape[0]):
-        total = total + got[q].astype(f32)
-    gelu_value, gelu_slope = gelu_pair(total[:, :hid])
-    dh[...] = (total[:, hid:] * gelu_slope).astype(bf16)
-    act[...] = gelu_value.astype(bf16)
     y, c = place[0] >> 1, core(place)
     hs = 4
     f = own.shape[0] // (2 * hs)
-    for out, at in ((theirs, 1 - c), (mine, c)):
+    copies = []
+    for i, at in enumerate((1 - c, c)):
         for src, q in (
             ((own, own), y),
             ((left_a, left_b), (y + 3) & 3),
@@ -152,9 +155,22 @@
             for h in range(hs):
                 ref = src[h // 2]
                 start = ((h if ref is own else h % 2) * 2 + at) * f
-                rows = ref[pl.ds(pl.multiple_of(start, f), f), :]
-                w[pl.ds(pl.multiple_of((h * 4 + q) * f, f), f), :] = rows
-        out[...] = dot(dh[...], w[...], ((1,), (1,))).astype(out.dtype)
+                rows = ref.at[pl.ds(pl.multiple_of(start, f), f)]
+                place_in_w = w.at[i, pl.ds(pl.multiple_of((h * 4 + q) * f, f), f)]
+                copies.append(pltpu.make_async_copy(rows, place_in_w, sems.at[len(copies)]))
+    for copy in copies:
+        copy.start()
+    hid = dh.shape[1]
+    total = got[0].astype(f32)
+    for q in range(1, got.shape[0]):
+        total = total + got[q].astype(f32)
+    gelu_value, gelu_slope = gelu_pair(total[:, :hid])
+    dh[...] = (total[:, hid:] * gelu_slope).astype(bf16)
+    act[...] = gelu_value.astype(bf16)
+    for i, out in enumerate((theirs, mine)):
+        for copy in copies[16 * i : 16 * (i + 1)]:
+            copy.wait()
+        out[...] = dot(dh[...], w[i], ((1,), (1,))).astype(out.dtype)
 
 
 def pack_kernel(place, mine, got, out):
@@ -231,7 +247,10 @@
             pltpu.VMEM((1, toks), f32),
             pltpu.VMEM((ys, toks, part), bf16),
             pltpu.VMEM((ys, toks, part), bf16),
-            pltpu.SemaphoreType.DMA((5 + 2 * ys,)),
+            pltpu.VMEM(w_in.shape, bf16),
+            pltpu.VMEM((ys, groups * 8 // ys, part), bf16),
+            pltpu.SemaphoreType.DMA((4 + 2 * ys,)),
+            pltpu.SemaphoreType.DMA((ys + 2,)),
         ],
         fetch=True,
     )
@@ -250,9 +269,8 @@
         back_kernel,
         [((chunk, ys * part), f32), ((chunk, ys * part), bf16), block, block],
         got,
-        w_in,
-        *gathered,
-        scratch=[pltpu.VMEM((ys * part, hid), bf16)],
+        scratch=[pltpu.VMEM((2, ys * part, hid), bf16), pltpu.SemaphoreType.DMA((32,))],
+        lazy=(w_in,) + gathered,
     )
     got = other_core(theirs)
     (sent,) = call(pack_kernel, [((ls, hs, xs * 4, part), bf16)], mine, got)

time: 159 us -> 163 us (1.025)
  Pallas kernels: 9.03 us -> 13.3 us
    pallas_call x8, Pallas kernels: 9.03 us -> 13.3 us  [call(): pl.pallas_call(kernel, out_shape=[jax.ShapeDtypeStruct(s, d) for s, d in...]
where the time goes in v10:
time: 163 us; the launch traced here: 162 us
  starting transfers between devices  67.1 us (41%)
  blocking collectives  57.4 us (35%)
  waiting for transfers between devices  21.5 us (13%)
  Pallas kernels  13.3 us (8%)
  local copies, waits for them, and re-layouts  2.2 us (1%)
    all_to_all x2, starting transfers between devices, exchange(): return lax.all_to_all(x, axes, split_axis=0, concat_axis=0, tiled=True)  42 us
    all_to_all x2, blocking collectives, exchange(): return lax.all_to_all(x, axes, split_axis=0, concat_axis=0, tiled=True)  30.5 us
    all_gather x2, blocking collectives, local(): dh, act = (lax.all_gather(a, 'y', axis=0, tiled=True) for a in (dh, act))  26.9 us
    ppermute x6, starting transfers between devices, over_y(): return lax.ppermute(x, 'y', [(y, (y + step) % 4) for y in range(4)])  21.2 us
    pallas_call x8, Pallas kernels, call(): pl.pallas_call(kernel, out_shape=[jax.ShapeDtypeStruct(s, d) for s, d in...  13.3 us
    ppermute x6, waiting for transfers between devices, over_y(): return lax.ppermute(x, 'y', [(y, (y + step) % 4) for y in range(4)])  11.7 us
    all_to_all x2, waiting for transfers between devices, exchange(): return lax.all_to_all(x, axes, split_axis=0, concat_axis=0, tiled=True)  6.47 us
    ppermute x2, starting transfers between devices, other_core(): return lax.ppermute(x, 'c', [(0, 1), (1, 0)])  3.84 us
  transfers between devices with their start and end apart: 10, of which 7 were waited for; matrix products, arithmetic and copies ran while one was open for 0% of the time, Pallas kernels for 1%

profile of v10, /device:TPU:32, one launch (start us, length us, event | category | flops | bytes accessed | tf_op | source)
XLA Modules:
  0.0 162.3 jit_solution(10757725411661458348)
XLA Ops:
  0.6 2.9 %shard_map.94 = (bf16[1024,256]{1,0:T(8,128)(2,1)}, bf16[256,640]{1,0:T(8,128)(2,1)}, bf16[256,640]{1,0:T(8,128)(2,1)}) custom-call(s32[1]{0:T(128)} %bitcast.place, s32[1,128]{1,0:T(1,128)} %bitcast.26, s32[1,128]{1,0:T(1,128)} %bitcast.28, f32[1,128]{1,0:T(1,128)} %bitcast.32, bf16[128,2048]{1,0:T(8,128)(2,1)} %tok.1, bf16[128,2048]{1,0:T(8,128)(2,1)} %cot.1, ...), custom_call_target="tpu_custom_call" | custom-call | bytes 2885120 | tf_op jit(solution)/shard_map/pallas_call | solution.py:41
  3.5 19.2 %all-to-all-start = ((bf16[128,8,256]{2,1,0:T(8,128)(2,1)}), bf16[128,8,256]{2,1,0:T(8,128)(2,1)S(1)}, u32[]{:S(2)}, u32[]{:S(2)}) async-start(bf16[128,8,256]{2,1,0:T(8,128)(2,1)} %bitcast.30), calls=%async_computation | async-start | bytes 1048576 | tf_op jit(solution)/shard_map/all_to_all | solution.py:215
  22.8 5.1 %collective-permute-start.2 = (bf16[256,640]{1,0:T(8,128)(2,1)}, bf16[256,640]{1,0:T(8,128)(2,1)S(1)}, u32[]{:S(2)}, u32[]{:S(2)}) collective-permute-start(bf16[256,640]{1,0:T(8,128)(2,1)} %get-tuple-element.14), channel_id=1, source_target_pairs={{0,768},{256,0},{512,256},{768,512},{1,769},{257,1},{513,257},{769... | collective-permute-start | bytes 983048 | tf_op jit(solution)/shard_map/ppermute | solution.py:223
  27.9 1.9 %collective-permute-start.4 = (bf16[256,640]{1,0:T(8,128)(2,1)}, bf16[256,640]{1,0:T(8,128)(2,1)S(1)}, u32[]{:S(2)}, u32[]{:S(2)}) collective-permute-start(bf16[256,640]{1,0:T(8,128)(2,1)} %get-tuple-element.15), channel_id=1, source_target_pairs={{0,256},{256,512},{512,768},{768,0},{1,257},{257,513},{513,769},{7... | collective-permute-start | bytes 983048 | tf_op jit(solution)/shard_map/ppermute | solution.py:223
  29.8 2.3 %collective-permute-start = (bf16[256,640]{1,0:T(8,128)(2,1)}, bf16[256,640]{1,0:T(8,128)(2,1)S(1)}, u32[]{:S(2)}, u32[]{:S(2)}) collective-permute-start(bf16[256,640]{1,0:T(8,128)(2,1)} %get-tuple-element.14), channel_id=1, source_target_pairs={{0,256},{256,512},{512,768},{768,0},{1,257},{257,513},{513,769},{7... | collective-permute-start | bytes 983048 | tf_op jit(solution)/shard_map/ppermute | solution.py:223
  32.1 4.8 %collective-permute-start.1 = (bf16[256,640]{1,0:T(8,128)(2,1)}, bf16[256,640]{1,0:T(8,128)(2,1)S(1)}, u32[]{:S(2)}, u32[]{:S(2)}) collective-permute-start(bf16[256,640]{1,0:T(8,128)(2,1)} %get-tuple-element.15), channel_id=1, source_target_pairs={{0,768},{256,0},{512,256},{768,512},{1,769},{257,1},{513,257},{769... | collective-permute-start | bytes 983048 | tf_op jit(solution)/shard_map/ppermute | solution.py:223
  36.9 1.0 collective-permute-done.2.right_a
  38.0 5.2 %collective-permute-start.3 = (bf16[256,640]{1,0:T(8,128)(2,1)S(1)}, bf16[256,640]{1,0:T(8,128)(2,1)S(1)}, u32[]{:S(2)}, u32[]{:S(2)}) collective-permute-start(bf16[256,640]{1,0:T(8,128)(2,1)S(1)} %collective-permute-done.2.right_a), channel_id=1, source_target_pairs={{0,768},{256,0},{512,256},{768,512},{1,769},{257,1},{513,257},{769... | collective-permute-start | bytes 983048 | tf_op jit(solution)/shard_map/ppermute | solution.py:223
  43.2 0.7 copy-done.4
  43.9 1.9 %collective-permute-start.5 = (bf16[256,640]{1,0:T(8,128)(2,1)S(1)}, bf16[256,640]{1,0:T(8,128)(2,1)S(1)}, u32[]{:S(2)}, u32[]{:S(2)}) collective-permute-start(bf16[256,640]{1,0:T(8,128)(2,1)S(1)} %collective-permute-done.4.left_b), channel_id=1, source_target_pairs={{0,256},{256,512},{512,768},{768,0},{1,257},{257,513},{513,769},{7... | collective-permute-start | bytes 983048 | tf_op jit(solution)/shard_map/ppermute | solution.py:223
  45.8 0.7 copy-done.6
  46.6 4.7 %collective-permute-done.left_a = bf16[256,640]{1,0:T(8,128)(2,1)S(1)} collective-permute-done((bf16[256,640]{1,0:T(8,128)(2,1)}, bf16[256,640]{1,0:T(8,128)(2,1)S(1)}, u32[]{:S(2)}, u32[]{:S(2)}) %collective-permute-start) | collective-permute-done | bytes 327712 | tf_op jit(solution)/shard_map/ppermute | solution.py:223
  51.2 1.4 collective-permute-done.3.far_a
  52.6 4.5 %collective-permute-done.5.far_b = bf16[256,640]{1,0:T(8,128)(2,1)S(1)} collective-permute-done((bf16[256,640]{1,0:T(8,128)(2,1)S(1)}, bf16[256,640]{1,0:T(8,128)(2,1)S(1)}, u32[]{:S(2)}, u32[]{:S(2)}) %collective-permute-start.5) | collective-permute-done | bytes 327712 | tf_op jit(solution)/shard_map/ppermute | solution.py:223
  57.2 0.7 copy-done.2
  57.9 0.3 shard_map.95.own
  58.2 1.9 %collective-permute-start.6 = (bf16[2,512,256]{2,1,0:T(8,128)(2,1)S(1)}, bf16[2,512,256]{2,1,0:T(8,128)(2,1)S(1)}, u32[]{:S(2)}, u32[]{:S(2)}) collective-permute-start(bf16[2,512,256]{2,1,0:T(8,128)(2,1)S(1)} %shard_map.95.own), channel_id=1, source_target_pairs={{0,1},{1,0},{2,3},{3,2},{4,5},{5,4},{6,7},{7,6},{8,9},{9,8},{10,11... | collective-permute-start | bytes 1572872 | tf_op jit(solution)/shard_map/ppermute | solution.py:219
  60.1 1.9 %collective-permute-done.6.other = bf16[2,512,256]{2,1,0:T(8,128)(2,1)S(1)} collective-permute-done((bf16[2,512,256]{2,1,0:T(8,128)(2,1)S(1)}, bf16[2,512,256]{2,1,0:T(8,128)(2,1)S(1)}, u32[]{:S(2)}, u32[]{:S(2)}) %collective-permute-start.6) | collective-permute-done | bytes 524320 | tf_op jit(solution)/shard_map/ppermute | solution.py:219
  62.0 1.0 shard_map.96
  63.0 21.0 %all_to_all.20.got = bf16[4,128,1280]{2,1,0:T(8,128)(2,1)S(1)} all-to-all(bf16[4,128,1280]{2,1,0:T(8,128)(2,1)S(1)} %bitcast.19), channel_id=1, replica_groups=mesh['y'=4,'x'=4,'l'=8,'h'=4,'c'=2] {'y'}, dimensions={0} | all-to-all | bytes 2621440 | tf_op jit(solution)/shard_map/all_to_all | solution.py:215
  84.1 5.5 %shard_map.97 = (f32[128,1024]{1,0:T(8,128)S(1)}, bf16[128,1024]{1,0:T(8,128)(2,1)S(1)}, bf16[128,640]{1,0:T(8,128)(2,1)S(1)}, bf16[128,640]{1,0:T(8,128)(2,1)S(1)}) custom-call(s32[1]{0:T(128)} %bitcast.place, bf16[4,128,1280]{2,1,0:T(8,128)(2,1)S(1)} %all_to_all.20.got, bf16[512,640]{1,0:T(8,128)(2,1)S(1)} %bitcast.18, ...), custom_call_target="tpu_custom_call" | custom-call | bytes 2424832 | tf_op jit(solution)/shard_map/pallas_call | solution.py:41
  89.6 1.9 %collective-permute-start.7 = (bf16[128,1024]{1,0:T(8,128)(2,1)S(1)}, bf16[128,1024]{1,0:T(8,128)(2,1)S(1)}, u32[]{:S(2)}, u32[]{:S(2)}) collective-permute-start(bf16[128,1024]{1,0:T(8,128)(2,1)S(1)} %get-tuple-element.17), channel_id=1, source_target_pairs={{0,1},{1,0},{2,3},{3,2},{4,5},{5,4},{6,7},{7,6},{8,9},{9,8},{10,11... | collective-permute-start | bytes 786440 | tf_op jit(solution)/shard_map/ppermute | solution.py:219
  91.5 1.5 collective-permute-done.7.got
  93.0 0.8 shard_map.98
  93.8 22.8 %all-to-all-start.2 = ((bf16[32,16,256]{2,1,0:T(8,128)(2,1)}), bf16[32,16,256]{2,1,0:T(8,128)(2,1)S(1)}, u32[]{:S(2)}, u32[]{:S(2)}) async-start(bf16[32,16,256]{2,1,0:T(8,128)(2,1)} %bitcast.9), calls=%async_computation.2 | async-start | bytes 524288 | tf_op jit(solution)/shard_map/all_to_all | solution.py:215
  116.6 13.8 %all_gather.6.dh = bf16[512,640]{1,0:T(8,128)(2,1)S(1)} all-gather(bf16[128,640]{1,0:T(8,128)(2,1)} %copy-done.8), channel_id=1, replica_groups=mesh['y'=4,'x'=4,'l'=8,'h'=4,'c'=2] {'y'}, dimensions={0}, use_global_device_ids=true | all-gather | bytes 819200 | tf_op jit(solution)/shard_map/all_gather | solution.py:278
  130.4 13.0 %all_gather.7.act = bf16[512,640]{1,0:T(8,128)(2,1)S(1)} all-gather(bf16[128,640]{1,0:T(8,128)(2,1)S(1)} %get-tuple-element.19), channel_id=1, replica_groups=mesh['y'=4,'x'=4,'l'=8,'h'=4,'c'=2] {'y'}, dimensions={0}, use_global_device_ids=true | all-gather | bytes 819200 | tf_op jit(solution)/shard_map/all_gather | solution.py:278
  143.5 1.9 %shard_map.99 = (bf16[512,640]{1,0:T(8,128)(2,1)}, bf16[640,512]{1,0:T(8,128)(2,1)}, f32[8,128]{1,0:T(8,128)S(1)}) custom-call(s32[1]{0:T(128)} %bitcast.place, bf16[2,512,256]{2,1,0:T(8,128)(2,1)S(1)} %shard_map.95.own, bf16[2,512,256]{2,1,0:T(8,128)(2,1)S(1)} %collective-permute-done.6.other, bf16[512,640]{1,0:T(8,128)(2,1)S(1)} %all_gather.6.dh, ...), custom_call_target="tpu_custom_call" | custom-call | bytes 3674112 | tf_op jit(solution)/shard_map/pallas_call | solution.py:41
  145.3 6.5 %all-to-all-done.2 = bf16[32,16,256]{2,1,0:T(8,128)(2,1)S(1)} async-done(((bf16[32,16,256]{2,1,0:T(8,128)(2,1)}), bf16[32,16,256]{2,1,0:T(8,128)(2,1)S(1)}, u32[]{:S(2)}, u32[]{:S(2)}) %all-to-all-start.2) | async-done | bytes 262176 | tf_op jit(solution)/shard_map/all_to_all | solution.py:215
  151.8 0.2 shard_map.100
  152.0 9.5 %all_to_all.21 = bf16[4,32,256]{2,1,0:T(8,128)(2,1)S(1)} all-to-all(bf16[4,32,256]{2,1,0:T(8,128)(2,1)S(1)} %bitcast.25), channel_id=1, replica_groups=mesh['y'=4,'x'=4,'l'=8,'h'=4,'c'=2] {'x'}, dimensions={0} | all-to-all | bytes 131072 | tf_op jit(solution)/shard_map/all_to_all | solution.py:215
  161.5 0.8 shard_map.101
  (26 shorter events, 0.1 us)
Async XLA Ops:
  0.6 57.3 %copy-start.1 = (bf16[1,640,512]{2,1,0:T(8,128)(2,1)S(1)}, bf16[1,640,512]{2,1,0:T(8,128)(2,1)}, u32[]{:S(2)}) copy-start(bf16[1,640,512]{2,1,0:T(8,128)(2,1)} %param.13) | copy-start | bytes 1966084
  3.5 58.5 %copy-start = (bf16[1,512,640]{2,1,0:T(8,128)(2,1)S(1)}, bf16[1,512,640]{2,1,0:T(8,128)(2,1)}, u32[]{:S(2)}) copy-start(bf16[1,512,640]{2,1,0:T(8,128)(2,1)} %param.12) | copy-start | bytes 1966084
  3.5 54.3 %all-to-all-start = ((bf16[128,8,256]{2,1,0:T(8,128)(2,1)}), bf16[128,8,256]{2,1,0:T(8,128)(2,1)S(1)}, u32[]{:S(2)}, u32[]{:S(2)}) async-start(bf16[128,8,256]{2,1,0:T(8,128)(2,1)} %bitcast.30), calls=%async_computation | async-start | bytes 1048576 | tf_op jit(solution)/shard_map/all_to_all | solution.py:215
  22.8 15.2 %collective-permute-start.2 = (bf16[256,640]{1,0:T(8,128)(2,1)}, bf16[256,640]{1,0:T(8,128)(2,1)S(1)}, u32[]{:S(2)}, u32[]{:S(2)}) collective-permute-start(bf16[256,640]{1,0:T(8,128)(2,1)} %get-tuple-element.14), channel_id=1, source_target_pairs={{0,768},{256,0},{512,256},{768,512},{1,769},{257,1},{513,257},{769... | collective-permute-start | bytes 983048 | tf_op jit(solution)/shard_map/ppermute | solution.py:223
  27.9 16.0 %collective-permute-start.4 = (bf16[256,640]{1,0:T(8,128)(2,1)}, bf16[256,640]{1,0:T(8,128)(2,1)S(1)}, u32[]{:S(2)}, u32[]{:S(2)}) collective-permute-start(bf16[256,640]{1,0:T(8,128)(2,1)} %get-tuple-element.15), channel_id=1, source_target_pairs={{0,256},{256,512},{512,768},{768,0},{1,257},{257,513},{513,769},{7... | collective-permute-start | bytes 983048 | tf_op jit(solution)/shard_map/ppermute | solution.py:223
  29.8 21.4 %collective-permute-start = (bf16[256,640]{1,0:T(8,128)(2,1)}, bf16[256,640]{1,0:T(8,128)(2,1)S(1)}, u32[]{:S(2)}, u32[]{:S(2)}) collective-permute-start(bf16[256,640]{1,0:T(8,128)(2,1)} %get-tuple-element.14), channel_id=1, source_target_pairs={{0,256},{256,512},{512,768},{768,0},{1,257},{257,513},{513,769},{7... | collective-permute-start | bytes 983048 | tf_op jit(solution)/shard_map/ppermute | solution.py:223
  32.1 19.1 %collective-permute-start.1 = (bf16[256,640]{1,0:T(8,128)(2,1)}, bf16[256,640]{1,0:T(8,128)(2,1)S(1)}, u32[]{:S(2)}, u32[]{:S(2)}) collective-permute-start(bf16[256,640]{1,0:T(8,128)(2,1)} %get-tuple-element.15), channel_id=1, source_target_pairs={{0,768},{256,0},{512,256},{768,512},{1,769},{257,1},{513,257},{769... | collective-permute-start | bytes 983048 | tf_op jit(solution)/shard_map/ppermute | solution.py:223
  38.0 14.7 %collective-permute-start.3 = (bf16[256,640]{1,0:T(8,128)(2,1)S(1)}, bf16[256,640]{1,0:T(8,128)(2,1)S(1)}, u32[]{:S(2)}, u32[]{:S(2)}) collective-permute-start(bf16[256,640]{1,0:T(8,128)(2,1)S(1)} %collective-permute-done.2.right_a), channel_id=1, source_target_pairs={{0,768},{256,0},{512,256},{768,512},{1,769},{257,1},{513,257},{769... | collective-permute-start | bytes 983048 | tf_op jit(solution)/shard_map/ppermute | solution.py:223
  43.2 0.7 copy-start.4
  43.9 13.3 %collective-permute-start.5 = (bf16[256,640]{1,0:T(8,128)(2,1)S(1)}, bf16[256,640]{1,0:T(8,128)(2,1)S(1)}, u32[]{:S(2)}, u32[]{:S(2)}) collective-permute-start(bf16[256,640]{1,0:T(8,128)(2,1)S(1)} %collective-permute-done.4.left_b), channel_id=1, source_target_pairs={{0,256},{256,512},{512,768},{768,0},{1,257},{257,513},{513,769},{7... | collective-permute-start | bytes 983048 | tf_op jit(solution)/shard_map/ppermute | solution.py:223
  45.8 0.7 copy-start.6
  57.2 0.7 copy-start.2
  58.2 3.8 %collective-permute-start.6 = (bf16[2,512,256]{2,1,0:T(8,128)(2,1)S(1)}, bf16[2,512,256]{2,1,0:T(8,128)(2,1)S(1)}, u32[]{:S(2)}, u32[]{:S(2)}) collective-permute-start(bf16[2,512,256]{2,1,0:T(8,128)(2,1)S(1)} %shard_map.95.own), channel_id=1, source_target_pairs={{0,1},{1,0},{2,3},{3,2},{4,5},{5,4},{6,7},{7,6},{8,9},{9,8},{10,11... | collective-permute-start | bytes 1572872 | tf_op jit(solution)/shard_map/ppermute | solution.py:219
  63.0 21.1 %copy-start.3 = (bf16[256,640]{1,0:T(8,128)(2,1)S(1)}, bf16[256,640]{1,0:T(8,128)(2,1)}, u32[]{:S(2)}) copy-start(bf16[256,640]{1,0:T(8,128)(2,1)} %copy-done.2) | copy-start | bytes 983044
  63.0 21.1 %copy-start.5 = (bf16[256,640]{1,0:T(8,128)(2,1)S(1)}, bf16[256,640]{1,0:T(8,128)(2,1)}, u32[]{:S(2)}) copy-start(bf16[256,640]{1,0:T(8,128)(2,1)} %copy-done.4) | copy-start | bytes 983044
  63.0 21.1 %copy-start.7 = (bf16[256,640]{1,0:T(8,128)(2,1)S(1)}, bf16[256,640]{1,0:T(8,128)(2,1)}, u32[]{:S(2)}) copy-start(bf16[256,640]{1,0:T(8,128)(2,1)} %copy-done.6) | copy-start | bytes 983044
  89.6 4.2 %copy-start.8 = (bf16[128,640]{1,0:T(8,128)(2,1)}, bf16[128,640]{1,0:T(8,128)(2,1)S(1)}, u32[]{:S(2)}) copy-start(bf16[128,640]{1,0:T(8,128)(2,1)S(1)} %get-tuple-element.18) | copy-start | bytes 491524
  89.6 3.4 %collective-permute-start.7 = (bf16[128,1024]{1,0:T(8,128)(2,1)S(1)}, bf16[128,1024]{1,0:T(8,128)(2,1)S(1)}, u32[]{:S(2)}, u32[]{:S(2)}) collective-permute-start(bf16[128,1024]{1,0:T(8,128)(2,1)S(1)} %get-tuple-element.17), channel_id=1, source_target_pairs={{0,1},{1,0},{2,3},{3,2},{4,5},{5,4},{6,7},{7,6},{8,9},{9,8},{10,11... | collective-permute-start | bytes 786440 | tf_op jit(solution)/shard_map/ppermute | solution.py:219
  93.8 58.0 %all-to-all-start.2 = ((bf16[32,16,256]{2,1,0:T(8,128)(2,1)}), bf16[32,16,256]{2,1,0:T(8,128)(2,1)S(1)}, u32[]{:S(2)}, u32[]{:S(2)}) async-start(bf16[32,16,256]{2,1,0:T(8,128)(2,1)} %bitcast.9), calls=%async_computation.2 | async-start | bytes 524288 | tf_op jit(solution)/shard_map/all_to_all | solution.py:215
  143.5 18.0 %copy-start.9 = (s32[128]{0:T(128)S(1)}, s32[128]{0:T(128)}, u32[]{:S(2)}) copy-start(s32[128]{0:T(128)} %param.10) | copy-start | bytes 1540
  143.5 18.0 %copy-start.10 = (s32[128]{0:T(128)S(1)}, s32[128]{0:T(128)}, u32[]{:S(2)}) copy-start(s32[128]{0:T(128)} %param.11) | copy-start | bytes 1540
